TPU v7x, 256 devices: a whole 4x4x8 slice. The times are simulated.
256 devices in a mesh: pipe: 8 (over y, core), expert: 16 (over x_hi, z), dp: 2 (over x_lo).
Axes of the slice: x: 4 (x_hi: 2, x_lo: 2; x = x_hi * 2 + x_lo), y: 4, z: 8, core: 2. Of those that a mesh axis runs over, the one named last changes fastest.
Arguments:
- fwd_in: bfloat16 [8, 4096, 3584], P('pipe', ('expert', 'dp')), may hold values from -6 to 6
- fwd_ids: int32 [8, 4096, 8], P('pipe', ('expert', 'dp')), may hold values from 0 to 255, all different within a row; in each aligned block of 128 rows (0 to 127, 128 to 255, ..., all dimensions but the last counted through in order) at most 8 rows name the same one
- fwd_score: float32 [8, 4096, 8], P('pipe', ('expert', 'dp')), may hold values from 0.05 to 1
- bwd_in: bfloat16 [8, 4096, 3584], P('pipe', ('expert', 'dp')), may hold values from -6 to 6
- bwd_ids: int32 [8, 4096, 8], P('pipe', ('expert', 'dp')), may hold values from 0 to 255, all different within a row; in each aligned block of 128 rows (0 to 127, 128 to 255, ..., all dimensions but the last counted through in order) at most 8 rows name the same one
- bwd_score: float32 [8, 4096, 8], P('pipe', ('expert', 'dp')), may hold values from 0.05 to 1
- bwd_cot: bfloat16 [8, 4096, 3584], P('pipe', ('expert', 'dp')), may hold values from -6 to 6
- w_gate: bfloat16 [8, 3584, 8192], P('pipe', None, ('expert', 'dp')), may hold values from -0.09375 to 0.09375
- w_up: bfloat16 [8, 3584, 8192], P('pipe', None, ('expert', 'dp')), may hold values from -0.09375 to 0.09375
- w_down: bfloat16 [8, 8192, 3584], P('pipe', ('expert', 'dp')), may hold values from -0.1875 to 0.1875
Outputs:
- fwd_out: bfloat16 [8, 4096, 3584], P('pipe', ('expert', 'dp'))
- bwd_out: bfloat16 [8, 4096, 3584], P('pipe', ('expert', 'dp'))
Inputs may be any that keep to these rules, and one draw needn't show every extreme that they name: `fwd_ids`: each token names 8 different experts; in each aligned block of 128 rows of one section no expert is named by more than 8 rows. `bwd_ids`: each token names 8 different experts; in each aligned block of 128 rows of one section no expert is named by more than 8 rows.
All inputs are finite; a program needn't handle non-finite values.
Results may differ from a plain program's by a relative error of at most 0.0045.
Values may be sent and summed in bfloat16 or wider, within the bound.
No kernel may reach another device: no remote copies, remote signals or barrier semaphores. Data moves between devices by JAX's collectives and lax.ppermute only.
A program may use at most 64 MiB of HBM per device.

v0:
```python
import jax
import jax.numpy as jnp
from jax import lax
from jax.sharding import PartitionSpec as P

CAP = 8


def from_behind(value, axis, steps):
    count = lax.axis_size(axis)
    initial, last = (max(0, -steps), min(count, count - steps))
    return lax.ppermute(value, axis, [(source, source + steps) for source in range(initial, last)])


def expert_forward(rows, gate_w, up_w, down_w):
    gate_pre = jnp.dot(rows, gate_w, preferred_element_type=jnp.float32)
    up_pre = jnp.dot(rows, up_w, preferred_element_type=jnp.float32)
    hidden = (jax.nn.silu(gate_pre) * up_pre).astype(jnp.bfloat16)
    return jnp.dot(hidden, down_w, preferred_element_type=jnp.float32)


def expert_backward(rows, cotan, gate_w, up_w, down_w):
    gate_pre = jnp.dot(rows, gate_w, preferred_element_type=jnp.float32)
    up_pre = jnp.dot(rows, up_w, preferred_element_type=jnp.float32)
    grad_hidden = jnp.dot(cotan, down_w.T, preferred_element_type=jnp.float32)
    sigma = jax.nn.sigmoid(gate_pre)
    grad_gate = (grad_hidden * up_pre * sigma * (1.0 + gate_pre * (1.0 - sigma))).astype(
        jnp.bfloat16
    )
    grad_up = (grad_hidden * jax.nn.silu(gate_pre)).astype(jnp.bfloat16)
    return jnp.dot(grad_gate, gate_w.T, preferred_element_type=jnp.float32) + jnp.dot(
        grad_up, up_w.T, preferred_element_type=jnp.float32
    )


def routing(ids, score, experts, capacity):
    tok_count, choices = ids.shape
    flat_ids = ids.reshape(-1)
    hits = (flat_ids[:, None] == jnp.arange(experts, dtype=jnp.int32)[None, :]).astype(jnp.int32)
    ranks = jnp.cumsum(hits, axis=0) - 1
    slot_of = jnp.sum(hits * ranks, axis=1)
    live = jnp.sum(hits, axis=1) > 0
    target = jnp.where(live, flat_ids * capacity + slot_of, -1).reshape(tok_count, choices)
    match = target[None, :, :] == jnp.arange(experts * capacity, dtype=jnp.int32)[:, None, None]
    dispatch = jnp.any(match, axis=-1).astype(jnp.bfloat16)
    mix = 2.5 * score / jnp.sum(score, axis=-1, keepdims=True)
    combine = jnp.sum(jnp.where(match, mix[None, :, :], 0.0), axis=-1).T
    return (dispatch, combine)


def pack_rows(dispatch, tokens, experts, capacity):
    packed = jnp.dot(dispatch, tokens, preferred_element_type=jnp.float32).astype(jnp.bfloat16)
    packed = packed.reshape(experts, capacity, tokens.shape[1])
    return jnp.repeat(packed, 2, axis=0)


def pair_total(results, experts, capacity, width):
    return jnp.sum(results.reshape(experts, 2, capacity, width), axis=1).astype(jnp.bfloat16)


def combine_rows(base, combine, results):
    width = base.shape[1]
    flat = results.reshape(-1, width).astype(jnp.float32)
    branch = jnp.dot(combine, flat, precision=lax.Precision.HIGHEST)
    return (base.astype(jnp.float32) + branch).astype(jnp.bfloat16)


def per_device(
    fwd_in, fwd_ids, fwd_score, bwd_in, bwd_ids, bwd_score, bwd_cot, w_gate, w_up, w_down
):
    experts = lax.axis_size("expert") // 2
    capacity = CAP
    width = fwd_in.shape[2]
    fwd_tokens = fwd_in[0]
    bwd_tokens = bwd_in[0]
    bwd_grads = bwd_cot[0]
    fwd_dispatch, fwd_combine = routing(fwd_ids[0], fwd_score[0], experts, capacity)
    bwd_dispatch, bwd_combine = routing(bwd_ids[0], bwd_score[0], experts, capacity)
    send_fwd = pack_rows(fwd_dispatch, fwd_tokens, experts, capacity)
    send_input = pack_rows(bwd_dispatch, bwd_tokens, experts, capacity)
    send_grad = pack_rows(bwd_dispatch, bwd_grads, experts, capacity)
    got_fwd = lax.all_to_all(send_fwd, "expert", split_axis=0, concat_axis=0, tiled=True)
    got_input, got_grad = (
        lax.all_to_all(send_input, "expert", split_axis=0, concat_axis=0, tiled=True),
        lax.all_to_all(send_grad, "expert", split_axis=0, concat_axis=0, tiled=True),
    )
    rows_fwd = got_fwd.reshape(-1, width)
    rows_input = got_input.reshape(-1, width)
    rows_grad = got_grad.reshape(-1, width)
    gate_half, up_half, down_half = (
        lax.all_gather(w_gate, "dp", axis=2, tiled=True),
        lax.all_gather(w_up, "dp", axis=2, tiled=True),
        lax.all_gather(w_down, "dp", axis=1, tiled=True),
    )
    fwd_result = expert_forward(rows_fwd, gate_half[0], up_half[0], down_half[0])
    bwd_result = expert_backward(rows_input, rows_grad, gate_half[0], up_half[0], down_half[0])
    fwd_result = fwd_result.reshape(got_fwd.shape)
    bwd_result = bwd_result.reshape(got_input.shape)
    back_fwd = lax.all_to_all(
        fwd_result.astype(jnp.bfloat16), "expert", split_axis=0, concat_axis=0, tiled=True
    ).astype(fwd_result.dtype)
    back_bwd = lax.all_to_all(
        bwd_result.astype(jnp.bfloat16), "expert", split_axis=0, concat_axis=0, tiled=True
    ).astype(bwd_result.dtype)
    summed_fwd = pair_total(back_fwd, experts, capacity, width)
    summed_bwd = pair_total(back_bwd, experts, capacity, width)
    layer_out = combine_rows(fwd_tokens, fwd_combine, summed_fwd)
    input_grad = combine_rows(bwd_grads, bwd_combine, summed_bwd)
    fwd_out = from_behind(layer_out[None], "pipe", 1)
    bwd_out = from_behind(input_grad[None], "pipe", -1)
    return (fwd_out, bwd_out)


def solution(mesh):
    in_specs = (
        P("pipe", ("expert", "dp"), None),
        P("pipe", ("expert", "dp"), None),
        P("pipe", ("expert", "dp"), None),
        P("pipe", ("expert", "dp"), None),
        P("pipe", ("expert", "dp"), None),
        P("pipe", ("expert", "dp"), None),
        P("pipe", ("expert", "dp"), None),
        P("pipe", None, ("expert", "dp")),
        P("pipe", None, ("expert", "dp")),
        P("pipe", ("expert", "dp"), None),
    )
    out_specs = (P("pipe", ("expert", "dp"), None), P("pipe", ("expert", "dp"), None))
    return jax.shard_map(
        per_device, mesh=mesh, in_specs=in_specs, out_specs=out_specs, check_vma=False
    )
```

profile of v0, /device:TPU:1, one launch (start us, length us, event | category | flops | bytes accessed | tf_op | source)
XLA Modules:
  0.0 301.6 jit_solution(16029074291332993658)
XLA Ops:
  7.2 0.7 all-gather.4.cloned.1.call-update
  8.0 0.7 all-gather.8.cloned.1.call-update
  8.7 0.1 copy.36
  9.0 2.3 reduce-window.14
  11.3 0.3 slice_reduce_fusion.1
  11.6 0.2 reduce-window.15
  12.0 0.1 reduce_sum.96
  12.2 0.1 fusion.70
  12.3 0.3 fusion.6
  12.6 1.0 broadcast_in_dim.54
  13.6 11.6 %all-to-all-start = ((bf16[16,8,3584]{2,1,0:T(8,128)(2,1)}), bf16[16,8,3584]{2,1,0:T(8,128)(2,1)S(1)}, u32[]{:S(2)}, u32[]{:S(2)}) async-start(bf16[16,8,3584]{2,1,0:T(8,128)(2,1)} %bitcast.137), calls=%async_computation | async-start | bytes 1835008 | tf_op jit(solution)/shard_map/all_to_all | solution.py:82
  25.2 0.7 all-gather.6.cloned.1.call-update
  25.9 0.1 copy.40
  26.2 2.3 reduce-window.16
  28.5 0.3 slice_reduce_fusion
  28.8 0.2 reduce-window.19
  29.2 0.1 reduce_sum.102
  29.4 0.1 fusion.64
  29.5 0.3 fusion.7
  29.8 18.8 %all-to-all-done = bf16[16,8,3584]{2,1,0:T(8,128)(2,1)S(1)} async-done(((bf16[16,8,3584]{2,1,0:T(8,128)(2,1)}), bf16[16,8,3584]{2,1,0:T(8,128)(2,1)S(1)}, u32[]{:S(2)}, u32[]{:S(2)}) %all-to-all-start) | async-done | bytes 917536 | tf_op jit(solution)/shard_map/all_to_all | solution.py:82
  48.6 1.0 broadcast_in_dim.58
  49.6 6.9 %all-to-all-start.2 = ((bf16[16,8,3584]{2,1,0:T(8,128)(2,1)}), bf16[16,8,3584]{2,1,0:T(8,128)(2,1)S(1)}, u32[]{:S(2)}, u32[]{:S(2)}) async-start(bf16[16,8,3584]{2,1,0:T(8,128)(2,1)} %bitcast.139), calls=%async_computation.2 | async-start | bytes 1835008 | tf_op jit(solution)/shard_map/all_to_all | solution.py:85
  56.4 0.3 fusion.8
  56.7 23.1 %all-to-all-done.2 = bf16[16,8,3584]{2,1,0:T(8,128)(2,1)S(1)} async-done(((bf16[16,8,3584]{2,1,0:T(8,128)(2,1)}), bf16[16,8,3584]{2,1,0:T(8,128)(2,1)S(1)}, u32[]{:S(2)}, u32[]{:S(2)}) %all-to-all-start.2) | async-done | bytes 917536 | tf_op jit(solution)/shard_map/all_to_all | solution.py:85
  79.8 1.1 broadcast_in_dim.59
  80.9 0.1 copy-done.2
  81.1 6.9 %all-to-all-start.3 = ((bf16[16,8,3584]{2,1,0:T(8,128)(2,1)}), bf16[16,8,3584]{2,1,0:T(8,128)(2,1)S(1)}, u32[]{:S(2)}, u32[]{:S(2)}) async-start(bf16[16,8,3584]{2,1,0:T(8,128)(2,1)} %bitcast.138), calls=%async_computation.3 | async-start | bytes 1835008 | tf_op jit(solution)/shard_map/all_to_all | solution.py:84
  88.0 2.7 fusion.21
  90.7 57.3 %all-gather.8.cloned.1.call-done = bf16[1,512,3584]{2,1,0:T(8,128)(2,1)} async-done(((bf16[1,256,3584]{2,1,0:T(8,128)(2,1)}), bf16[1,512,3584]{2,1,0:T(8,128)(2,1)}) %all-gather.8.cloned.1.call-update) | async-done | bytes 3670032 | tf_op jit(solution)/shard_map/all_gather | solution.py:93
  148.0 57.4 %all-gather.6.cloned.1.call-done = bf16[1,3584,512]{2,1,0:T(8,128)(2,1)} async-done(((bf16[1,3584,256]{2,1,0:T(8,128)(2,1)}), bf16[1,3584,512]{2,1,0:T(8,128)(2,1)}) %all-gather.6.cloned.1.call-update) | async-done | bytes 3670032 | tf_op jit(solution)/shard_map/all_gather | solution.py:92
  205.4 5.3 %convolution_convert_fusion = bf16[16,8,3584]{2,1,0:T(8,128)(2,1)} fusion(bf16[1,512,3584]{2,1,0:T(8,128)(2,1)} %all-gather.8.cloned.1.call-done, bf16[1,3584,512]{2,1,0:T(8,128)(2,1)} %all-gather.6.cloned.1.call-done, bf16[16,8,3584]{2,1,0:T(8,128)(2,1)S(1)} %all-to-all-done, f32[128,512]{1,0:T(8,128)S(1)} %fusion.21), kind=kOutput, calls=%fused_computation.6 | convolution fusion | flops 940376064 | bytes 9437184 | tf_op jit(solution)/shard_map/dot_general | solution.py:19
  210.7 9.0 %all-to-all-start.1 = ((bf16[16,8,3584]{2,1,0:T(8,128)(2,1)}), bf16[16,8,3584]{2,1,0:T(8,128)(2,1)}, u32[]{:S(2)}, u32[]{:S(2)}) async-start(bf16[16,8,3584]{2,1,0:T(8,128)(2,1)} %convolution_convert_fusion), calls=%async_computation.1 | async-start | bytes 1835008 | tf_op jit(solution)/shard_map/all_to_all | solution.py:99
  219.8 3.7 %fusion.10 = f32[128,512]{1,0:T(8,128)S(1)} fusion(bf16[1,512,3584]{2,1,0:T(8,128)(2,1)} %all-gather.8.cloned.1.call-done, bf16[16,8,3584]{2,1,0:T(8,128)(2,1)} %copy-done.2), kind=kOutput, calls=%fused_computation.17 | convolution fusion | flops 469762048 | bytes 4849664 | tf_op jit(solution)/shard_map/dot_general | solution.py:25
  223.5 0.6 fusion.19
  224.2 6.4 %fusion.17 = f32[128,3584]{1,0:T(8,128)} fusion(bf16[1,3584,512]{2,1,0:T(8,128)(2,1)} %all-gather.4.cloned.1.call-done, f32[128,512]{1,0:T(8,128)S(1)} %fusion.10, bf16[1,3584,512]{2,1,0:T(8,128)(2,1)} %all-gather.6.cloned.1.call-done, bf16[16,8,3584]{2,1,0:T(8,128)(2,1)S(1)} %all-to-all-done.3, f32[128,512]{1,0:T(8,128)S(1)} %fusion.19), kind=kOutput, calls=%fused_computation.24 | convolution fusion | flops 940179456 | bytes 10616832 | tf_op jit(solution)/shard_map/dot_general | solution.py:31
  230.5 4.9 %fusion.5 = bf16[16,8,3584]{2,1,0:T(8,128)(2,1)} fusion(f32[128,3584]{1,0:T(8,128)} %fusion.17, bf16[1,3584,512]{2,1,0:T(8,128)(2,1)} %all-gather.6.cloned.1.call-done, f32[128,512]{1,0:T(8,128)S(1)} %fusion.10, f32[128,512]{1,0:T(8,128)S(1)} %fusion.19), kind=kOutput, calls=%fused_computation.9 | convolution fusion | flops 471072768 | bytes 6946816 | tf_op jit(solution)/shard_map/dot_general | solution.py:31
  235.5 7.7 %all-to-all-done.1 = bf16[16,8,3584]{2,1,0:T(8,128)(2,1)} async-done(((bf16[16,8,3584]{2,1,0:T(8,128)(2,1)}), bf16[16,8,3584]{2,1,0:T(8,128)(2,1)}, u32[]{:S(2)}, u32[]{:S(2)}) %all-to-all-start.1) | async-done | bytes 917536 | tf_op jit(solution)/shard_map/all_to_all | solution.py:99
  243.2 6.9 %all-to-all-start.4 = ((bf16[16,8,3584]{2,1,0:T(8,128)(2,1)}), bf16[16,8,3584]{2,1,0:T(8,128)(2,1)}, u32[]{:S(2)}, u32[]{:S(2)}) async-start(bf16[16,8,3584]{2,1,0:T(8,128)(2,1)} %fusion.5), calls=%async_computation.4 | async-start | bytes 1835008 | tf_op jit(solution)/shard_map/all_to_all | solution.py:102
  250.4 1.3 bitcast_reduce_fusion.1
  251.7 1.9 fusion.4
  253.6 3.9 %collective-permute-start = (bf16[1,128,3584]{2,1,0:T(8,128)(2,1)}, bf16[1,128,3584]{2,1,0:T(8,128)(2,1)S(1)}, u32[]{:S(2)}, u32[]{:S(2)}) collective-permute-start(bf16[1,128,3584]{2,1,0:T(8,128)(2,1)} %fusion.4), channel_id=1, source_target_pairs={{0,32},{32,64},{64,96},{96,128},{128,160},{160,192},{192,224},{1,3... | collective-permute-start | bytes 2752520 | tf_op jit(solution)/shard_map/ppermute | solution.py:12
  257.5 16.1 %all-to-all-done.4 = bf16[16,8,3584]{2,1,0:T(8,128)(2,1)} async-done(((bf16[16,8,3584]{2,1,0:T(8,128)(2,1)}), bf16[16,8,3584]{2,1,0:T(8,128)(2,1)}, u32[]{:S(2)}, u32[]{:S(2)}) %all-to-all-start.4) | async-done | bytes 917536 | tf_op jit(solution)/shard_map/all_to_all | solution.py:102
  273.6 1.3 bitcast_reduce_fusion
  274.9 1.0 fusion.3
  275.9 5.1 %collective-permute-start.1 = (bf16[1,128,3584]{2,1,0:T(8,128)(2,1)S(1)}, bf16[1,128,3584]{2,1,0:T(8,128)(2,1)S(1)}, u32[]{:S(2)}, u32[]{:S(2)}) collective-permute-start(bf16[1,128,3584]{2,1,0:T(8,128)(2,1)S(1)} %fusion.3), channel_id=1, source_target_pairs={{32,0},{64,32},{96,64},{128,96},{160,128},{192,160},{224,192},{33,... | collective-permute-start | bytes 2752520 | tf_op jit(solution)/shard_map/ppermute | solution.py:12
  281.1 12.1 %collective-permute-done.1 = bf16[1,128,3584]{2,1,0:T(8,128)(2,1)S(1)} collective-permute-done((bf16[1,128,3584]{2,1,0:T(8,128)(2,1)S(1)}, bf16[1,128,3584]{2,1,0:T(8,128)(2,1)S(1)}, u32[]{:S(2)}, u32[]{:S(2)}) %collective-permute-start.1) | collective-permute-done | bytes 917536 | tf_op jit(solution)/shard_map/ppermute | solution.py:12
  293.2 0.9 copy.50
  294.1 0.9 copy.51
  (53 shorter events, 1.4 us)
Async XLA Ops:
  7.2 49.3 %copy-start = (bf16[1,128,3584]{2,1,0:T(8,128)(2,1)S(1)}, bf16[1,128,3584]{2,1,0:T(8,128)(2,1)}, u32[]{:S(2)}) copy-start(bf16[1,128,3584]{2,1,0:T(8,128)(2,1)} %param.13) | copy-start | bytes 2752516
  7.2 1.5 copy-start.7
  7.2 5.1 %copy-start.3 = (bf16[1,128,3584]{2,1,0:T(8,128)(2,1)S(1)}, bf16[1,128,3584]{2,1,0:T(8,128)(2,1)}, u32[]{:S(2)}) copy-start(bf16[1,128,3584]{2,1,0:T(8,128)(2,1)} %param.10) | copy-start | bytes 2752516
  7.2 80.8 %all-gather.4.cloned.1.call-start = ((), (), s32[]{:S(2)}) async-start(), calls=%async_computation.5 | async-start | bytes 5505024 | tf_op jit(solution)/shard_map/all_gather | solution.py:91
  7.9 140.1 %all-gather.8.cloned.1.call-start = ((), (), s32[]{:S(2)}) async-start(), calls=%async_computation.7 | async-start | bytes 5505024 | tf_op jit(solution)/shard_map/all_gather | solution.py:93
  8.7 17.2 %copy-start.8 = (s32[1,128,8]{1,2,0:T(8,128)S(1)}, s32[1,128,8]{1,2,0:T(8,128)}, u32[]{:S(2)}) copy-start(s32[1,128,8]{1,2,0:T(8,128)} %param.14) | copy-start | bytes 12292
  11.8 17.7 %copy-start.5 = (bf16[1,128,3584]{2,1,0:T(8,128)(2,1)S(1)}, bf16[1,128,3584]{2,1,0:T(8,128)(2,1)}, u32[]{:S(2)}) copy-start(bf16[1,128,3584]{2,1,0:T(8,128)(2,1)} %param.16) | copy-start | bytes 2752516
  13.6 35.0 %all-to-all-start = ((bf16[16,8,3584]{2,1,0:T(8,128)(2,1)}), bf16[16,8,3584]{2,1,0:T(8,128)(2,1)S(1)}, u32[]{:S(2)}, u32[]{:S(2)}) async-start(bf16[16,8,3584]{2,1,0:T(8,128)(2,1)} %bitcast.137), calls=%async_computation | async-start | bytes 1835008 | tf_op jit(solution)/shard_map/all_to_all | solution.py:82
  25.2 180.3 %all-gather.6.cloned.1.call-start = ((), (), s32[]{:S(2)}) async-start(), calls=%async_computation.6 | async-start | bytes 5505024 | tf_op jit(solution)/shard_map/all_gather | solution.py:92
  49.6 30.3 %all-to-all-start.2 = ((bf16[16,8,3584]{2,1,0:T(8,128)(2,1)}), bf16[16,8,3584]{2,1,0:T(8,128)(2,1)S(1)}, u32[]{:S(2)}, u32[]{:S(2)}) async-start(bf16[16,8,3584]{2,1,0:T(8,128)(2,1)} %bitcast.139), calls=%async_computation.2 | async-start | bytes 1835008 | tf_op jit(solution)/shard_map/all_to_all | solution.py:85
  79.8 1.2 copy-start.2
  81.1 129.7 %all-to-all-start.3 = ((bf16[16,8,3584]{2,1,0:T(8,128)(2,1)}), bf16[16,8,3584]{2,1,0:T(8,128)(2,1)S(1)}, u32[]{:S(2)}, u32[]{:S(2)}) async-start(bf16[16,8,3584]{2,1,0:T(8,128)(2,1)} %bitcast.138), calls=%async_computation.3 | async-start | bytes 1835008 | tf_op jit(solution)/shard_map/all_to_all | solution.py:84
  210.7 32.5 %all-to-all-start.1 = ((bf16[16,8,3584]{2,1,0:T(8,128)(2,1)}), bf16[16,8,3584]{2,1,0:T(8,128)(2,1)}, u32[]{:S(2)}, u32[]{:S(2)}) async-start(bf16[16,8,3584]{2,1,0:T(8,128)(2,1)} %convolution_convert_fusion), calls=%async_computation.1 | async-start | bytes 1835008 | tf_op jit(solution)/shard_map/all_to_all | solution.py:99
  219.8 3.8 %copy-start.1 = (bf16[1,3584,512]{2,1,0:T(8,128)(2,1)S(1)}, bf16[1,3584,512]{2,1,0:T(8,128)(2,1)}, u32[]{:S(2)}) copy-start(bf16[1,3584,512]{2,1,0:T(8,128)(2,1)} %all-gather.4.cloned.1.call-done) | copy-start | bytes 11010052
  230.5 19.6 %copy-start.9 = (f32[1,128,8]{1,2,0:T(8,128)S(1)}, f32[1,128,8]{1,2,0:T(8,128)}, u32[]{:S(2)}) copy-start(f32[1,128,8]{1,2,0:T(8,128)} %param.12) | copy-start | bytes 12292
  230.5 19.6 %copy-start.10 = (f32[1,128,8]{1,2,0:T(8,128)S(1)}, f32[1,128,8]{1,2,0:T(8,128)}, u32[]{:S(2)}) copy-start(f32[1,128,8]{1,2,0:T(8,128)} %param.15) | copy-start | bytes 12292
  230.5 21.2 %copy-start.4 = (bf16[1,128,3584]{2,1,0:T(8,128)(2,1)S(1)}, bf16[1,128,3584]{2,1,0:T(8,128)(2,1)}, u32[]{:S(2)}) copy-start(bf16[1,128,3584]{2,1,0:T(8,128)(2,1)} %param.10) | copy-start | bytes 2752516
  235.5 39.4 %copy-start.6 = (bf16[1,128,3584]{2,1,0:T(8,128)(2,1)S(1)}, bf16[1,128,3584]{2,1,0:T(8,128)(2,1)}, u32[]{:S(2)}) copy-start(bf16[1,128,3584]{2,1,0:T(8,128)(2,1)} %param.16) | copy-start | bytes 2752516
  243.2 30.4 %all-to-all-start.4 = ((bf16[16,8,3584]{2,1,0:T(8,128)(2,1)}), bf16[16,8,3584]{2,1,0:T(8,128)(2,1)}, u32[]{:S(2)}, u32[]{:S(2)}) async-start(bf16[16,8,3584]{2,1,0:T(8,128)(2,1)} %fusion.5), calls=%async_computation.4 | async-start | bytes 1835008 | tf_op jit(solution)/shard_map/all_to_all | solution.py:102
  253.6 27.5 %collective-permute-start = (bf16[1,128,3584]{2,1,0:T(8,128)(2,1)}, bf16[1,128,3584]{2,1,0:T(8,128)(2,1)S(1)}, u32[]{:S(2)}, u32[]{:S(2)}) collective-permute-start(bf16[1,128,3584]{2,1,0:T(8,128)(2,1)} %fusion.4), channel_id=1, source_target_pairs={{0,32},{32,64},{64,96},{96,128},{128,160},{160,192},{192,224},{1,3... | collective-permute-start | bytes 2752520 | tf_op jit(solution)/shard_map/ppermute | solution.py:12
  275.9 17.3 %collective-permute-start.1 = (bf16[1,128,3584]{2,1,0:T(8,128)(2,1)S(1)}, bf16[1,128,3584]{2,1,0:T(8,128)(2,1)S(1)}, u32[]{:S(2)}, u32[]{:S(2)}) collective-permute-start(bf16[1,128,3584]{2,1,0:T(8,128)(2,1)S(1)} %fusion.3), channel_id=1, source_target_pairs={{32,0},{64,32},{96,64},{128,96},{160,128},{192,160},{224,192},{33,... | collective-permute-start | bytes 2752520 | tf_op jit(solution)/shard_map/ppermute | solution.py:12
Sparse Core Ops, SparseCore 0:
  9.8 77.1 all-gather.3
  88.8 59.1 all-gather.7
  149.8 55.5 all-gather.5
where the time goes:
time: 302 us
  waiting for transfers between devices  195 us (65%)
  starting transfers between devices  50.3 us (17%)
  matrix products  27.3 us (9%)
  between operations  14.1 us (5%)
  other arithmetic  8.17 us (3%)
  local copies, waits for them, and re-layouts  6.83 us (2%)
    all_gather x1, waiting for transfers between devices, per_device(): lax.all_gather(w_up, 'dp', axis=2, tiled=True)  57.4 us
    all_gather x1, waiting for transfers between devices, per_device(): lax.all_gather(w_down, 'dp', axis=1, tiled=True)  57.3 us
    all_to_all x1, waiting for transfers between devices, per_device(): lax.all_to_all(send_grad, 'expert', split_axis=0, concat_axis=0, tiled=True)  23.1 us
    all_to_all x1, waiting for transfers between devices, per_device(): lax.all_to_all(send_fwd, 'expert', split_axis=0, concat_axis=0, tiled=True)  18.8 us
    all_to_all x1, waiting for transfers between devices, per_device(): lax.all_to_all(bwd_result.astype(jnp.bfloat16), 'expert', split_axis=0, c...  16.1 us
    ppermute x2, waiting for transfers between devices, from_behind(): lax.ppermute(value, axis, [(source, source + steps) for source in range(i...  12.1 us
    all_to_all x1, starting transfers between devices, per_device(): lax.all_to_all(send_fwd, 'expert', split_axis=0, concat_axis=0, tiled=True)  11.6 us
    ppermute x2, starting transfers between devices, from_behind(): lax.ppermute(value, axis, [(source, source + steps) for source in range(i...  9.01 us
  transfers between devices with their start and end apart: 10, of which 7 were waited for; matrix products, arithmetic and copies ran while one was open for 13% of the time, Pallas kernels for 0%

commit v1 on v0

v1 whole, which is shorter than its diff:
```python
import jax
import jax.numpy as jnp
from jax import lax
from jax.experimental import pallas as pl
from jax.experimental.pallas import tpu as pltpu
from jax.sharding import PartitionSpec as P

CAP = 8
PAIRS = 4
BLOCK = 2 * CAP
HALF = PAIRS * CAP
HOME = PAIRS * BLOCK
BF16 = jnp.bfloat16
F32 = jnp.float32
CHUNKS = 2


def call(body, outs, args, flops=0, smem=()):
    total = sum(a.size * a.dtype.itemsize for a in args)
    total += sum(o.size * o.dtype.itemsize for o in outs)
    specs = [
        pl.BlockSpec(memory_space=pltpu.SMEM if i in smem else pltpu.VMEM)
        for i in range(len(args))
    ]
    return pl.pallas_call(
        body,
        out_shape=tuple(outs),
        in_specs=specs,
        out_specs=tuple(pl.BlockSpec(memory_space=pltpu.VMEM) for _ in outs),
        compiler_params=pltpu.CompilerParams(vmem_limit_bytes=48 * 1024 * 1024),
        cost_estimate=pl.CostEstimate(flops=flops, bytes_accessed=total, transcendentals=0),
    )(*args)


def shape(rows, cols, dtype=BF16):
    return jax.ShapeDtypeStruct((rows, cols), dtype)


def dot(a, b):
    return lax.dot_general(a, b, (((1,), (0,)), ((), ())), preferred_element_type=F32)


def dot_t(a, b):
    return lax.dot_general(a, b, (((1,), (1,)), ((), ())), preferred_element_type=F32)


def section_perm(move):
    pairs = []
    for xh in range(2):
        for z in range(8):
            for d in range(2):
                nxh, nz, nd = move(xh, z, d)
                pairs.append(((xh * 8 + z) * 2 + d, (nxh * 8 + nz % 8) * 2 + nd))
    return pairs


def inverse(pairs):
    return [(b, a) for a, b in pairs]


ACROSS_XHI = section_perm(lambda xh, z, d: (1 - xh, z, 1 - d))
SHIFT_A = section_perm(lambda xh, z, d: (xh, z + (2 if z % 2 == 0 else -2), d))
SHIFT_B = section_perm(lambda xh, z, d: (xh, z + (-1 if z % 2 == 0 else 1), d))
SHIFT_C = section_perm(lambda xh, z, d: (xh, z + (-3 if z % 2 == 0 else 3), d))
Z_PAIR = section_perm(lambda xh, z, d: (xh, z ^ 1, d))
DP_PAIR = section_perm(lambda xh, z, d: (xh, z, 1 - d))
STAY = section_perm(lambda xh, z, d: (xh, z, d))


def move(value, pairs):
    return lax.ppermute(value, ("expert", "dp"), pairs)


def relay(value, pairs, step):
    sections = lax.axis_size("pipe")
    size = len(pairs)
    full = []
    for s in range(sections):
        t = s + step
        if 0 <= t < sections:
            full += [(s * size + a, t * size + b) for a, b in pairs]
    return lax.ppermute(value, ("pipe", "expert", "dp"), full)


def slot_tables(where_ref, ids_ref, score_ref):
    tokens = ids_ref.shape[0]
    where = where_ref[0]
    xh = where // 8
    z = where % 8
    pair = z // 2
    sign = 1 - 2 * (z % 2)
    shape2 = (tokens, 2 * HOME)
    lane = lax.broadcasted_iota(jnp.int32, shape2, 1)
    slot = lane & (HOME - 1)
    half = slot >> 5
    q = (slot >> 3) & 3
    rank_of = slot & 7
    gray = q ^ (q >> 1)
    expert = (xh ^ half) * PAIRS + ((pair + sign * gray) & 3)
    ids = ids_ref[...]
    score = score_ref[...]
    mix = 2.5 * score / jnp.sum(score, axis=1, keepdims=True)
    hit = jnp.zeros(shape2, F32)
    weight = jnp.zeros(shape2, F32)
    for k in range(ids.shape[1]):
        same = ids[:, k : k + 1] == expert
        hit = jnp.where(same, 1.0, hit)
        weight = jnp.where(same, mix[:, k : k + 1], weight)
    row = lax.broadcasted_iota(jnp.int32, (tokens, tokens), 0)
    col = lax.broadcasted_iota(jnp.int32, (tokens, tokens), 1)
    before = jnp.where(row > col, 1.0, 0.0).astype(BF16)
    rank = dot(before, hit.astype(BF16))
    taken = jnp.where((hit > 0.0) & (rank == rank_of.astype(F32)), 1.0, 0.0)
    weight = weight * taken
    high = weight.astype(BF16).astype(F32)
    comb = jnp.where(lane < HOME, high, weight - high).astype(BF16)
    dispatch = jnp.transpose(taken)[:HOME].astype(BF16)
    return dispatch, comb


def pack_one(where_ref, ids_ref, score_ref, tok_ref, own_ref, far_ref, comb_ref):
    dispatch, comb = slot_tables(where_ref, ids_ref, score_ref)
    comb_ref[...] = comb
    own_ref[...] = dot(dispatch[:HALF], tok_ref[...]).astype(BF16)
    far_ref[...] = dot(dispatch[HALF:], tok_ref[...]).astype(BF16)


def pack_two(
    where_ref, ids_ref, score_ref, tok_ref, cot_ref,
    own_ref, far_ref, cown_ref, cfar_ref, comb_ref,
):
    dispatch, comb = slot_tables(where_ref, ids_ref, score_ref)
    comb_ref[...] = comb
    own_ref[...] = dot(dispatch[:HALF], tok_ref[...]).astype(BF16)
    far_ref[...] = dot(dispatch[HALF:], tok_ref[...]).astype(BF16)
    cown_ref[...] = dot(dispatch[:HALF], cot_ref[...]).astype(BF16)
    cfar_ref[...] = dot(dispatch[HALF:], cot_ref[...]).astype(BF16)


def weave_body(own_ref, got_ref, *block_refs):
    own = own_ref[...].astype(F32)
    got = got_ref[...].astype(F32)
    for q, ref in enumerate(block_refs):
        rows = slice(q * CAP, (q + 1) * CAP)
        ref[...] = jnp.concatenate([own[rows], got[rows]], axis=0).astype(BF16)


def part_body(b0, b1, b2, b3, own_ref, far_ref):
    blocks = [b[...].astype(F32) for b in (b0, b1, b2, b3)]
    own_ref[...] = jnp.concatenate([b[:CAP] for b in blocks], axis=0).astype(BF16)
    far_ref[...] = jnp.concatenate([b[CAP:] for b in blocks], axis=0).astype(BF16)


def hidden_body(a_ref, b_ref, wg_ref, wu_ref, out_ref):
    rows = jnp.concatenate([a_ref[...], b_ref[...]], axis=0)
    gate = dot(rows, wg_ref[...])
    up = dot(rows, wu_ref[...])
    out_ref[...] = (gate * jax.nn.sigmoid(gate) * up).astype(BF16)


def down_body(mine_ref, theirs_ref, wd_ref, wdp_ref, keep_ref, send_ref):
    total = dot(mine_ref[...], wd_ref[...]) + dot(theirs_ref[...], wdp_ref[...])
    keep_ref[...] = total[:HOME]
    send_ref[...] = total[HOME:].astype(BF16)


def finish_body(keep_ref, got_ref, *block_refs):
    total = keep_ref[...] + got_ref[...].astype(F32)
    for q, ref in enumerate(block_refs):
        ref[...] = total[q * BLOCK : (q + 1) * BLOCK].astype(BF16)


def slopes(rows, wg_ref, wu_ref):
    gate = dot(rows, wg_ref[...])
    up = dot(rows, wu_ref[...])
    sigma = jax.nn.sigmoid(gate)
    return up * sigma * (1.0 + gate * (1.0 - sigma)), gate * sigma


def slope_body(a_ref, b_ref, wg_ref, wu_ref, sg_ref, su_ref):
    rows = jnp.concatenate([a_ref[...], b_ref[...]], axis=0)
    sg, su = slopes(rows, wg_ref, wu_ref)
    sg_ref[...] = sg
    su_ref[...] = su


def grad_hidden_body(a_ref, b_ref, wd_ref, wdp_ref, mine_ref, send_ref):
    rows = jnp.concatenate([a_ref[...], b_ref[...]], axis=0)
    mine_ref[...] = dot_t(rows, wd_ref[...])
    send_ref[...] = dot_t(rows, wdp_ref[...])


def grads_body(
    a_ref, b_ref, wg_ref, wu_ref, sg_ref, su_ref, mine_ref, got_ref, gg_ref, gu_ref
):
    rows = jnp.concatenate([a_ref[...], b_ref[...]], axis=0)
    count = rows.shape[0]
    sgx, sux = slopes(rows, wg_ref, wu_ref)
    mine = mine_ref[...]
    got = got_ref[...]
    gg_ref[:count] = (mine * sg_ref[...]).astype(BF16)
    gg_ref[count:] = (got * sgx).astype(BF16)
    gu_ref[:count] = (mine * su_ref[...]).astype(BF16)
    gu_ref[count:] = (got * sux).astype(BF16)


def back_body(gg_ref, gu_ref, wg_ref, wu_ref, keep_ref, send_ref):
    total = dot_t(gg_ref[...], wg_ref[...]) + dot_t(gu_ref[...], wu_ref[...])
    count = keep_ref.shape[0]
    keep_ref[...] = total[:count]
    send_ref[...] = total[count:].astype(BF16)


def fold_body(keep_ref, got_ref, own_ref, send_ref):
    total = keep_ref[...] + got_ref[...].astype(F32)
    own_ref[...] = total[:HOME]
    send_ref[...] = total[HOME:].astype(BF16)


def combine_body(base_ref, comb_ref, *rest):
    out_ref = rest[-1]
    comb = comb_ref[...]
    col = 0
    for i in range(0, len(rest) - 1, 2):
        rows = jnp.concatenate([rest[i][...], rest[i + 1][...]], axis=0)
        width = rows.shape[1]
        cols = slice(col, col + width)
        total = dot(comb, jnp.concatenate([rows, rows], axis=0))
        out_ref[:, cols] = (base_ref[:, cols].astype(F32) + total).astype(BF16)
        col += width


def back_call(gg, gu, wg, wu, index, chunks):
    width = wg.shape[0] // chunks
    rows = gg.shape[0]
    whole = pl.BlockSpec((rows, gg.shape[1]), lambda i: (0, 0))
    part = pl.BlockSpec((width, wg.shape[1]), lambda i: (index, 0))
    half = rows // 2
    return pl.pallas_call(
        back_body,
        grid=(1,),
        out_shape=(shape(half, width, F32), shape(half, width)),
        in_specs=[whole, whole, part, part],
        out_specs=(
            pl.BlockSpec((half, width), lambda i: (0, 0)),
            pl.BlockSpec((half, width), lambda i: (0, 0)),
        ),
        compiler_params=pltpu.CompilerParams(vmem_limit_bytes=48 * 1024 * 1024),
        cost_estimate=pl.CostEstimate(
            flops=4 * rows * width * gg.shape[1],
            bytes_accessed=4 * width * wg.shape[1] + 6 * half * width,
            transcendentals=0,
        ),
    )(gg, gu, wg, wu)


def gather_home(own, far):
    width = own.shape[1]
    got = move(far, ACROSS_XHI)
    blocks = call(weave_body, [shape(BLOCK, width)] * PAIRS, [own, got])
    home = jnp.concatenate(
        [
            blocks[0],
            move(blocks[1], SHIFT_A),
            move(blocks[2], SHIFT_B),
            move(blocks[3], SHIFT_C),
        ],
        axis=0,
    )
    return home, move(home, Z_PAIR)


def send_back(blocks, step):
    width = blocks[0].shape[1]
    b0 = blocks[0]
    b1 = move(blocks[1], inverse(SHIFT_A))
    b2 = move(blocks[2], inverse(SHIFT_B))
    b3 = move(blocks[3], inverse(SHIFT_C))
    own, far = call(part_body, [shape(HALF, width)] * 2, [b0, b1, b2, b3])
    return relay(own, STAY, step), relay(far, ACROSS_XHI, step)


def per_device(
    fwd_in, fwd_ids, fwd_score, bwd_in, bwd_ids, bwd_score, bwd_cot, w_gate, w_up, w_down
):
    tokens, width = fwd_in.shape[1:]
    wg, wu, wd = w_gate[0], w_up[0], w_down[0]
    hid = wg.shape[1]
    wdp = move(wd, DP_PAIR)
    where = lax.axis_index("expert").astype(jnp.int32).reshape(1)
    packed = [shape(HALF, width)] * 2
    table = [shape(tokens, 2 * HOME)]

    own, far, fcomb = call(
        pack_one, packed + table, [where, fwd_ids[0], fwd_score[0], fwd_in[0]], smem=(0,)
    )
    fy, fyz = gather_home(own, far)
    bown, bfar, cown, cfar, bcomb = call(
        pack_two,
        packed * 2 + table,
        [where, bwd_ids[0], bwd_score[0], bwd_in[0], bwd_cot[0]],
        smem=(0,),
    )
    by, byz = gather_home(bown, bfar)
    cy, cyz = gather_home(cown, cfar)
    fyx, fyzx = move(fy, DP_PAIR), move(fyz, DP_PAIR)
    byx, byzx = move(by, DP_PAIR), move(byz, DP_PAIR)

    fbase = relay(fwd_in[0], STAY, 1)
    fcomb = relay(fcomb, STAY, 1)
    bbase = relay(bwd_cot[0], STAY, -1)
    bcomb = relay(bcomb, STAY, -1)

    rows = 2 * HOME
    proj = 4 * rows * width * hid
    (mine,) = call(hidden_body, [shape(rows, hid)], [fy, fyz, wg, wu], proj)
    (theirs,) = call(hidden_body, [shape(rows, hid)], [fyx, fyzx, wg, wu], proj)
    theirs = move(theirs, DP_PAIR)
    keep, send = call(
        down_body, [shape(HOME, width, F32), shape(HOME, width)], [mine, theirs, wd, wdp], proj
    )
    blocks = call(finish_body, [shape(BLOCK, width)] * PAIRS, [keep, move(send, Z_PAIR)])
    fown, ffar = send_back(blocks, 1)
    (fwd_out,) = call(combine_body, [shape(tokens, width)], [fbase, fcomb, fown, ffar])

    sg, su = call(slope_body, [shape(rows, hid, F32)] * 2, [by, byz, wg, wu], proj)
    gh, gh_send = call(
        grad_hidden_body, [shape(rows, hid, F32)] * 2, [cy, cyz, wd, wdp], proj
    )
    gh_got = move(gh_send, DP_PAIR)
    gg, gu = call(
        grads_body,
        [shape(2 * rows, hid)] * 2,
        [byx, byzx, wg, wu, sg, su, gh, gh_got],
        proj,
    )
    pieces = []
    for index in range(CHUNKS):
        part = width // CHUNKS
        keep, send = back_call(gg, gu, wg, wu, index, CHUNKS)
        keep, send = call(
            fold_body,
            [shape(HOME, part, F32), shape(HOME, part)],
            [keep, move(send, DP_PAIR)],
        )
        blocks = call(finish_body, [shape(BLOCK, part)] * PAIRS, [keep, move(send, Z_PAIR)])
        pieces += send_back(blocks, -1)
    (bwd_out,) = call(combine_body, [shape(tokens, width)], [bbase, bcomb] + pieces)
    return fwd_out[None], bwd_out[None]


def solution(mesh):
    rows = P("pipe", ("expert", "dp"), None)
    cols = P("pipe", None, ("expert", "dp"))
    return jax.shard_map(
        per_device,
        mesh=mesh,
        in_specs=(rows,) * 7 + (cols, cols, rows),
        out_specs=(rows, rows),
        check_vma=False,
    )
```

time: 302 us -> 206 us (0.68)
  waiting for transfers between devices: 195 us -> 82 us
  starting transfers between devices: 50.3 us -> 101 us
  matrix products: 27.3 us -> 0 us
  Pallas kernels: 0 us -> 14 us
  between operations: 14.1 us -> 1.16 us
  other arithmetic: 8.17 us -> 0 us
    all_gather x3 -> x0, waiting for transfers between devices: 115 us -> none  [the longest x1 57.4 us: per_device(): lax.all_gather(w_up, 'dp', axis=2, tiled=True)]
    ppermute x2 -> x46, starting transfers between devices: 9.01 us -> 101 us  [the longest x36 55.3 us: move(): return lax.ppermute(value, ('expert', 'dp'), pairs)]
    ppermute x2 -> x46, waiting for transfers between devices: 12.1 us -> 82 us  [the longest x36 68.2 us: move(): return lax.ppermute(value, ('expert', 'dp'), pairs)]
    all_to_all x5 -> x0, waiting for transfers between devices: 65.8 us -> none  [the longest x1 23.1 us: per_device(): lax.all_to_all(send_grad, 'expert', split_axis=0, concat_axis=0, tiled=True)]
    all_to_all x5 -> x0, starting transfers between devices: 41.2 us -> none  [the longest x1 11.6 us: per_device(): lax.all_to_all(send_fwd, 'expert', split_axis=0, concat_axis=0, tiled=True)]
    dot_general x11 -> x0, matrix products: 27.3 us -> none  [the longest x1 6.36 us: expert_backward(): jnp.dot(grad_gate, gate_w.T, preferred_element_type=jnp.float32)]
    pallas_call x0 -> x23, Pallas kernels: none -> 14 us  [the longest x21 12.7 us: call(): pl.pallas_call(body, out_shape=tuple(outs), in_specs=specs, out_specs=tup...]
    another operation x4 -> x0, other arithmetic: 4.86 us -> none
  transfers between devices with their start and end apart: 10 -> 46, of which waited for: 7 -> 17; matrix products, arithmetic and copies ran while one was open for 13% -> 0% of each run, Pallas kernels for 0% -> 6%
where the time goes in v1:
time: 206 us; the launch traced here: 204 us
  starting transfers between devices  101 us (49%)
  waiting for transfers between devices  82 us (40%)
  Pallas kernels  14 us (7%)
  local copies, waits for them, and re-layouts  5.58 us (3%)
    ppermute x36, waiting for transfers between devices, move(): return lax.ppermute(value, ('expert', 'dp'), pairs)  68.2 us
    ppermute x36, starting transfers between devices, move(): return lax.ppermute(value, ('expert', 'dp'), pairs)  55.3 us
    ppermute x10, starting transfers between devices, relay(): return lax.ppermute(value, ('pipe', 'expert', 'dp'), full)  46.1 us
    ppermute x10, waiting for transfers between devices, relay(): return lax.ppermute(value, ('pipe', 'expert', 'dp'), full)  13.8 us
    pallas_call x21, Pallas kernels, call(): pl.pallas_call(body, out_shape=tuple(outs), in_specs=specs, out_specs=tup...  12.7 us
    unnamed x33, local copies, waits for them, and re-layouts  5.55 us
  transfers between devices with their start and end apart: 46, of which 17 were waited for; matrix products, arithmetic and copies ran while one was open for 0% of the time, Pallas kernels for 6%

profile of v1, /device:TPU:1, one launch (start us, length us, event | category | flops | bytes accessed | tf_op | source)
XLA Modules:
  0.0 204.2 jit_solution(11087620307621652729)
XLA Ops:
  5.8 3.4 %collective-permute-start.19 = (bf16[32,3584]{1,0:T(8,128)(2,1)S(1)}, bf16[32,3584]{1,0:T(8,128)(2,1)S(1)}, u32[]{:S(2)}, u32[]{:S(2)}) collective-permute-start(bf16[32,3584]{1,0:T(8,128)(2,1)S(1)} %get-tuple-element.73), channel_id=1, source_target_pairs={{0,17},{1,16},{2,19},{3,18},{4,21},{5,20},{6,23},{7,22},{8,25},{9,... | collective-permute-start | bytes 688136 | tf_op jit(solution)/shard_map/ppermute | solution.py:71
  11.7 2.6 %collective-permute-start.2 = (bf16[32,3584]{1,0:T(8,128)(2,1)S(1)}, bf16[32,3584]{1,0:T(8,128)(2,1)S(1)}, u32[]{:S(2)}, u32[]{:S(2)}) collective-permute-start(bf16[32,3584]{1,0:T(8,128)(2,1)S(1)} %get-tuple-element.58), channel_id=1, source_target_pairs={{0,17},{1,16},{2,19},{3,18},{4,21},{5,20},{6,23},{7,22},{8,25},{9,... | collective-permute-start | bytes 688136 | tf_op jit(solution)/shard_map/ppermute | solution.py:71
  14.3 3.2 %collective-permute-start.20 = (bf16[16,3584]{1,0:T(8,128)(2,1)S(1)}, bf16[16,3584]{1,0:T(8,128)(2,1)S(1)}, u32[]{:S(2)}, u32[]{:S(2)}) collective-permute-start(bf16[16,3584]{1,0:T(8,128)(2,1)S(1)} %get-tuple-element.75), channel_id=1, source_target_pairs={{0,4},{1,5},{2,14},{3,15},{4,8},{5,9},{6,2},{7,3},{8,12},{9,13},{1... | collective-permute-start | bytes 344072 | tf_op jit(solution)/shard_map/ppermute | solution.py:71
  17.5 3.7 %collective-permute-start.21 = (bf16[16,3584]{1,0:T(8,128)(2,1)S(1)}, bf16[16,3584]{1,0:T(8,128)(2,1)S(1)}, u32[]{:S(2)}, u32[]{:S(2)}) collective-permute-start(bf16[16,3584]{1,0:T(8,128)(2,1)S(1)} %get-tuple-element.76), channel_id=1, source_target_pairs={{0,14},{1,15},{2,4},{3,5},{4,2},{5,3},{6,8},{7,9},{8,6},{9,7},{10,... | collective-permute-start | bytes 344072 | tf_op jit(solution)/shard_map/ppermute | solution.py:71
  21.3 4.5 %collective-permute-start.22 = (bf16[16,3584]{1,0:T(8,128)(2,1)S(1)}, bf16[16,3584]{1,0:T(8,128)(2,1)S(1)}, u32[]{:S(2)}, u32[]{:S(2)}) collective-permute-start(bf16[16,3584]{1,0:T(8,128)(2,1)S(1)} %get-tuple-element.77), channel_id=1, source_target_pairs={{0,10},{1,11},{2,8},{3,9},{4,14},{5,15},{6,12},{7,13},{8,2},{9,3},... | collective-permute-start | bytes 344072 | tf_op jit(solution)/shard_map/ppermute | solution.py:71
  25.9 1.4 collective-permute-start.27
  27.3 3.8 %collective-permute-start.28 = (bf16[16,3584]{1,0:T(8,128)(2,1)S(1)}, bf16[16,3584]{1,0:T(8,128)(2,1)S(1)}, u32[]{:S(2)}, u32[]{:S(2)}) collective-permute-start(bf16[16,3584]{1,0:T(8,128)(2,1)S(1)} %get-tuple-element.84), channel_id=1, source_target_pairs={{0,14},{1,15},{2,4},{3,5},{4,2},{5,3},{6,8},{7,9},{8,6},{9,7},{10,... | collective-permute-start | bytes 344072 | tf_op jit(solution)/shard_map/ppermute | solution.py:71
  31.7 1.7 collective-permute-start.3
  33.5 4.2 %collective-permute-done.3 = bf16[16,3584]{1,0:T(8,128)(2,1)S(1)} collective-permute-done((bf16[16,3584]{1,0:T(8,128)(2,1)S(1)}, bf16[16,3584]{1,0:T(8,128)(2,1)S(1)}, u32[]{:S(2)}, u32[]{:S(2)}) %collective-permute-start.3) | collective-permute-done | bytes 114720 | tf_op jit(solution)/shard_map/ppermute | solution.py:71
  37.7 6.4 %collective-permute-start.4 = (bf16[16,3584]{1,0:T(8,128)(2,1)S(1)}, bf16[16,3584]{1,0:T(8,128)(2,1)S(1)}, u32[]{:S(2)}, u32[]{:S(2)}) collective-permute-start(bf16[16,3584]{1,0:T(8,128)(2,1)S(1)} %get-tuple-element.61), channel_id=1, source_target_pairs={{0,14},{1,15},{2,4},{3,5},{4,2},{5,3},{6,8},{7,9},{8,6},{9,7},{10,... | collective-permute-start | bytes 344072 | tf_op jit(solution)/shard_map/ppermute | solution.py:71
  44.0 2.5 %collective-permute-done.4 = bf16[16,3584]{1,0:T(8,128)(2,1)S(1)} collective-permute-done((bf16[16,3584]{1,0:T(8,128)(2,1)S(1)}, bf16[16,3584]{1,0:T(8,128)(2,1)S(1)}, u32[]{:S(2)}, u32[]{:S(2)}) %collective-permute-start.4) | collective-permute-done | bytes 114720 | tf_op jit(solution)/shard_map/ppermute | solution.py:71
  47.5 6.8 %collective-permute-done.5 = bf16[16,3584]{1,0:T(8,128)(2,1)S(1)} collective-permute-done((bf16[16,3584]{1,0:T(8,128)(2,1)S(1)}, bf16[16,3584]{1,0:T(8,128)(2,1)S(1)}, u32[]{:S(2)}, u32[]{:S(2)}) %collective-permute-start.5) | collective-permute-done | bytes 114720 | tf_op jit(solution)/shard_map/ppermute | solution.py:71
  54.3 1.5 collective-permute-start.6
  56.8 17.0 %collective-permute-done.6.b_ref = bf16[64,3584]{1,0:T(8,128)(2,1)S(1)} collective-permute-done((bf16[64,3584]{1,0:T(8,128)(2,1)S(1)}, bf16[64,3584]{1,0:T(8,128)(2,1)S(1)}, u32[]{:S(2)}, u32[]{:S(2)}) %collective-permute-start.6) | collective-permute-done | bytes 458784 | tf_op jit(solution)/shard_map/ppermute | solution.py:71
  73.9 1.5 collective-permute-start.23
  75.3 8.4 %collective-permute-done.30.b_ref = bf16[64,3584]{1,0:T(8,128)(2,1)S(1)} collective-permute-done((bf16[64,3584]{1,0:T(8,128)(2,1)S(1)}, bf16[64,3584]{1,0:T(8,128)(2,1)S(1)}, u32[]{:S(2)}, u32[]{:S(2)}) %collective-permute-start.30) | collective-permute-done | bytes 458784 | tf_op jit(solution)/shard_map/ppermute | solution.py:71
  83.7 2.8 %shard_map.125 = (f32[128,256]{1,0:T(8,128)S(1)}, f32[128,256]{1,0:T(8,128)S(1)}) custom-call(bf16[64,3584]{1,0:T(8,128)(2,1)S(1)} %constant_dynamic-update-slice_fusion.8.a_ref, bf16[64,3584]{1,0:T(8,128)(2,1)S(1)} %collective-permute-done.30.b_ref, bf16[256,3584]{1,0:T(8,128)(2,1)S(1)} %bitcast.26, bf16[256,3584]{1,0:T(8,128)(2,1)} %collective-permute-done.10.wdp_ref), custom_call_target="tpu_custom_call" | custom-call | flops 469762048 | bytes 4849664 | tf_op jit(solution)/shard_map/pallas_call | solution.py:25
  86.5 1.5 collective-permute-start.31
  89.5 7.6 %collective-permute-done.25.b_ref = bf16[64,3584]{1,0:T(8,128)(2,1)S(1)} collective-permute-done((bf16[64,3584]{1,0:T(8,128)(2,1)S(1)}, bf16[64,3584]{1,0:T(8,128)(2,1)S(1)}, u32[]{:S(2)}, u32[]{:S(2)}) %collective-permute-start.25) | collective-permute-done | bytes 458784 | tf_op jit(solution)/shard_map/ppermute | solution.py:71
  97.1 2.8 %collective-permute-done.31.got_ref = f32[128,256]{1,0:T(8,128)S(1)} collective-permute-done((f32[128,256]{1,0:T(8,128)S(1)}, f32[128,256]{1,0:T(8,128)S(1)}, u32[]{:S(2)}, u32[]{:S(2)}) %collective-permute-start.31) | collective-permute-done | bytes 131104 | tf_op jit(solution)/shard_map/ppermute | solution.py:71
  102.0 2.1 %shard_map.117 = (f32[64,3584]{1,0:T(8,128)S(1)}, bf16[64,3584]{1,0:T(8,128)(2,1)S(1)}) custom-call(bf16[128,256]{1,0:T(8,128)(2,1)S(1)} %shard_map.115.mine_ref, bf16[128,256]{1,0:T(8,128)(2,1)S(1)} %collective-permute-done.9.theirs_ref, bf16[256,3584]{1,0:T(8,128)(2,1)S(1)} %bitcast.27, bf16[256,3584]{1,0:T(8,128)(2,1)} %collective-permute-done.10.wdp_ref), custom_call_target="tpu_custom_call" | custom-call | flops 469762048 | bytes 5177344 | tf_op jit(solution)/shard_map/pallas_call | solution.py:25
  105.0 1.5 collective-permute-start.32
  106.5 19.6 %collective-permute-start = (bf16[128,3584]{1,0:T(8,128)(2,1)S(1)}, bf16[128,3584]{1,0:T(8,128)(2,1)S(1)}, u32[]{:S(2)}, u32[]{:S(2)}) collective-permute-start(bf16[128,3584]{1,0:T(8,128)(2,1)S(1)} %bitcast.32), channel_id=1, source_target_pairs={{0,32},{1,33},{2,34},{3,35},{4,36},{5,37},{6,38},{7,39},{8,40},{9,... | collective-permute-start | bytes 2752520 | tf_op jit(solution)/shard_map/ppermute | solution.py:82
  126.1 1.9 collective-permute-start.17
  128.2 1.4 collective-permute-start.40
  129.6 1.9 collective-permute-start.18
  131.6 2.5 %collective-permute-start.12 = (bf16[16,3584]{1,0:T(8,128)(2,1)S(1)}, bf16[16,3584]{1,0:T(8,128)(2,1)S(1)}, u32[]{:S(2)}, u32[]{:S(2)}) collective-permute-start(bf16[16,3584]{1,0:T(8,128)(2,1)S(1)} %get-tuple-element.66), channel_id=1, source_target_pairs={{4,0},{5,1},{14,2},{15,3},{8,4},{9,5},{2,6},{3,7},{12,8},{13,9},{6... | collective-permute-start | bytes 344072 | tf_op jit(solution)/shard_map/ppermute | solution.py:71
  134.1 7.1 %collective-permute-done.18.comb_ref = bf16[128,128]{1,0:T(8,128)(2,1)S(1)} collective-permute-done((bf16[128,128]{1,0:T(8,128)(2,1)S(1)}, bf16[128,128]{1,0:T(8,128)(2,1)S(1)}, u32[]{:S(2)}, u32[]{:S(2)}) %collective-permute-start.18) | collective-permute-done | bytes 32800 | tf_op jit(solution)/shard_map/ppermute | solution.py:82
  141.2 1.6 collective-permute-start.33
  142.8 2.6 %collective-permute-start.13 = (bf16[16,3584]{1,0:T(8,128)(2,1)S(1)}, bf16[16,3584]{1,0:T(8,128)(2,1)S(1)}, u32[]{:S(2)}, u32[]{:S(2)}) collective-permute-start(bf16[16,3584]{1,0:T(8,128)(2,1)S(1)} %get-tuple-element.67), channel_id=1, source_target_pairs={{14,0},{15,1},{4,2},{5,3},{2,4},{3,5},{8,6},{9,7},{6,8},{7,9},{12,... | collective-permute-start | bytes 344072 | tf_op jit(solution)/shard_map/ppermute | solution.py:71
  146.4 2.9 %collective-permute-done.13.b2 = bf16[16,3584]{1,0:T(8,128)(2,1)S(1)} collective-permute-done((bf16[16,3584]{1,0:T(8,128)(2,1)S(1)}, bf16[16,3584]{1,0:T(8,128)(2,1)S(1)}, u32[]{:S(2)}, u32[]{:S(2)}) %collective-permute-start.13) | collective-permute-done | bytes 114720 | tf_op jit(solution)/shard_map/ppermute | solution.py:71
  150.2 2.5 %collective-permute-done.14.b3 = bf16[16,3584]{1,0:T(8,128)(2,1)S(1)} collective-permute-done((bf16[16,3584]{1,0:T(8,128)(2,1)S(1)}, bf16[16,3584]{1,0:T(8,128)(2,1)S(1)}, u32[]{:S(2)}, u32[]{:S(2)}) %collective-permute-start.14) | collective-permute-done | bytes 114720 | tf_op jit(solution)/shard_map/ppermute | solution.py:71
  153.6 2.7 %collective-permute-start.43 = (bf16[16,1792]{1,0:T(8,128)(2,1)S(1)}, bf16[16,1792]{1,0:T(8,128)(2,1)S(1)}, u32[]{:S(2)}, u32[]{:S(2)}) collective-permute-start(bf16[16,1792]{1,0:T(8,128)(2,1)S(1)} %get-tuple-element.107), channel_id=1, source_target_pairs={{10,0},{11,1},{8,2},{9,3},{14,4},{15,5},{12,6},{13,7},{2,8},{3,9},... | collective-permute-start | bytes 172040 | tf_op jit(solution)/shard_map/ppermute | solution.py:71
  156.4 4.6 %collective-permute-start.15 = (bf16[32,3584]{1,0:T(8,128)(2,1)S(1)}, bf16[32,3584]{1,0:T(8,128)(2,1)S(1)}, u32[]{:S(2)}, u32[]{:S(2)}) collective-permute-start(bf16[32,3584]{1,0:T(8,128)(2,1)S(1)} %get-tuple-element.69), channel_id=1, source_target_pairs={{0,32},{1,33},{2,34},{3,35},{4,36},{5,37},{6,38},{7,39},{8,40},{9,... | collective-permute-start | bytes 688136 | tf_op jit(solution)/shard_map/ppermute | solution.py:82
  161.0 5.4 %collective-permute-start.16 = (bf16[32,3584]{1,0:T(8,128)(2,1)S(1)}, bf16[32,3584]{1,0:T(8,128)(2,1)S(1)}, u32[]{:S(2)}, u32[]{:S(2)}) collective-permute-start(bf16[32,3584]{1,0:T(8,128)(2,1)S(1)} %get-tuple-element.70), channel_id=1, source_target_pairs={{0,49},{1,48},{2,51},{3,50},{4,53},{5,52},{6,55},{7,54},{8,57},{9,... | collective-permute-start | bytes 688136 | tf_op jit(solution)/shard_map/ppermute | solution.py:82
  166.4 1.2 collective-permute-start.34
  167.6 3.5 %collective-permute-done.34.b1 = bf16[16,1792]{1,0:T(8,128)(2,1)S(1)} collective-permute-done((bf16[16,1792]{1,0:T(8,128)(2,1)S(1)}, bf16[16,1792]{1,0:T(8,128)(2,1)S(1)}, u32[]{:S(2)}, u32[]{:S(2)}) %collective-permute-start.34) | collective-permute-done | bytes 57376 | tf_op jit(solution)/shard_map/ppermute | solution.py:71
  171.3 4.0 %collective-permute-done.35.b2 = bf16[16,1792]{1,0:T(8,128)(2,1)S(1)} collective-permute-done((bf16[16,1792]{1,0:T(8,128)(2,1)S(1)}, bf16[16,1792]{1,0:T(8,128)(2,1)S(1)}, u32[]{:S(2)}, u32[]{:S(2)}) %collective-permute-start.35) | collective-permute-done | bytes 57376 | tf_op jit(solution)/shard_map/ppermute | solution.py:71
  176.1 5.9 %collective-permute-done.36.b3 = bf16[16,1792]{1,0:T(8,128)(2,1)S(1)} collective-permute-done((bf16[16,1792]{1,0:T(8,128)(2,1)S(1)}, bf16[16,1792]{1,0:T(8,128)(2,1)S(1)}, u32[]{:S(2)}, u32[]{:S(2)}) %collective-permute-start.36) | collective-permute-done | bytes 57376 | tf_op jit(solution)/shard_map/ppermute | solution.py:71
  182.0 5.1 %collective-permute-start.1 = (bf16[128,128]{1,0:T(8,128)(2,1)S(1)}, bf16[128,128]{1,0:T(8,128)(2,1)S(1)}, u32[]{:S(2)}, u32[]{:S(2)}) collective-permute-start(bf16[128,128]{1,0:T(8,128)(2,1)S(1)} %get-tuple-element.56), channel_id=1, source_target_pairs={{0,32},{1,33},{2,34},{3,35},{4,36},{5,37},{6,38},{7,39},{8,40},{9,... | collective-permute-start | bytes 98312 | tf_op jit(solution)/shard_map/ppermute | solution.py:82
  188.1 1.9 collective-permute-start.44
  190.1 1.9 collective-permute-start.45
  192.0 1.9 collective-permute-start.37
  193.9 1.9 collective-permute-start.38
  195.9 1.3 shard_map.120
  197.2 1.8 collective-permute-done.45.rest_3_
  199.5 3.4 %collective-permute-done.38.rest_1_ = bf16[32,1792]{1,0:T(8,128)(2,1)S(1)} collective-permute-done((bf16[32,1792]{1,0:T(8,128)(2,1)S(1)}, bf16[32,1792]{1,0:T(8,128)(2,1)S(1)}, u32[]{:S(2)}, u32[]{:S(2)}) %collective-permute-start.38) | collective-permute-done | bytes 114720 | tf_op jit(solution)/shard_map/ppermute | solution.py:82
  202.9 1.3 shard_map.135
  (103 shorter events, 20.1 us)
Async XLA Ops:
  5.8 8.5 %collective-permute-start.19 = (bf16[32,3584]{1,0:T(8,128)(2,1)S(1)}, bf16[32,3584]{1,0:T(8,128)(2,1)S(1)}, u32[]{:S(2)}, u32[]{:S(2)}) collective-permute-start(bf16[32,3584]{1,0:T(8,128)(2,1)S(1)} %get-tuple-element.73), channel_id=1, source_target_pairs={{0,17},{1,16},{2,19},{3,18},{4,21},{5,20},{6,23},{7,22},{8,25},{9,... | collective-permute-start | bytes 688136 | tf_op jit(solution)/shard_map/ppermute | solution.py:71
  9.2 12.1 %collective-permute-start.26 = (bf16[32,3584]{1,0:T(8,128)(2,1)S(1)}, bf16[32,3584]{1,0:T(8,128)(2,1)S(1)}, u32[]{:S(2)}, u32[]{:S(2)}) collective-permute-start(bf16[32,3584]{1,0:T(8,128)(2,1)S(1)} %get-tuple-element.81), channel_id=1, source_target_pairs={{0,17},{1,16},{2,19},{3,18},{4,21},{5,20},{6,23},{7,22},{8,25},{9,... | collective-permute-start | bytes 688136 | tf_op jit(solution)/shard_map/ppermute | solution.py:71
  9.3 74.4 %collective-permute-start.10 = (bf16[256,3584]{1,0:T(8,128)(2,1)S(1)}, bf16[256,3584]{1,0:T(8,128)(2,1)}, u32[]{:S(2)}, u32[]{:S(2)}) collective-permute-start(bf16[256,3584]{1,0:T(8,128)(2,1)S(1)} %bitcast.25), channel_id=1, source_target_pairs={{0,1},{1,0},{2,3},{3,2},{4,5},{5,4},{6,7},{7,6},{8,9},{9,8},{10,11... | collective-permute-start | bytes 5505032 | tf_op jit(solution)/shard_map/ppermute | solution.py:71
  11.7 14.1 %collective-permute-start.2 = (bf16[32,3584]{1,0:T(8,128)(2,1)S(1)}, bf16[32,3584]{1,0:T(8,128)(2,1)S(1)}, u32[]{:S(2)}, u32[]{:S(2)}) collective-permute-start(bf16[32,3584]{1,0:T(8,128)(2,1)S(1)} %get-tuple-element.58), channel_id=1, source_target_pairs={{0,17},{1,16},{2,19},{3,18},{4,21},{5,20},{6,23},{7,22},{8,25},{9,... | collective-permute-start | bytes 688136 | tf_op jit(solution)/shard_map/ppermute | solution.py:71
  14.3 13.0 %collective-permute-start.20 = (bf16[16,3584]{1,0:T(8,128)(2,1)S(1)}, bf16[16,3584]{1,0:T(8,128)(2,1)S(1)}, u32[]{:S(2)}, u32[]{:S(2)}) collective-permute-start(bf16[16,3584]{1,0:T(8,128)(2,1)S(1)} %get-tuple-element.75), channel_id=1, source_target_pairs={{0,4},{1,5},{2,14},{3,15},{4,8},{5,9},{6,2},{7,3},{8,12},{9,13},{1... | collective-permute-start | bytes 344072 | tf_op jit(solution)/shard_map/ppermute | solution.py:71
  17.5 13.6 %collective-permute-start.21 = (bf16[16,3584]{1,0:T(8,128)(2,1)S(1)}, bf16[16,3584]{1,0:T(8,128)(2,1)S(1)}, u32[]{:S(2)}, u32[]{:S(2)}) collective-permute-start(bf16[16,3584]{1,0:T(8,128)(2,1)S(1)} %get-tuple-element.76), channel_id=1, source_target_pairs={{0,14},{1,15},{2,4},{3,5},{4,2},{5,3},{6,8},{7,9},{8,6},{9,7},{10,... | collective-permute-start | bytes 344072 | tf_op jit(solution)/shard_map/ppermute | solution.py:71
  21.3 10.4 %collective-permute-start.22 = (bf16[16,3584]{1,0:T(8,128)(2,1)S(1)}, bf16[16,3584]{1,0:T(8,128)(2,1)S(1)}, u32[]{:S(2)}, u32[]{:S(2)}) collective-permute-start(bf16[16,3584]{1,0:T(8,128)(2,1)S(1)} %get-tuple-element.77), channel_id=1, source_target_pairs={{0,10},{1,11},{2,8},{3,9},{4,14},{5,15},{6,12},{7,13},{8,2},{9,3},... | collective-permute-start | bytes 344072 | tf_op jit(solution)/shard_map/ppermute | solution.py:71
  25.9 28.5 %collective-permute-start.27 = (bf16[16,3584]{1,0:T(8,128)(2,1)S(1)}, bf16[16,3584]{1,0:T(8,128)(2,1)S(1)}, u32[]{:S(2)}, u32[]{:S(2)}) collective-permute-start(bf16[16,3584]{1,0:T(8,128)(2,1)S(1)} %get-tuple-element.83), channel_id=1, source_target_pairs={{0,4},{1,5},{2,14},{3,15},{4,8},{5,9},{6,2},{7,3},{8,12},{9,13},{1... | collective-permute-start | bytes 344072 | tf_op jit(solution)/shard_map/ppermute | solution.py:71
  27.3 28.6 %collective-permute-start.28 = (bf16[16,3584]{1,0:T(8,128)(2,1)S(1)}, bf16[16,3584]{1,0:T(8,128)(2,1)S(1)}, u32[]{:S(2)}, u32[]{:S(2)}) collective-permute-start(bf16[16,3584]{1,0:T(8,128)(2,1)S(1)} %get-tuple-element.84), channel_id=1, source_target_pairs={{0,14},{1,15},{2,4},{3,5},{4,2},{5,3},{6,8},{7,9},{8,6},{9,7},{10,... | collective-permute-start | bytes 344072 | tf_op jit(solution)/shard_map/ppermute | solution.py:71
  31.2 24.8 %collective-permute-start.29 = (bf16[16,3584]{1,0:T(8,128)(2,1)S(1)}, bf16[16,3584]{1,0:T(8,128)(2,1)S(1)}, u32[]{:S(2)}, u32[]{:S(2)}) collective-permute-start(bf16[16,3584]{1,0:T(8,128)(2,1)S(1)} %get-tuple-element.85), channel_id=1, source_target_pairs={{0,10},{1,11},{2,8},{3,9},{4,14},{5,15},{6,12},{7,13},{8,2},{9,3},... | collective-permute-start | bytes 344072 | tf_op jit(solution)/shard_map/ppermute | solution.py:71
  31.7 5.9 %collective-permute-start.3 = (bf16[16,3584]{1,0:T(8,128)(2,1)S(1)}, bf16[16,3584]{1,0:T(8,128)(2,1)S(1)}, u32[]{:S(2)}, u32[]{:S(2)}) collective-permute-start(bf16[16,3584]{1,0:T(8,128)(2,1)S(1)} %get-tuple-element.60), channel_id=1, source_target_pairs={{0,4},{1,5},{2,14},{3,15},{4,8},{5,9},{6,2},{7,3},{8,12},{9,13},{1... | collective-permute-start | bytes 344072 | tf_op jit(solution)/shard_map/ppermute | solution.py:71
  37.7 8.8 %collective-permute-start.4 = (bf16[16,3584]{1,0:T(8,128)(2,1)S(1)}, bf16[16,3584]{1,0:T(8,128)(2,1)S(1)}, u32[]{:S(2)}, u32[]{:S(2)}) collective-permute-start(bf16[16,3584]{1,0:T(8,128)(2,1)S(1)} %get-tuple-element.61), channel_id=1, source_target_pairs={{0,14},{1,15},{2,4},{3,5},{4,2},{5,3},{6,8},{7,9},{8,6},{9,7},{10,... | collective-permute-start | bytes 344072 | tf_op jit(solution)/shard_map/ppermute | solution.py:71
  46.5 7.8 %collective-permute-start.5 = (bf16[16,3584]{1,0:T(8,128)(2,1)S(1)}, bf16[16,3584]{1,0:T(8,128)(2,1)S(1)}, u32[]{:S(2)}, u32[]{:S(2)}) collective-permute-start(bf16[16,3584]{1,0:T(8,128)(2,1)S(1)} %get-tuple-element.62), channel_id=1, source_target_pairs={{0,10},{1,11},{2,8},{3,9},{4,14},{5,15},{6,12},{7,13},{8,2},{9,3},... | collective-permute-start | bytes 344072 | tf_op jit(solution)/shard_map/ppermute | solution.py:71
  54.3 19.6 %collective-permute-start.24 = (bf16[64,3584]{1,0:T(8,128)(2,1)S(1)}, bf16[64,3584]{1,0:T(8,128)(2,1)S(1)}, u32[]{:S(2)}, u32[]{:S(2)}) collective-permute-start(bf16[64,3584]{1,0:T(8,128)(2,1)S(1)} %constant_dynamic-update-slice_fusion.4.a_ref), channel_id=1, source_target_pairs={{0,2},{1,3},{2,0},{3,1},{4,6},{5,7},{6,4},{7,5},{8,10},{9,11},{10,... | collective-permute-start | bytes 1376264 | tf_op jit(solution)/shard_map/ppermute | solution.py:71
  54.3 19.5 %collective-permute-start.6 = (bf16[64,3584]{1,0:T(8,128)(2,1)S(1)}, bf16[64,3584]{1,0:T(8,128)(2,1)S(1)}, u32[]{:S(2)}, u32[]{:S(2)}) collective-permute-start(bf16[64,3584]{1,0:T(8,128)(2,1)S(1)} %constant_dynamic-update-slice_fusion.a_ref), channel_id=1, source_target_pairs={{0,2},{1,3},{2,0},{3,1},{4,6},{5,7},{6,4},{7,5},{8,10},{9,11},{10,... | collective-permute-start | bytes 1376264 | tf_op jit(solution)/shard_map/ppermute | solution.py:71
  55.9 32.1 %copy-start = (bf16[1,3584,256]{2,1,0:T(8,128)(2,1)S(1)}, bf16[1,3584,256]{2,1,0:T(8,128)(2,1)}, u32[]{:S(2)}) copy-start(bf16[1,3584,256]{2,1,0:T(8,128)(2,1)} %param.17) | copy-start | bytes 5505028
  56.0 32.1 %copy-start.1 = (bf16[1,3584,256]{2,1,0:T(8,128)(2,1)S(1)}, bf16[1,3584,256]{2,1,0:T(8,128)(2,1)}, u32[]{:S(2)}) copy-start(bf16[1,3584,256]{2,1,0:T(8,128)(2,1)} %param.18) | copy-start | bytes 5505028
  56.0 27.7 %collective-permute-start.30 = (bf16[64,3584]{1,0:T(8,128)(2,1)S(1)}, bf16[64,3584]{1,0:T(8,128)(2,1)S(1)}, u32[]{:S(2)}, u32[]{:S(2)}) collective-permute-start(bf16[64,3584]{1,0:T(8,128)(2,1)S(1)} %constant_dynamic-update-slice_fusion.8.a_ref), channel_id=1, source_target_pairs={{0,2},{1,3},{2,0},{3,1},{4,6},{5,7},{6,4},{7,5},{8,10},{9,11},{10,... | collective-permute-start | bytes 1376264 | tf_op jit(solution)/shard_map/ppermute | solution.py:71
  56.1 32.6 %collective-permute-start.7 = (bf16[64,3584]{1,0:T(8,128)(2,1)S(1)}, bf16[64,3584]{1,0:T(8,128)(2,1)S(1)}, u32[]{:S(2)}, u32[]{:S(2)}) collective-permute-start(bf16[64,3584]{1,0:T(8,128)(2,1)S(1)} %constant_dynamic-update-slice_fusion.a_ref), channel_id=1, source_target_pairs={{0,1},{1,0},{2,3},{3,2},{4,5},{5,4},{6,7},{7,6},{8,9},{9,8},{10,11... | collective-permute-start | bytes 1376264 | tf_op jit(solution)/shard_map/ppermute | solution.py:71
  73.9 14.9 %collective-permute-start.8 = (bf16[64,3584]{1,0:T(8,128)(2,1)S(1)}, bf16[64,3584]{1,0:T(8,128)(2,1)S(1)}, u32[]{:S(2)}, u32[]{:S(2)}) collective-permute-start(bf16[64,3584]{1,0:T(8,128)(2,1)S(1)} %collective-permute-done.6.b_ref), channel_id=1, source_target_pairs={{0,1},{1,0},{2,3},{3,2},{4,5},{5,4},{6,7},{7,6},{8,9},{9,8},{10,11... | collective-permute-start | bytes 1376264 | tf_op jit(solution)/shard_map/ppermute | solution.py:71
  73.9 15.6 %collective-permute-start.23 = (bf16[64,3584]{1,0:T(8,128)(2,1)S(1)}, bf16[64,3584]{1,0:T(8,128)(2,1)S(1)}, u32[]{:S(2)}, u32[]{:S(2)}) collective-permute-start(bf16[64,3584]{1,0:T(8,128)(2,1)S(1)} %constant_dynamic-update-slice_fusion.4.a_ref), channel_id=1, source_target_pairs={{0,1},{1,0},{2,3},{3,2},{4,5},{5,4},{6,7},{7,6},{8,9},{9,8},{10,11... | collective-permute-start | bytes 1376264 | tf_op jit(solution)/shard_map/ppermute | solution.py:71
  83.7 13.4 %collective-permute-start.25 = (bf16[64,3584]{1,0:T(8,128)(2,1)S(1)}, bf16[64,3584]{1,0:T(8,128)(2,1)S(1)}, u32[]{:S(2)}, u32[]{:S(2)}) collective-permute-start(bf16[64,3584]{1,0:T(8,128)(2,1)S(1)} %collective-permute-done.24.b_ref), channel_id=1, source_target_pairs={{0,1},{1,0},{2,3},{3,2},{4,5},{5,4},{6,7},{7,6},{8,9},{9,8},{10,11... | collective-permute-start | bytes 1376264 | tf_op jit(solution)/shard_map/ppermute | solution.py:71
  86.5 13.4 %collective-permute-start.31 = (f32[128,256]{1,0:T(8,128)S(1)}, f32[128,256]{1,0:T(8,128)S(1)}, u32[]{:S(2)}, u32[]{:S(2)}) collective-permute-start(f32[128,256]{1,0:T(8,128)S(1)} %get-tuple-element.87), channel_id=1, source_target_pairs={{0,1},{1,0},{2,3},{3,2},{4,5},{5,4},{6,7},{7,6},{8,9},{9,8},{10,11... | collective-permute-start | bytes 393224 | tf_op jit(solution)/shard_map/ppermute | solution.py:71
  89.4 12.6 %collective-permute-start.9 = (bf16[128,256]{1,0:T(8,128)(2,1)S(1)}, bf16[128,256]{1,0:T(8,128)(2,1)S(1)}, u32[]{:S(2)}, u32[]{:S(2)}) collective-permute-start(bf16[128,256]{1,0:T(8,128)(2,1)S(1)} %shard_map.116), channel_id=1, source_target_pairs={{0,1},{1,0},{2,3},{3,2},{4,5},{5,4},{6,7},{7,6},{8,9},{9,8},{10,11... | collective-permute-start | bytes 196616 | tf_op jit(solution)/shard_map/ppermute | solution.py:71
  101.3 26.8 %collective-permute-start.39 = (bf16[128,1792]{1,0:T(8,128)(2,1)S(1)}, bf16[128,1792]{1,0:T(8,128)(2,1)S(1)}, u32[]{:S(2)}, u32[]{:S(2)}) collective-permute-start(bf16[128,1792]{1,0:T(8,128)(2,1)S(1)} %get-tuple-element.101), channel_id=1, source_target_pairs={{0,1},{1,0},{2,3},{3,2},{4,5},{5,4},{6,7},{7,6},{8,9},{9,8},{10,11... | collective-permute-start | bytes 1376264 | tf_op jit(solution)/shard_map/ppermute | solution.py:71
  104.2 25.3 %collective-permute-start.11 = (bf16[64,3584]{1,0:T(8,128)(2,1)S(1)}, bf16[64,3584]{1,0:T(8,128)(2,1)S(1)}, u32[]{:S(2)}, u32[]{:S(2)}) collective-permute-start(bf16[64,3584]{1,0:T(8,128)(2,1)S(1)} %get-tuple-element.64), channel_id=1, source_target_pairs={{0,2},{1,3},{2,0},{3,1},{4,6},{5,7},{6,4},{7,5},{8,10},{9,11},{10,... | collective-permute-start | bytes 1376264 | tf_op jit(solution)/shard_map/ppermute | solution.py:71
  105.0 26.6 %collective-permute-start.32 = (bf16[128,1792]{1,0:T(8,128)(2,1)S(1)}, bf16[128,1792]{1,0:T(8,128)(2,1)S(1)}, u32[]{:S(2)}, u32[]{:S(2)}) collective-permute-start(bf16[128,1792]{1,0:T(8,128)(2,1)S(1)} %get-tuple-element.91), channel_id=1, source_target_pairs={{0,1},{1,0},{2,3},{3,2},{4,5},{5,4},{6,7},{7,6},{8,9},{9,8},{10,11... | collective-permute-start | bytes 1376264 | tf_op jit(solution)/shard_map/ppermute | solution.py:71
  106.5 83.5 %collective-permute-start = (bf16[128,3584]{1,0:T(8,128)(2,1)S(1)}, bf16[128,3584]{1,0:T(8,128)(2,1)S(1)}, u32[]{:S(2)}, u32[]{:S(2)}) collective-permute-start(bf16[128,3584]{1,0:T(8,128)(2,1)S(1)} %bitcast.32), channel_id=1, source_target_pairs={{0,32},{1,33},{2,34},{3,35},{4,36},{5,37},{6,38},{7,39},{8,40},{9,... | collective-permute-start | bytes 2752520 | tf_op jit(solution)/shard_map/ppermute | solution.py:82
  126.1 71.0 %collective-permute-start.17 = (bf16[128,3584]{1,0:T(8,128)(2,1)S(1)}, bf16[128,3584]{1,0:T(8,128)(2,1)S(1)}, u32[]{:S(2)}, u32[]{:S(2)}) collective-permute-start(bf16[128,3584]{1,0:T(8,128)(2,1)S(1)} %bitcast.30), channel_id=1, source_target_pairs={{32,0},{33,1},{34,2},{35,3},{36,4},{37,5},{38,6},{39,7},{40,8},{41... | collective-permute-start | bytes 2752520 | tf_op jit(solution)/shard_map/ppermute | solution.py:82
  128.2 17.3 %collective-permute-start.40 = (bf16[64,1792]{1,0:T(8,128)(2,1)S(1)}, bf16[64,1792]{1,0:T(8,128)(2,1)S(1)}, u32[]{:S(2)}, u32[]{:S(2)}) collective-permute-start(bf16[64,1792]{1,0:T(8,128)(2,1)S(1)} %get-tuple-element.103), channel_id=1, source_target_pairs={{0,2},{1,3},{2,0},{3,1},{4,6},{5,7},{6,4},{7,5},{8,10},{9,11},{10,... | collective-permute-start | bytes 688136 | tf_op jit(solution)/shard_map/ppermute | solution.py:71
  129.6 11.7 %collective-permute-start.18 = (bf16[128,128]{1,0:T(8,128)(2,1)S(1)}, bf16[128,128]{1,0:T(8,128)(2,1)S(1)}, u32[]{:S(2)}, u32[]{:S(2)}) collective-permute-start(bf16[128,128]{1,0:T(8,128)(2,1)S(1)} %get-tuple-element.71), channel_id=1, source_target_pairs={{32,0},{33,1},{34,2},{35,3},{36,4},{37,5},{38,6},{39,7},{40,8},{41... | collective-permute-start | bytes 98312 | tf_op jit(solution)/shard_map/ppermute | solution.py:82
  131.6 11.2 %collective-permute-start.12 = (bf16[16,3584]{1,0:T(8,128)(2,1)S(1)}, bf16[16,3584]{1,0:T(8,128)(2,1)S(1)}, u32[]{:S(2)}, u32[]{:S(2)}) collective-permute-start(bf16[16,3584]{1,0:T(8,128)(2,1)S(1)} %get-tuple-element.66), channel_id=1, source_target_pairs={{4,0},{5,1},{14,2},{15,3},{8,4},{9,5},{2,6},{3,7},{12,8},{13,9},{6... | collective-permute-start | bytes 344072 | tf_op jit(solution)/shard_map/ppermute | solution.py:71
  141.2 12.4 %collective-permute-start.33 = (bf16[64,1792]{1,0:T(8,128)(2,1)S(1)}, bf16[64,1792]{1,0:T(8,128)(2,1)S(1)}, u32[]{:S(2)}, u32[]{:S(2)}) collective-permute-start(bf16[64,1792]{1,0:T(8,128)(2,1)S(1)} %get-tuple-element.93), channel_id=1, source_target_pairs={{0,2},{1,3},{2,0},{3,1},{4,6},{5,7},{6,4},{7,5},{8,10},{9,11},{10,... | collective-permute-start | bytes 688136 | tf_op jit(solution)/shard_map/ppermute | solution.py:71
  142.8 6.5 %collective-permute-start.13 = (bf16[16,3584]{1,0:T(8,128)(2,1)S(1)}, bf16[16,3584]{1,0:T(8,128)(2,1)S(1)}, u32[]{:S(2)}, u32[]{:S(2)}) collective-permute-start(bf16[16,3584]{1,0:T(8,128)(2,1)S(1)} %get-tuple-element.67), channel_id=1, source_target_pairs={{14,0},{15,1},{4,2},{5,3},{2,4},{3,5},{8,6},{9,7},{6,8},{7,9},{12,... | collective-permute-start | bytes 344072 | tf_op jit(solution)/shard_map/ppermute | solution.py:71
  145.4 7.3 %collective-permute-start.14 = (bf16[16,3584]{1,0:T(8,128)(2,1)S(1)}, bf16[16,3584]{1,0:T(8,128)(2,1)S(1)}, u32[]{:S(2)}, u32[]{:S(2)}) collective-permute-start(bf16[16,3584]{1,0:T(8,128)(2,1)S(1)} %get-tuple-element.68), channel_id=1, source_target_pairs={{10,0},{11,1},{8,2},{9,3},{14,4},{15,5},{12,6},{13,7},{2,8},{3,9},... | collective-permute-start | bytes 344072 | tf_op jit(solution)/shard_map/ppermute | solution.py:71
  149.3 7.1 %collective-permute-start.41 = (bf16[16,1792]{1,0:T(8,128)(2,1)S(1)}, bf16[16,1792]{1,0:T(8,128)(2,1)S(1)}, u32[]{:S(2)}, u32[]{:S(2)}) collective-permute-start(bf16[16,1792]{1,0:T(8,128)(2,1)S(1)} %get-tuple-element.105), channel_id=1, source_target_pairs={{4,0},{5,1},{14,2},{15,3},{8,4},{9,5},{2,6},{3,7},{12,8},{13,9},{6... | collective-permute-start | bytes 172040 | tf_op jit(solution)/shard_map/ppermute | solution.py:71
  152.7 8.2 %collective-permute-start.42 = (bf16[16,1792]{1,0:T(8,128)(2,1)S(1)}, bf16[16,1792]{1,0:T(8,128)(2,1)S(1)}, u32[]{:S(2)}, u32[]{:S(2)}) collective-permute-start(bf16[16,1792]{1,0:T(8,128)(2,1)S(1)} %get-tuple-element.106), channel_id=1, source_target_pairs={{14,0},{15,1},{4,2},{5,3},{2,4},{3,5},{8,6},{9,7},{6,8},{7,9},{12,... | collective-permute-start | bytes 172040 | tf_op jit(solution)/shard_map/ppermute | solution.py:71
  153.6 12.8 %collective-permute-start.43 = (bf16[16,1792]{1,0:T(8,128)(2,1)S(1)}, bf16[16,1792]{1,0:T(8,128)(2,1)S(1)}, u32[]{:S(2)}, u32[]{:S(2)}) collective-permute-start(bf16[16,1792]{1,0:T(8,128)(2,1)S(1)} %get-tuple-element.107), channel_id=1, source_target_pairs={{10,0},{11,1},{8,2},{9,3},{14,4},{15,5},{12,6},{13,7},{2,8},{3,9},... | collective-permute-start | bytes 172040 | tf_op jit(solution)/shard_map/ppermute | solution.py:71
  156.4 35.6 %collective-permute-start.15 = (bf16[32,3584]{1,0:T(8,128)(2,1)S(1)}, bf16[32,3584]{1,0:T(8,128)(2,1)S(1)}, u32[]{:S(2)}, u32[]{:S(2)}) collective-permute-start(bf16[32,3584]{1,0:T(8,128)(2,1)S(1)} %get-tuple-element.69), channel_id=1, source_target_pairs={{0,32},{1,33},{2,34},{3,35},{4,36},{5,37},{6,38},{7,39},{8,40},{9,... | collective-permute-start | bytes 688136 | tf_op jit(solution)/shard_map/ppermute | solution.py:82
  161.0 33.0 %collective-permute-start.16 = (bf16[32,3584]{1,0:T(8,128)(2,1)S(1)}, bf16[32,3584]{1,0:T(8,128)(2,1)S(1)}, u32[]{:S(2)}, u32[]{:S(2)}) collective-permute-start(bf16[32,3584]{1,0:T(8,128)(2,1)S(1)} %get-tuple-element.70), channel_id=1, source_target_pairs={{0,49},{1,48},{2,51},{3,50},{4,53},{5,52},{6,55},{7,54},{8,57},{9,... | collective-permute-start | bytes 688136 | tf_op jit(solution)/shard_map/ppermute | solution.py:82
  166.4 4.7 %collective-permute-start.34 = (bf16[16,1792]{1,0:T(8,128)(2,1)S(1)}, bf16[16,1792]{1,0:T(8,128)(2,1)S(1)}, u32[]{:S(2)}, u32[]{:S(2)}) collective-permute-start(bf16[16,1792]{1,0:T(8,128)(2,1)S(1)} %get-tuple-element.95), channel_id=1, source_target_pairs={{4,0},{5,1},{14,2},{15,3},{8,4},{9,5},{2,6},{3,7},{12,8},{13,9},{6... | collective-permute-start | bytes 172040 | tf_op jit(solution)/shard_map/ppermute | solution.py:71
  171.1 4.2 %collective-permute-start.35 = (bf16[16,1792]{1,0:T(8,128)(2,1)S(1)}, bf16[16,1792]{1,0:T(8,128)(2,1)S(1)}, u32[]{:S(2)}, u32[]{:S(2)}) collective-permute-start(bf16[16,1792]{1,0:T(8,128)(2,1)S(1)} %get-tuple-element.96), channel_id=1, source_target_pairs={{14,0},{15,1},{4,2},{5,3},{2,4},{3,5},{8,6},{9,7},{6,8},{7,9},{12,... | collective-permute-start | bytes 172040 | tf_op jit(solution)/shard_map/ppermute | solution.py:71
  175.4 6.7 %collective-permute-start.36 = (bf16[16,1792]{1,0:T(8,128)(2,1)S(1)}, bf16[16,1792]{1,0:T(8,128)(2,1)S(1)}, u32[]{:S(2)}, u32[]{:S(2)}) collective-permute-start(bf16[16,1792]{1,0:T(8,128)(2,1)S(1)} %get-tuple-element.97), channel_id=1, source_target_pairs={{10,0},{11,1},{8,2},{9,3},{14,4},{15,5},{12,6},{13,7},{2,8},{3,9},... | collective-permute-start | bytes 172040 | tf_op jit(solution)/shard_map/ppermute | solution.py:71
  182.0 6.1 %collective-permute-start.1 = (bf16[128,128]{1,0:T(8,128)(2,1)S(1)}, bf16[128,128]{1,0:T(8,128)(2,1)S(1)}, u32[]{:S(2)}, u32[]{:S(2)}) collective-permute-start(bf16[128,128]{1,0:T(8,128)(2,1)S(1)} %get-tuple-element.56), channel_id=1, source_target_pairs={{0,32},{1,33},{2,34},{3,35},{4,36},{5,37},{6,38},{7,39},{8,40},{9,... | collective-permute-start | bytes 98312 | tf_op jit(solution)/shard_map/ppermute | solution.py:82
  188.1 9.1 %collective-permute-start.44 = (bf16[32,1792]{1,0:T(8,128)(2,1)S(1)}, bf16[32,1792]{1,0:T(8,128)(2,1)S(1)}, u32[]{:S(2)}, u32[]{:S(2)}) collective-permute-start(bf16[32,1792]{1,0:T(8,128)(2,1)S(1)} %get-tuple-element.108), channel_id=1, source_target_pairs={{32,0},{33,1},{34,2},{35,3},{36,4},{37,5},{38,6},{39,7},{40,8},{41... | collective-permute-start | bytes 344072 | tf_op jit(solution)/shard_map/ppermute | solution.py:82
  190.1 9.0 %collective-permute-start.45 = (bf16[32,1792]{1,0:T(8,128)(2,1)S(1)}, bf16[32,1792]{1,0:T(8,128)(2,1)S(1)}, u32[]{:S(2)}, u32[]{:S(2)}) collective-permute-start(bf16[32,1792]{1,0:T(8,128)(2,1)S(1)} %get-tuple-element.109), channel_id=1, source_target_pairs={{32,17},{33,16},{34,19},{35,18},{36,21},{37,20},{38,23},{39,22},{4... | collective-permute-start | bytes 344072 | tf_op jit(solution)/shard_map/ppermute | solution.py:82
  192.0 7.5 %collective-permute-start.37 = (bf16[32,1792]{1,0:T(8,128)(2,1)S(1)}, bf16[32,1792]{1,0:T(8,128)(2,1)S(1)}, u32[]{:S(2)}, u32[]{:S(2)}) collective-permute-start(bf16[32,1792]{1,0:T(8,128)(2,1)S(1)} %get-tuple-element.98), channel_id=1, source_target_pairs={{32,0},{33,1},{34,2},{35,3},{36,4},{37,5},{38,6},{39,7},{40,8},{41... | collective-permute-start | bytes 344072 | tf_op jit(solution)/shard_map/ppermute | solution.py:82
  193.9 9.0 %collective-permute-start.38 = (bf16[32,1792]{1,0:T(8,128)(2,1)S(1)}, bf16[32,1792]{1,0:T(8,128)(2,1)S(1)}, u32[]{:S(2)}, u32[]{:S(2)}) collective-permute-start(bf16[32,1792]{1,0:T(8,128)(2,1)S(1)} %get-tuple-element.99), channel_id=1, source_target_pairs={{32,17},{33,16},{34,19},{35,18},{36,21},{37,20},{38,23},{39,22},{4... | collective-permute-start | bytes 344072 | tf_op jit(solution)/shard_map/ppermute | solution.py:82
  (8 other events, 46.0 us)

commit v2 on v1

v2 whole, which is shorter than its diff:
```python
import jax
import jax.numpy as jnp
from jax import lax
from jax.experimental import pallas as pl
from jax.experimental.pallas import tpu as pltpu
from jax.sharding import PartitionSpec as P

CAP = 8
PAIRS = 4
BLOCK = 2 * CAP
HALF = PAIRS * CAP
HOME = PAIRS * BLOCK
BF16 = jnp.bfloat16
F32 = jnp.float32


def call(body, outs, args, flops=0, smem=(), after=(), limit=48):
    total = sum(a.size * a.dtype.itemsize for a in args)
    total += sum(o.size * o.dtype.itemsize for o in outs)
    specs = [
        pl.BlockSpec(memory_space=pltpu.SMEM if i in smem else pltpu.VMEM)
        for i in range(len(args))
    ]
    specs += [pl.BlockSpec(memory_space=pl.ANY)] * len(after)
    used, extra = len(args), len(after)

    def run(*refs):
        body(*refs[:used], *refs[used + extra :])

    return pl.pallas_call(
        run,
        out_shape=tuple(outs),
        in_specs=specs,
        out_specs=tuple(pl.BlockSpec(memory_space=pltpu.VMEM) for _ in outs),
        compiler_params=pltpu.CompilerParams(vmem_limit_bytes=limit * 1024 * 1024),
        cost_estimate=pl.CostEstimate(flops=flops, bytes_accessed=total, transcendentals=0),
    )(*args, *after)


def shape(rows, cols, dtype=BF16):
    return jax.ShapeDtypeStruct((rows, cols), dtype)


def dot(a, b):
    return lax.dot_general(a, b, (((1,), (0,)), ((), ())), preferred_element_type=F32)


def dot_t(a, b):
    return lax.dot_general(a, b, (((1,), (1,)), ((), ())), preferred_element_type=F32)


def section_perm(move):
    pairs = []
    for xh in range(2):
        for z in range(8):
            for d in range(2):
                nxh, nz, nd = move(xh, z, d)
                pairs.append(((xh * 8 + z) * 2 + d, (nxh * 8 + nz % 8) * 2 + nd))
    return pairs


def inverse(pairs):
    return [(b, a) for a, b in pairs]


ACROSS_XHI = section_perm(lambda xh, z, d: (1 - xh, z, 1 - d))
SHIFT_A = section_perm(lambda xh, z, d: (xh, z + (2 if z % 2 == 0 else -2), d))
SHIFT_B = section_perm(lambda xh, z, d: (xh, z + (-1 if z % 2 == 0 else 1), d))
SHIFT_C = section_perm(lambda xh, z, d: (xh, z + (-3 if z % 2 == 0 else 3), d))
Z_PAIR = section_perm(lambda xh, z, d: (xh, z ^ 1, d))
DP_PAIR = section_perm(lambda xh, z, d: (xh, z, 1 - d))
STAY = section_perm(lambda xh, z, d: (xh, z, d))


def move(value, pairs):
    return lax.ppermute(value, ("expert", "dp"), pairs)


def relay(value, pairs, step):
    sections = lax.axis_size("pipe")
    size = len(pairs)
    full = []
    for s in range(sections):
        t = s + step
        if 0 <= t < sections:
            full += [(s * size + a, t * size + b) for a, b in pairs]
    return lax.ppermute(value, ("pipe", "expert", "dp"), full)


def slot_tables(where_ref, ids_ref, score_ref):
    choices, tokens = ids_ref.shape
    where = where_ref[0]
    xh = where // 8
    z = where % 8
    pair = z // 2
    sign = 1 - 2 * (z % 2)
    shape2 = (2 * HOME, tokens)
    index = lax.broadcasted_iota(jnp.int32, shape2, 0)
    slot = index & (HOME - 1)
    half = slot >> 5
    q = (slot >> 3) & 3
    rank_of = slot & 7
    gray = q ^ (q >> 1)
    expert = (xh ^ half) * PAIRS + ((pair + sign * gray) & 3)
    ids = ids_ref[...]
    score = score_ref[...]
    mix = 2.5 * score / jnp.sum(score, axis=0, keepdims=True)
    hit = jnp.zeros(shape2, F32)
    weight = jnp.zeros(shape2, F32)
    for k in range(choices):
        same = ids[k : k + 1] == expert
        hit = jnp.where(same, 1.0, hit)
        weight = jnp.where(same, mix[k : k + 1], weight)
    row = lax.broadcasted_iota(jnp.int32, (tokens, tokens), 0)
    col = lax.broadcasted_iota(jnp.int32, (tokens, tokens), 1)
    before = jnp.where(row < col, 1.0, 0.0).astype(BF16)
    rank = dot(hit.astype(BF16), before)
    taken = jnp.where((hit > 0.0) & (rank == rank_of.astype(F32)), 1.0, 0.0)
    weight = weight * taken
    high = weight.astype(BF16).astype(F32)
    comb = jnp.where(index < HOME, high, weight - high)
    return taken[:HOME].astype(BF16), jnp.transpose(comb).astype(BF16)


def pack_body(where_ref, ids_ref, score_ref, *refs):
    tok_refs, (own_ref, far_ref, comb_ref) = refs[:-3], refs[-3:]
    dispatch, comb = slot_tables(where_ref, ids_ref, score_ref)
    comb_ref[...] = comb
    for i, ref in enumerate(tok_refs):
        rows = slice(i * HALF, (i + 1) * HALF)
        picked = dot(dispatch, ref[...]).astype(BF16)
        own_ref[rows] = picked[:HALF]
        far_ref[rows] = picked[HALF:]


def weave_body(own_ref, got_ref, *block_refs):
    own = own_ref[...].astype(F32)
    got = got_ref[...].astype(F32)
    for q, ref in enumerate(block_refs):
        parts = []
        for base in range(0, own.shape[0], HALF):
            rows = slice(base + q * CAP, base + (q + 1) * CAP)
            parts += [own[rows], got[rows]]
        ref[...] = jnp.concatenate(parts, axis=0).astype(BF16)


def part_body(b0, b1, b2, b3, own_ref, far_ref):
    blocks = [b[...].astype(F32) for b in (b0, b1, b2, b3)]
    own_ref[...] = jnp.concatenate([b[:CAP] for b in blocks], axis=0).astype(BF16)
    far_ref[...] = jnp.concatenate([b[CAP:] for b in blocks], axis=0).astype(BF16)


def join_body(*refs):
    refs[-1][...] = jnp.concatenate([r[...] for r in refs[:-1]], axis=0)


def hidden_body(rows_ref, wg_ref, wu_ref, out_ref):
    rows = rows_ref[...]
    gate = dot(rows, wg_ref[...])
    up = dot(rows, wu_ref[...])
    out_ref[...] = (gate * jax.nn.sigmoid(gate) * up).astype(BF16)


def down_body(mine_ref, theirs_ref, wd_ref, wdp_ref, keep_ref, send_ref):
    total = dot(mine_ref[...], wd_ref[...]) + dot(theirs_ref[...], wdp_ref[...])
    keep_ref[...] = total[:HOME]
    send_ref[...] = total[HOME:].astype(BF16)


def finish_body(*refs):
    blocks, pairs = refs[-PAIRS:], refs[:-PAIRS]
    col = 0
    for i in range(0, len(pairs), 2):
        total = pairs[i][...] + pairs[i + 1][...].astype(F32)
        cols = slice(col, col + total.shape[1])
        for q, ref in enumerate(blocks):
            ref[:, cols] = total[q * BLOCK : (q + 1) * BLOCK].astype(BF16)
        col += total.shape[1]


def slopes(rows, wg_ref, wu_ref):
    gate = dot(rows, wg_ref[...])
    up = dot(rows, wu_ref[...])
    sigma = jax.nn.sigmoid(gate)
    return up * sigma * (1.0 + gate * (1.0 - sigma)), gate * sigma


def slope_body(rows_ref, wg_ref, wu_ref, sg_ref, su_ref):
    sg_ref[...], su_ref[...] = slopes(rows_ref[...], wg_ref, wu_ref)


def grad_hidden_body(rows_ref, wd_ref, wdp_ref, mine_ref, send_ref):
    rows = rows_ref[...]
    mine_ref[...] = dot_t(rows, wd_ref[...])
    send_ref[...] = dot_t(rows, wdp_ref[...])


def grads_body(
    rows_ref, wg_ref, wu_ref, sg_ref, su_ref, mine_ref, got_ref, gg_ref, gu_ref
):
    rows = rows_ref[...]
    count = rows.shape[0]
    sgx, sux = slopes(rows, wg_ref, wu_ref)
    mine = mine_ref[...]
    got = got_ref[...]
    gg_ref[:count] = (mine * sg_ref[...]).astype(BF16)
    gg_ref[count:] = (got * sgx).astype(BF16)
    gu_ref[:count] = (mine * su_ref[...]).astype(BF16)
    gu_ref[count:] = (got * sux).astype(BF16)


def back_x_body(gg_ref, gu_ref, wg_ref, wu_ref, keep_ref, send_ref):
    total = dot_t(gg_ref[...], wg_ref[...]) + dot_t(gu_ref[...], wu_ref[...])
    count = keep_ref.shape[0]
    keep_ref[...] = total[:count]
    send_ref[...] = total[count:].astype(BF16)


def back_z_body(gg_ref, gu_ref, wg_ref, wu_ref, keep_ref, send_ref):
    total = dot_t(gg_ref[...], wg_ref[...]) + dot_t(gu_ref[...], wu_ref[...])
    keep_ref[:HOME] = total[:HOME]
    keep_ref[HOME:] = total[2 * HOME : 3 * HOME]
    send_ref[:HOME] = total[HOME : 2 * HOME].astype(BF16)
    send_ref[HOME:] = total[3 * HOME :].astype(BF16)


def fold_body(keep_ref, got_ref, own_ref, send_ref):
    total = keep_ref[...] + got_ref[...].astype(F32)
    own_ref[...] = total[:HOME]
    send_ref[...] = total[HOME:].astype(BF16)


def combine_body(base_ref, comb_ref, own_ref, far_ref, out_ref):
    rows = jnp.concatenate([own_ref[...], far_ref[...]], axis=0)
    total = dot(comb_ref[...], jnp.concatenate([rows, rows], axis=0))
    out_ref[...] = (base_ref[...].astype(F32) + total).astype(BF16)


def back_call(body, gg, gu, wg, wu, index, chunks):
    width = wg.shape[0] // chunks
    rows = gg.shape[0]
    whole = pl.BlockSpec((rows, gg.shape[1]), lambda i: (0, 0))
    part = pl.BlockSpec((width, wg.shape[1]), lambda i: (index, 0))
    half = rows // 2
    return pl.pallas_call(
        body,
        grid=(1,),
        out_shape=(shape(half, width, F32), shape(half, width)),
        in_specs=[whole, whole, part, part],
        out_specs=(
            pl.BlockSpec((half, width), lambda i: (0, 0)),
            pl.BlockSpec((half, width), lambda i: (0, 0)),
        ),
        compiler_params=pltpu.CompilerParams(vmem_limit_bytes=48 * 1024 * 1024),
        cost_estimate=pl.CostEstimate(
            flops=4 * rows * width * gg.shape[1],
            bytes_accessed=4 * width * wg.shape[1] + 6 * half * width,
            transcendentals=0,
        ),
    )(gg, gu, wg, wu)


def join(parts, after=()):
    rows = sum(p.shape[0] for p in parts)
    return call(join_body, [shape(rows, parts[0].shape[1])], parts, after=after)[0]


def shifts(blocks, back):
    a, b, c = SHIFT_A, SHIFT_B, SHIFT_C
    if back:
        a, b, c = inverse(a), inverse(b), inverse(c)
    return [blocks[0], move(blocks[1], a), move(blocks[2], b), move(blocks[3], c)]


def per_device(
    fwd_in, fwd_ids, fwd_score, bwd_in, bwd_ids, bwd_score, bwd_cot, w_gate, w_up, w_down
):
    tokens, width = fwd_in.shape[1:]
    wg, wu, wd = w_gate[0], w_up[0], w_down[0]
    hid = wg.shape[1]
    rows = 2 * HOME
    proj = 4 * rows * width * hid
    wdp = move(wd, DP_PAIR)
    where = lax.axis_index("expert").astype(jnp.int32).reshape(1)
    table = shape(tokens, 2 * HOME)

    own, far, fcomb = call(
        pack_body,
        [shape(HALF, width)] * 2 + [table],
        [where, fwd_ids[0].T, fwd_score[0].T, fwd_in[0]],
        smem=(0,),
        limit=60,
    )
    bown, bfar, bcomb = call(
        pack_body,
        [shape(2 * HALF, width)] * 2 + [table],
        [where, bwd_ids[0].T, bwd_score[0].T, bwd_in[0], bwd_cot[0]],
        smem=(0,),
        limit=60,
        after=(far,),
    )
    bbase = relay(bwd_cot[0], STAY, -1)
    bcomb = relay(bcomb, STAY, -1)
    blocks = call(weave_body, [shape(BLOCK, width)] * PAIRS, [own, move(far, ACROSS_XHI)])
    fy = jnp.concatenate(shifts(blocks, False), axis=0)
    bblocks = call(
        weave_body,
        [shape(2 * BLOCK, width)] * PAIRS,
        [bown, move(bfar, ACROSS_XHI)],
        after=(fy, bcomb),
    )
    fy = jnp.concatenate([fy, move(fy, Z_PAIR)], axis=0)
    fyx = move(fy, DP_PAIR)
    (mine,) = call(hidden_body, [shape(rows, hid)], [fy, wg, wu], proj)

    parts = shifts(bblocks, False)
    by = jnp.concatenate([p[:BLOCK] for p in parts], axis=0)
    cy = jnp.concatenate([p[BLOCK:] for p in parts], axis=0)
    byz = move(by, Z_PAIR)
    cy = jnp.concatenate([cy, move(cy, Z_PAIR)], axis=0)

    (theirs,) = call(hidden_body, [shape(rows, hid)], [fyx, wg, wu], proj, after=(mine,))
    theirs = move(theirs, DP_PAIR)
    by = join([by, byz], after=(theirs,))
    byx = move(by, DP_PAIR)
    keep, send = call(
        down_body, [shape(HOME, width, F32), shape(HOME, width)], [mine, theirs, wd, wdp], proj
    )
    blocks = call(finish_body, [shape(BLOCK, width)] * PAIRS, [keep, move(send, Z_PAIR)])
    own, far = call(part_body, [shape(HALF, width)] * 2, shifts(blocks, True))
    far = move(far, ACROSS_XHI)
    (fwd_out,) = call(combine_body, [shape(tokens, width)], [fwd_in[0], fcomb, own, far])
    fwd_out = relay(fwd_out, STAY, 1)

    sg, su = call(
        slope_body, [shape(rows, hid, F32)] * 2, [by, wg, wu], proj, after=(bbase,)
    )
    gh, gh_send = call(grad_hidden_body, [shape(rows, hid, F32)] * 2, [cy, wd, wdp], proj)
    gh_got = move(gh_send, DP_PAIR)
    gg, gu = call(
        grads_body, [shape(2 * rows, hid)] * 2, [byx, wg, wu, sg, su, gh, gh_got], proj
    )
    half = width // 2
    fold = [shape(HOME, half, F32), shape(HOME, half)]
    xkeep, xsend = back_call(back_x_body, gg, gu, wg, wu, 0, 2)
    zkeep, zsend = back_call(back_z_body, gg, gu, wg, wu, 1, 2)
    xgot, zgot = move(xsend, DP_PAIR), move(zsend, Z_PAIR)
    xkeep, xsend = call(fold_body, fold, [xkeep, xgot])
    zkeep, zsend = call(fold_body, fold, [zkeep, zgot])
    xgot, zgot = move(xsend, Z_PAIR), move(zsend, DP_PAIR)
    blocks = call(
        finish_body, [shape(BLOCK, width)] * PAIRS, [xkeep, xgot, zkeep, zgot]
    )
    own, far = call(part_body, [shape(HALF, width)] * 2, shifts(blocks, True))
    own, far = relay(own, STAY, -1), relay(far, ACROSS_XHI, -1)
    (bwd_out,) = call(combine_body, [shape(tokens, width)], [bbase, bcomb, own, far])
    return fwd_out[None], bwd_out[None]


def solution(mesh):
    rows = P("pipe", ("expert", "dp"), None)
    cols = P("pipe", None, ("expert", "dp"))
    return jax.shard_map(
        per_device,
        mesh=mesh,
        in_specs=(rows,) * 7 + (cols, cols, rows),
        out_specs=(rows, rows),
        check_vma=False,
    )
```

time: 206 us -> 157 us (0.76)
  starting transfers between devices: 101 us -> 76.7 us
  waiting for transfers between devices: 82 us -> 63.8 us
  local copies, waits for them, and re-layouts: 5.58 us -> 1.18 us
    ppermute x10 -> x5, starting transfers between devices: 46.1 us -> 31.6 us  [relay(): return lax.ppermute(value, ('pipe', 'expert', 'dp'), full)]
    ppermute x36 -> x28, waiting for transfers between devices: 68.2 us -> 54 us  [move(): return lax.ppermute(value, ('expert', 'dp'), pairs)]
    ppermute x36 -> x28, starting transfers between devices: 55.3 us -> 45.1 us  [move(): return lax.ppermute(value, ('expert', 'dp'), pairs)]
    unnamed x33 -> x20, local copies, waits for them, and re-layouts: 5.55 us -> 1.01 us
    ppermute x10 -> x5, waiting for transfers between devices: 13.8 us -> 9.76 us  [relay(): return lax.ppermute(value, ('pipe', 'expert', 'dp'), full)]
    pallas_call x23 -> x21, Pallas kernels: 14 us -> 13.7 us  [the longest x19 12.3 us: call(): pl.pallas_call(run, out_shape=tuple(outs), in_specs=specs, out_specs=tupl...]
  transfers between devices with their start and end apart: 46 -> 33, of which waited for: 17 -> 15; matrix products, arithmetic and copies ran while one was open for 0% -> 0% of each run, Pallas kernels for 6% -> 6%
where the time goes in v2:
time: 157 us; the launch traced here: 156 us
  starting transfers between devices  76.7 us (49%)
  waiting for transfers between devices  63.8 us (41%)
  Pallas kernels  13.7 us (9%)
    ppermute x28, waiting for transfers between devices, move(): return lax.ppermute(value, ('expert', 'dp'), pairs)  54 us
    ppermute x28, starting transfers between devices, move(): return lax.ppermute(value, ('expert', 'dp'), pairs)  45.1 us
    ppermute x5, starting transfers between devices, relay(): return lax.ppermute(value, ('pipe', 'expert', 'dp'), full)  31.6 us
    pallas_call x19, Pallas kernels, call(): pl.pallas_call(run, out_shape=tuple(outs), in_specs=specs, out_specs=tupl...  12.3 us
    ppermute x5, waiting for transfers between devices, relay(): return lax.ppermute(value, ('pipe', 'expert', 'dp'), full)  9.76 us
  transfers between devices with their start and end apart: 33, of which 15 were waited for; matrix products, arithmetic and copies ran while one was open for 0% of the time, Pallas kernels for 6%

profile of v2, /device:TPU:1, one launch (start us, length us, event | category | flops | bytes accessed | tf_op | source)
XLA Modules:
  0.0 156.4 jit_solution(17830159280390661057)
XLA Ops:
  0.6 2.6 %shard_map.113 = (bf16[32,3584]{1,0:T(8,128)(2,1)}, bf16[32,3584]{1,0:T(8,128)(2,1)}, bf16[128,128]{1,0:T(8,128)(2,1)}) custom-call(s32[1]{0:T(128)} %bitcast.1.refs_0_, s32[8,128]{1,0:T(8,128)} %bitcast.43, f32[8,128]{1,0:T(8,128)} %bitcast.44, bf16[128,3584]{1,0:T(8,128)(2,1)} %bitcast.36), custom_call_target="tpu_custom_call" | custom-call | bytes 1417220 | tf_op jit(solution)/shard_map/pallas_call | solution.py:30
  3.2 3.3 %collective-permute-start = (bf16[32,3584]{1,0:T(8,128)(2,1)}, bf16[32,3584]{1,0:T(8,128)(2,1)S(1)}, u32[]{:S(2)}, u32[]{:S(2)}) collective-permute-start(bf16[32,3584]{1,0:T(8,128)(2,1)} %get-tuple-element.46.refs_5_), channel_id=1, source_target_pairs={{0,17},{1,16},{2,19},{3,18},{4,21},{5,20},{6,23},{7,22},{8,25},{9,... | collective-permute-start | bytes 688136 | tf_op jit(solution)/shard_map/ppermute | solution.py:76
  6.5 3.0 %shard_map.121 = (bf16[64,3584]{1,0:T(8,128)(2,1)}, bf16[64,3584]{1,0:T(8,128)(2,1)}, bf16[128,128]{1,0:T(8,128)(2,1)}) custom-call(s32[1]{0:T(128)} %bitcast.1.refs_0_, s32[8,128]{1,0:T(8,128)} %bitcast.45, f32[8,128]{1,0:T(8,128)} %bitcast.46, bf16[128,3584]{1,0:T(8,128)(2,1)} %bitcast.38, bf16[128,3584]{1,0:T(8,128)(2,1)} %bitcast.39, ...), custom_call_target="tpu_custom_call" | custom-call | bytes 2793476 | tf_op jit(solution)/shard_map/pallas_call | solution.py:30
  9.5 3.0 %collective-permute-start.15 = (bf16[128,128]{1,0:T(8,128)(2,1)}, bf16[128,128]{1,0:T(8,128)(2,1)S(1)}, u32[]{:S(2)}, u32[]{:S(2)}) collective-permute-start(bf16[128,128]{1,0:T(8,128)(2,1)} %get-tuple-element.59), channel_id=1, source_target_pairs={{32,0},{33,1},{34,2},{35,3},{36,4},{37,5},{38,6},{39,7},{40,8},{41... | collective-permute-start | bytes 98312 | tf_op jit(solution)/shard_map/ppermute | solution.py:87
  12.5 2.0 %collective-permute-start.16 = (bf16[64,3584]{1,0:T(8,128)(2,1)}, bf16[64,3584]{1,0:T(8,128)(2,1)S(1)}, u32[]{:S(2)}, u32[]{:S(2)}) collective-permute-start(bf16[64,3584]{1,0:T(8,128)(2,1)} %get-tuple-element.61), channel_id=1, source_target_pairs={{0,17},{1,16},{2,19},{3,18},{4,21},{5,20},{6,23},{7,22},{8,25},{9,... | collective-permute-start | bytes 1376264 | tf_op jit(solution)/shard_map/ppermute | solution.py:76
  14.6 1.3 collective-permute-start.1
  15.9 3.8 %collective-permute-start.2 = (bf16[16,3584]{1,0:T(8,128)(2,1)S(1)}, bf16[16,3584]{1,0:T(8,128)(2,1)S(1)}, u32[]{:S(2)}, u32[]{:S(2)}) collective-permute-start(bf16[16,3584]{1,0:T(8,128)(2,1)S(1)} %get-tuple-element.49), channel_id=1, source_target_pairs={{0,14},{1,15},{2,4},{3,5},{4,2},{5,3},{6,8},{7,9},{8,6},{9,7},{10,... | collective-permute-start | bytes 344072 | tf_op jit(solution)/shard_map/ppermute | solution.py:76
  19.7 2.0 %collective-permute-done.1 = bf16[16,3584]{1,0:T(8,128)(2,1)S(1)} collective-permute-done((bf16[16,3584]{1,0:T(8,128)(2,1)S(1)}, bf16[16,3584]{1,0:T(8,128)(2,1)S(1)}, u32[]{:S(2)}, u32[]{:S(2)}) %collective-permute-start.1) | collective-permute-done | bytes 114720 | tf_op jit(solution)/shard_map/ppermute | solution.py:76
  21.8 2.6 %collective-permute-start.3 = (bf16[16,3584]{1,0:T(8,128)(2,1)S(1)}, bf16[16,3584]{1,0:T(8,128)(2,1)S(1)}, u32[]{:S(2)}, u32[]{:S(2)}) collective-permute-start(bf16[16,3584]{1,0:T(8,128)(2,1)S(1)} %get-tuple-element.50), channel_id=1, source_target_pairs={{0,10},{1,11},{2,8},{3,9},{4,14},{5,15},{6,12},{7,13},{8,2},{9,3},... | collective-permute-start | bytes 344072 | tf_op jit(solution)/shard_map/ppermute | solution.py:76
  25.0 3.5 %collective-permute-done.3 = bf16[16,3584]{1,0:T(8,128)(2,1)S(1)} collective-permute-done((bf16[16,3584]{1,0:T(8,128)(2,1)S(1)}, bf16[16,3584]{1,0:T(8,128)(2,1)S(1)}, u32[]{:S(2)}, u32[]{:S(2)}) %collective-permute-start.3) | collective-permute-done | bytes 114720 | tf_op jit(solution)/shard_map/ppermute | solution.py:76
  28.7 1.9 %collective-permute-start.17 = (bf16[32,3584]{1,0:T(8,128)(2,1)S(1)}, bf16[32,3584]{1,0:T(8,128)(2,1)S(1)}, u32[]{:S(2)}, u32[]{:S(2)}) collective-permute-start(bf16[32,3584]{1,0:T(8,128)(2,1)S(1)} %get-tuple-element.63), channel_id=1, source_target_pairs={{0,4},{1,5},{2,14},{3,15},{4,8},{5,9},{6,2},{7,3},{8,12},{9,13},{1... | collective-permute-start | bytes 688136 | tf_op jit(solution)/shard_map/ppermute | solution.py:76
  30.7 3.5 %collective-permute-start.18 = (bf16[32,3584]{1,0:T(8,128)(2,1)S(1)}, bf16[32,3584]{1,0:T(8,128)(2,1)S(1)}, u32[]{:S(2)}, u32[]{:S(2)}) collective-permute-start(bf16[32,3584]{1,0:T(8,128)(2,1)S(1)} %get-tuple-element.64), channel_id=1, source_target_pairs={{0,14},{1,15},{2,4},{3,5},{4,2},{5,3},{6,8},{7,9},{8,6},{9,7},{10,... | collective-permute-start | bytes 688136 | tf_op jit(solution)/shard_map/ppermute | solution.py:76
  34.6 11.7 %collective-permute-done.17 = bf16[32,3584]{1,0:T(8,128)(2,1)S(1)} collective-permute-done((bf16[32,3584]{1,0:T(8,128)(2,1)S(1)}, bf16[32,3584]{1,0:T(8,128)(2,1)S(1)}, u32[]{:S(2)}, u32[]{:S(2)}) %collective-permute-start.17) | collective-permute-done | bytes 229408 | tf_op jit(solution)/shard_map/ppermute | solution.py:76
  46.4 5.2 %collective-permute-done.19 = bf16[32,3584]{1,0:T(8,128)(2,1)S(1)} collective-permute-done((bf16[32,3584]{1,0:T(8,128)(2,1)S(1)}, bf16[32,3584]{1,0:T(8,128)(2,1)S(1)}, u32[]{:S(2)}, u32[]{:S(2)}) %collective-permute-start.19) | collective-permute-done | bytes 229408 | tf_op jit(solution)/shard_map/ppermute | solution.py:76
  51.7 4.9 %collective-permute-start.5 = (bf16[128,3584]{1,0:T(8,128)(2,1)S(1)}, bf16[128,3584]{1,0:T(8,128)(2,1)S(1)}, u32[]{:S(2)}, u32[]{:S(2)}) collective-permute-start(bf16[128,3584]{1,0:T(8,128)(2,1)S(1)} %constant_dynamic-update-slice_fusion.4.refs_0_), channel_id=1, source_target_pairs={{0,1},{1,0},{2,3},{3,2},{4,5},{5,4},{6,7},{7,6},{8,9},{9,8},{10,11... | collective-permute-start | bytes 2752520 | tf_op jit(solution)/shard_map/ppermute | solution.py:76
  56.8 1.5 collective-permute-start.22
  58.3 6.4 %collective-permute-start.14 = (bf16[128,3584]{1,0:T(8,128)(2,1)S(1)}, bf16[128,3584]{1,0:T(8,128)(2,1)S(1)}, u32[]{:S(2)}, u32[]{:S(2)}) collective-permute-start(bf16[128,3584]{1,0:T(8,128)(2,1)S(1)} %bitcast.40), channel_id=1, source_target_pairs={{32,0},{33,1},{34,2},{35,3},{36,4},{37,5},{38,6},{39,7},{40,8},{41... | collective-permute-start | bytes 2752520 | tf_op jit(solution)/shard_map/ppermute | solution.py:87
  65.4 8.4 %collective-permute-done.5.refs_0_ = bf16[128,3584]{1,0:T(8,128)(2,1)S(1)} collective-permute-done((bf16[128,3584]{1,0:T(8,128)(2,1)S(1)}, bf16[128,3584]{1,0:T(8,128)(2,1)S(1)}, u32[]{:S(2)}, u32[]{:S(2)}) %collective-permute-start.5) | collective-permute-done | bytes 917536 | tf_op jit(solution)/shard_map/ppermute | solution.py:76
  74.5 1.3 collective-permute-start.6
  75.7 2.5 %collective-permute-done.6.refs_1_.refs_2_ = bf16[128,256]{1,0:T(8,128)(2,1)S(1)} collective-permute-done((bf16[128,256]{1,0:T(8,128)(2,1)S(1)}, bf16[128,256]{1,0:T(8,128)(2,1)S(1)}, u32[]{:S(2)}, u32[]{:S(2)}) %collective-permute-start.6) | collective-permute-done | bytes 65568 | tf_op jit(solution)/shard_map/ppermute | solution.py:76
  78.3 1.3 collective-permute-start.21
  80.5 1.3 shard_map.125
  82.2 5.9 %collective-permute-done.8.refs_1_ = bf16[64,3584]{1,0:T(8,128)(2,1)S(1)} collective-permute-done((bf16[64,3584]{1,0:T(8,128)(2,1)S(1)}, bf16[64,3584]{1,0:T(8,128)(2,1)S(1)}, u32[]{:S(2)}, u32[]{:S(2)}) %collective-permute-start.8) | collective-permute-done | bytes 458784 | tf_op jit(solution)/shard_map/ppermute | solution.py:76
  88.2 3.9 %collective-permute-start.10 = (bf16[16,3584]{1,0:T(8,128)(2,1)S(1)}, bf16[16,3584]{1,0:T(8,128)(2,1)S(1)}, u32[]{:S(2)}, u32[]{:S(2)}) collective-permute-start(bf16[16,3584]{1,0:T(8,128)(2,1)S(1)} %get-tuple-element.55), channel_id=1, source_target_pairs={{14,0},{15,1},{4,2},{5,3},{2,4},{3,5},{8,6},{9,7},{6,8},{7,9},{12,... | collective-permute-start | bytes 344072 | tf_op jit(solution)/shard_map/ppermute | solution.py:76
  92.1 0.9 collective-permute-start.11
  93.0 2.1 %collective-permute-start.9 = (bf16[16,3584]{1,0:T(8,128)(2,1)S(1)}, bf16[16,3584]{1,0:T(8,128)(2,1)S(1)}, u32[]{:S(2)}, u32[]{:S(2)}) collective-permute-start(bf16[16,3584]{1,0:T(8,128)(2,1)S(1)} %get-tuple-element.54), channel_id=1, source_target_pairs={{4,0},{5,1},{14,2},{15,3},{8,4},{9,5},{2,6},{3,7},{12,8},{13,9},{6... | collective-permute-start | bytes 344072 | tf_op jit(solution)/shard_map/ppermute | solution.py:76
  95.1 0.7 shard_map.124
  95.7 3.2 %collective-permute-done.11.refs_3_ = bf16[16,3584]{1,0:T(8,128)(2,1)S(1)} collective-permute-done((bf16[16,3584]{1,0:T(8,128)(2,1)S(1)}, bf16[16,3584]{1,0:T(8,128)(2,1)S(1)}, u32[]{:S(2)}, u32[]{:S(2)}) %collective-permute-start.11) | collective-permute-done | bytes 114720 | tf_op jit(solution)/shard_map/ppermute | solution.py:76
  99.0 2.5 %collective-permute-start.12 = (bf16[32,3584]{1,0:T(8,128)(2,1)S(1)}, bf16[32,3584]{1,0:T(8,128)(2,1)S(1)}, u32[]{:S(2)}, u32[]{:S(2)}) collective-permute-start(bf16[32,3584]{1,0:T(8,128)(2,1)S(1)} %get-tuple-element.58), channel_id=1, source_target_pairs={{0,17},{1,16},{2,19},{3,18},{4,21},{5,20},{6,23},{7,22},{8,25},{9,... | collective-permute-start | bytes 688136 | tf_op jit(solution)/shard_map/ppermute | solution.py:76
  101.5 0.7 shard_map.126
  102.2 0.7 shard_map.129
  103.0 0.7 shard_map.127
  103.7 0.9 collective-permute-start.24
  104.7 0.8 collective-permute-done.12.refs_3_
  105.9 11.5 %collective-permute-start.13 = (bf16[128,3584]{1,0:T(8,128)(2,1)S(1)}, bf16[128,3584]{1,0:T(8,128)(2,1)S(1)}, u32[]{:S(2)}, u32[]{:S(2)}) collective-permute-start(bf16[128,3584]{1,0:T(8,128)(2,1)S(1)} %shard_map.120), channel_id=1, source_target_pairs={{0,32},{1,33},{2,34},{3,35},{4,36},{5,37},{6,38},{7,39},{8,40},{9,... | collective-permute-start | bytes 2752520 | tf_op jit(solution)/shard_map/ppermute | solution.py:87
  117.5 0.7 collective-permute-start.27
  118.3 0.7 collective-permute-start.25
  118.9 6.0 %collective-permute-done.27.refs_3_ = bf16[64,1792]{1,0:T(8,128)(2,1)S(1)} collective-permute-done((bf16[64,1792]{1,0:T(8,128)(2,1)S(1)}, bf16[64,1792]{1,0:T(8,128)(2,1)S(1)}, u32[]{:S(2)}, u32[]{:S(2)}) %collective-permute-start.27) | collective-permute-done | bytes 229408 | tf_op jit(solution)/shard_map/ppermute | solution.py:76
  125.7 1.3 collective-permute-start.29
  127.0 2.7 %collective-permute-start.30 = (bf16[16,3584]{1,0:T(8,128)(2,1)S(1)}, bf16[16,3584]{1,0:T(8,128)(2,1)S(1)}, u32[]{:S(2)}, u32[]{:S(2)}) collective-permute-start(bf16[16,3584]{1,0:T(8,128)(2,1)S(1)} %get-tuple-element.83), channel_id=1, source_target_pairs={{10,0},{11,1},{8,2},{9,3},{14,4},{15,5},{12,6},{13,7},{2,8},{3,9},... | collective-permute-start | bytes 344072 | tf_op jit(solution)/shard_map/ppermute | solution.py:76
  129.6 0.9 collective-permute-done.29.refs_2_
  130.5 3.2 %collective-permute-done.30.refs_3_ = bf16[16,3584]{1,0:T(8,128)(2,1)S(1)} collective-permute-done((bf16[16,3584]{1,0:T(8,128)(2,1)S(1)}, bf16[16,3584]{1,0:T(8,128)(2,1)S(1)}, u32[]{:S(2)}, u32[]{:S(2)}) %collective-permute-start.30) | collective-permute-done | bytes 114720 | tf_op jit(solution)/shard_map/ppermute | solution.py:76
  133.8 8.7 %collective-permute-start.31 = (bf16[32,3584]{1,0:T(8,128)(2,1)S(1)}, bf16[32,3584]{1,0:T(8,128)(2,1)S(1)}, u32[]{:S(2)}, u32[]{:S(2)}) collective-permute-start(bf16[32,3584]{1,0:T(8,128)(2,1)S(1)} %get-tuple-element.84), channel_id=1, source_target_pairs={{32,0},{33,1},{34,2},{35,3},{36,4},{37,5},{38,6},{39,7},{40,8},{41... | collective-permute-start | bytes 688136 | tf_op jit(solution)/shard_map/ppermute | solution.py:87
  142.5 1.9 %collective-permute-start.32 = (bf16[32,3584]{1,0:T(8,128)(2,1)S(1)}, bf16[32,3584]{1,0:T(8,128)(2,1)S(1)}, u32[]{:S(2)}, u32[]{:S(2)}) collective-permute-start(bf16[32,3584]{1,0:T(8,128)(2,1)S(1)} %get-tuple-element.85), channel_id=1, source_target_pairs={{32,17},{33,16},{34,19},{35,18},{36,21},{37,20},{38,23},{39,22},{4... | collective-permute-start | bytes 688136 | tf_op jit(solution)/shard_map/ppermute | solution.py:87
  144.4 3.6 %collective-permute-done.31.refs_2_ = bf16[32,3584]{1,0:T(8,128)(2,1)S(1)} collective-permute-done((bf16[32,3584]{1,0:T(8,128)(2,1)S(1)}, bf16[32,3584]{1,0:T(8,128)(2,1)S(1)}, u32[]{:S(2)}, u32[]{:S(2)}) %collective-permute-start.31) | collective-permute-done | bytes 229408 | tf_op jit(solution)/shard_map/ppermute | solution.py:87
  148.0 6.2 %collective-permute-done.32.refs_3_ = bf16[32,3584]{1,0:T(8,128)(2,1)S(1)} collective-permute-done((bf16[32,3584]{1,0:T(8,128)(2,1)S(1)}, bf16[32,3584]{1,0:T(8,128)(2,1)S(1)}, u32[]{:S(2)}, u32[]{:S(2)}) %collective-permute-start.32) | collective-permute-done | bytes 229408 | tf_op jit(solution)/shard_map/ppermute | solution.py:87
  154.2 1.3 shard_map.133
  155.5 0.9 copy.24
  (68 shorter events, 5.9 us)
Async XLA Ops:
  0.6 13.9 %copy-start.2 = (bf16[1,256,3584]{2,1,0:T(8,128)(2,1)S(1)}, bf16[1,256,3584]{2,1,0:T(8,128)(2,1)}, u32[]{:S(2)}) copy-start(bf16[1,256,3584]{2,1,0:T(8,128)(2,1)} %param.19) | copy-start | bytes 5505028
  3.2 11.3 %copy-start.5 = (bf16[32,3584]{1,0:T(8,128)(2,1)S(1)}, bf16[32,3584]{1,0:T(8,128)(2,1)}, u32[]{:S(2)}) copy-start(bf16[32,3584]{1,0:T(8,128)(2,1)} %get-tuple-element.45.refs_0_) | copy-start | bytes 688132
  3.2 11.3 %collective-permute-start = (bf16[32,3584]{1,0:T(8,128)(2,1)}, bf16[32,3584]{1,0:T(8,128)(2,1)S(1)}, u32[]{:S(2)}, u32[]{:S(2)}) collective-permute-start(bf16[32,3584]{1,0:T(8,128)(2,1)} %get-tuple-element.46.refs_5_), channel_id=1, source_target_pairs={{0,17},{1,16},{2,19},{3,18},{4,21},{5,20},{6,23},{7,22},{8,25},{9,... | collective-permute-start | bytes 688136 | tf_op jit(solution)/shard_map/ppermute | solution.py:76
  9.5 19.2 %copy-start.4 = (bf16[64,3584]{1,0:T(8,128)(2,1)S(1)}, bf16[64,3584]{1,0:T(8,128)(2,1)}, u32[]{:S(2)}) copy-start(bf16[64,3584]{1,0:T(8,128)(2,1)} %get-tuple-element.60.refs_0_) | copy-start | bytes 1376260
  9.5 19.1 %collective-permute-start.15 = (bf16[128,128]{1,0:T(8,128)(2,1)}, bf16[128,128]{1,0:T(8,128)(2,1)S(1)}, u32[]{:S(2)}, u32[]{:S(2)}) collective-permute-start(bf16[128,128]{1,0:T(8,128)(2,1)} %get-tuple-element.59), channel_id=1, source_target_pairs={{32,0},{33,1},{34,2},{35,3},{36,4},{37,5},{38,6},{39,7},{40,8},{41... | collective-permute-start | bytes 98312 | tf_op jit(solution)/shard_map/ppermute | solution.py:87
  12.5 16.2 %collective-permute-start.16 = (bf16[64,3584]{1,0:T(8,128)(2,1)}, bf16[64,3584]{1,0:T(8,128)(2,1)S(1)}, u32[]{:S(2)}, u32[]{:S(2)}) collective-permute-start(bf16[64,3584]{1,0:T(8,128)(2,1)} %get-tuple-element.61), channel_id=1, source_target_pairs={{0,17},{1,16},{2,19},{3,18},{4,21},{5,20},{6,23},{7,22},{8,25},{9,... | collective-permute-start | bytes 1376264 | tf_op jit(solution)/shard_map/ppermute | solution.py:76
  14.5 65.1 %collective-permute-start.7 = (bf16[256,3584]{1,0:T(8,128)(2,1)S(1)}, bf16[256,3584]{1,0:T(8,128)(2,1)S(1)}, u32[]{:S(2)}, u32[]{:S(2)}) collective-permute-start(bf16[256,3584]{1,0:T(8,128)(2,1)S(1)} %bitcast.33), channel_id=1, source_target_pairs={{0,1},{1,0},{2,3},{3,2},{4,5},{5,4},{6,7},{7,6},{8,9},{9,8},{10,11... | collective-permute-start | bytes 5505032 | tf_op jit(solution)/shard_map/ppermute | solution.py:76
  14.6 7.2 %collective-permute-start.1 = (bf16[16,3584]{1,0:T(8,128)(2,1)S(1)}, bf16[16,3584]{1,0:T(8,128)(2,1)S(1)}, u32[]{:S(2)}, u32[]{:S(2)}) collective-permute-start(bf16[16,3584]{1,0:T(8,128)(2,1)S(1)} %get-tuple-element.48), channel_id=1, source_target_pairs={{0,4},{1,5},{2,14},{3,15},{4,8},{5,9},{6,2},{7,3},{8,12},{9,13},{1... | collective-permute-start | bytes 344072 | tf_op jit(solution)/shard_map/ppermute | solution.py:76
  15.9 9.1 %collective-permute-start.2 = (bf16[16,3584]{1,0:T(8,128)(2,1)S(1)}, bf16[16,3584]{1,0:T(8,128)(2,1)S(1)}, u32[]{:S(2)}, u32[]{:S(2)}) collective-permute-start(bf16[16,3584]{1,0:T(8,128)(2,1)S(1)} %get-tuple-element.49), channel_id=1, source_target_pairs={{0,14},{1,15},{2,4},{3,5},{4,2},{5,3},{6,8},{7,9},{8,6},{9,7},{10,... | collective-permute-start | bytes 344072 | tf_op jit(solution)/shard_map/ppermute | solution.py:76
  21.8 6.8 %collective-permute-start.3 = (bf16[16,3584]{1,0:T(8,128)(2,1)S(1)}, bf16[16,3584]{1,0:T(8,128)(2,1)S(1)}, u32[]{:S(2)}, u32[]{:S(2)}) collective-permute-start(bf16[16,3584]{1,0:T(8,128)(2,1)S(1)} %get-tuple-element.50), channel_id=1, source_target_pairs={{0,10},{1,11},{2,8},{3,9},{4,14},{5,15},{6,12},{7,13},{8,2},{9,3},... | collective-permute-start | bytes 344072 | tf_op jit(solution)/shard_map/ppermute | solution.py:76
  28.5 23.1 %collective-permute-start.4 = (bf16[64,3584]{1,0:T(8,128)(2,1)S(1)}, bf16[64,3584]{1,0:T(8,128)(2,1)S(1)}, u32[]{:S(2)}, u32[]{:S(2)}) collective-permute-start(bf16[64,3584]{1,0:T(8,128)(2,1)S(1)} %get-tuple-element.98.refs_2_), channel_id=1, source_target_pairs={{0,2},{1,3},{2,0},{3,1},{4,6},{5,7},{6,4},{7,5},{8,10},{9,11},{10,... | collective-permute-start | bytes 1376264 | tf_op jit(solution)/shard_map/ppermute | solution.py:76
  28.7 17.6 %collective-permute-start.17 = (bf16[32,3584]{1,0:T(8,128)(2,1)S(1)}, bf16[32,3584]{1,0:T(8,128)(2,1)S(1)}, u32[]{:S(2)}, u32[]{:S(2)}) collective-permute-start(bf16[32,3584]{1,0:T(8,128)(2,1)S(1)} %get-tuple-element.63), channel_id=1, source_target_pairs={{0,4},{1,5},{2,14},{3,15},{4,8},{5,9},{6,2},{7,3},{8,12},{9,13},{1... | collective-permute-start | bytes 688136 | tf_op jit(solution)/shard_map/ppermute | solution.py:76
  30.6 27.7 %copy-start.7 = (bf16[1,128,3584]{2,1,0:T(8,128)(2,1)S(1)}, bf16[1,128,3584]{2,1,0:T(8,128)(2,1)}, u32[]{:S(2)}) copy-start(bf16[1,128,3584]{2,1,0:T(8,128)(2,1)} %param.16) | copy-start | bytes 2752516
  30.7 15.7 %collective-permute-start.18 = (bf16[32,3584]{1,0:T(8,128)(2,1)S(1)}, bf16[32,3584]{1,0:T(8,128)(2,1)S(1)}, u32[]{:S(2)}, u32[]{:S(2)}) collective-permute-start(bf16[32,3584]{1,0:T(8,128)(2,1)S(1)} %get-tuple-element.64), channel_id=1, source_target_pairs={{0,14},{1,15},{2,4},{3,5},{4,2},{5,3},{6,8},{7,9},{8,6},{9,7},{10,... | collective-permute-start | bytes 688136 | tf_op jit(solution)/shard_map/ppermute | solution.py:76
  34.1 17.5 %collective-permute-start.19 = (bf16[32,3584]{1,0:T(8,128)(2,1)S(1)}, bf16[32,3584]{1,0:T(8,128)(2,1)S(1)}, u32[]{:S(2)}, u32[]{:S(2)}) collective-permute-start(bf16[32,3584]{1,0:T(8,128)(2,1)S(1)} %get-tuple-element.65), channel_id=1, source_target_pairs={{0,10},{1,11},{2,8},{3,9},{4,14},{5,15},{6,12},{7,13},{8,2},{9,3},... | collective-permute-start | bytes 688136 | tf_op jit(solution)/shard_map/ppermute | solution.py:76
  46.3 18.4 %copy-start = (bf16[1,3584,256]{2,1,0:T(8,128)(2,1)S(1)}, bf16[1,3584,256]{2,1,0:T(8,128)(2,1)}, u32[]{:S(2)}) copy-start(bf16[1,3584,256]{2,1,0:T(8,128)(2,1)} %param.17) | copy-start | bytes 5505028
  46.4 18.4 %copy-start.1 = (bf16[1,3584,256]{2,1,0:T(8,128)(2,1)S(1)}, bf16[1,3584,256]{2,1,0:T(8,128)(2,1)}, u32[]{:S(2)}) copy-start(bf16[1,3584,256]{2,1,0:T(8,128)(2,1)} %param.18) | copy-start | bytes 5505028
  51.7 22.1 %collective-permute-start.5 = (bf16[128,3584]{1,0:T(8,128)(2,1)S(1)}, bf16[128,3584]{1,0:T(8,128)(2,1)S(1)}, u32[]{:S(2)}, u32[]{:S(2)}) collective-permute-start(bf16[128,3584]{1,0:T(8,128)(2,1)S(1)} %constant_dynamic-update-slice_fusion.4.refs_0_), channel_id=1, source_target_pairs={{0,1},{1,0},{2,3},{3,2},{4,5},{5,4},{6,7},{7,6},{8,9},{9,8},{10,11... | collective-permute-start | bytes 2752520 | tf_op jit(solution)/shard_map/ppermute | solution.py:76
  56.6 19.1 %collective-permute-start.20 = (bf16[64,3584]{1,0:T(8,128)(2,1)S(1)}, bf16[64,3584]{1,0:T(8,128)(2,1)S(1)}, u32[]{:S(2)}, u32[]{:S(2)}) collective-permute-start(bf16[64,3584]{1,0:T(8,128)(2,1)S(1)} %pad_maximum_fusion.refs_0_), channel_id=1, source_target_pairs={{0,2},{1,3},{2,0},{3,1},{4,6},{5,7},{6,4},{7,5},{8,10},{9,11},{10,... | collective-permute-start | bytes 1376264 | tf_op jit(solution)/shard_map/ppermute | solution.py:76
  56.8 23.7 %collective-permute-start.22 = (bf16[64,3584]{1,0:T(8,128)(2,1)S(1)}, bf16[64,3584]{1,0:T(8,128)(2,1)S(1)}, u32[]{:S(2)}, u32[]{:S(2)}) collective-permute-start(bf16[64,3584]{1,0:T(8,128)(2,1)S(1)} %pad_maximum_fusion.1), channel_id=1, source_target_pairs={{0,2},{1,3},{2,0},{3,1},{4,6},{5,7},{6,4},{7,5},{8,10},{9,11},{10,... | collective-permute-start | bytes 1376264 | tf_op jit(solution)/shard_map/ppermute | solution.py:76
  58.3 34.7 %collective-permute-start.14 = (bf16[128,3584]{1,0:T(8,128)(2,1)S(1)}, bf16[128,3584]{1,0:T(8,128)(2,1)S(1)}, u32[]{:S(2)}, u32[]{:S(2)}) collective-permute-start(bf16[128,3584]{1,0:T(8,128)(2,1)S(1)} %bitcast.40), channel_id=1, source_target_pairs={{32,0},{33,1},{34,2},{35,3},{36,4},{37,5},{38,6},{39,7},{40,8},{41... | collective-permute-start | bytes 2752520 | tf_op jit(solution)/shard_map/ppermute | solution.py:87
  74.5 3.7 %collective-permute-start.6 = (bf16[128,256]{1,0:T(8,128)(2,1)S(1)}, bf16[128,256]{1,0:T(8,128)(2,1)S(1)}, u32[]{:S(2)}, u32[]{:S(2)}) collective-permute-start(bf16[128,256]{1,0:T(8,128)(2,1)S(1)} %shard_map.116), channel_id=1, source_target_pairs={{0,1},{1,0},{2,3},{3,2},{4,5},{5,4},{6,7},{7,6},{8,9},{9,8},{10,11... | collective-permute-start | bytes 196616 | tf_op jit(solution)/shard_map/ppermute | solution.py:76
  78.3 23.3 %collective-permute-start.21 = (bf16[128,3584]{1,0:T(8,128)(2,1)S(1)}, bf16[128,3584]{1,0:T(8,128)(2,1)S(1)}, u32[]{:S(2)}, u32[]{:S(2)}) collective-permute-start(bf16[128,3584]{1,0:T(8,128)(2,1)S(1)} %shard_map.123.refs_0_), channel_id=1, source_target_pairs={{0,1},{1,0},{2,3},{3,2},{4,5},{5,4},{6,7},{7,6},{8,9},{9,8},{10,11... | collective-permute-start | bytes 2752520 | tf_op jit(solution)/shard_map/ppermute | solution.py:76
  80.2 7.9 %collective-permute-start.8 = (bf16[64,3584]{1,0:T(8,128)(2,1)S(1)}, bf16[64,3584]{1,0:T(8,128)(2,1)S(1)}, u32[]{:S(2)}, u32[]{:S(2)}) collective-permute-start(bf16[64,3584]{1,0:T(8,128)(2,1)S(1)} %get-tuple-element.52), channel_id=1, source_target_pairs={{0,2},{1,3},{2,0},{3,1},{4,6},{5,7},{6,4},{7,5},{8,10},{9,11},{10,... | collective-permute-start | bytes 1376264 | tf_op jit(solution)/shard_map/ppermute | solution.py:76
  81.8 19.7 %collective-permute-start.23 = (f32[128,256]{1,0:T(8,128)S(1)}, f32[128,256]{1,0:T(8,128)S(1)}, u32[]{:S(2)}, u32[]{:S(2)}) collective-permute-start(f32[128,256]{1,0:T(8,128)S(1)} %get-tuple-element.69), channel_id=1, source_target_pairs={{0,1},{1,0},{2,3},{3,2},{4,5},{5,4},{6,7},{7,6},{8,9},{9,8},{10,11... | collective-permute-start | bytes 393224 | tf_op jit(solution)/shard_map/ppermute | solution.py:76
  88.2 7.6 %collective-permute-start.10 = (bf16[16,3584]{1,0:T(8,128)(2,1)S(1)}, bf16[16,3584]{1,0:T(8,128)(2,1)S(1)}, u32[]{:S(2)}, u32[]{:S(2)}) collective-permute-start(bf16[16,3584]{1,0:T(8,128)(2,1)S(1)} %get-tuple-element.55), channel_id=1, source_target_pairs={{14,0},{15,1},{4,2},{5,3},{2,4},{3,5},{8,6},{9,7},{6,8},{7,9},{12,... | collective-permute-start | bytes 344072 | tf_op jit(solution)/shard_map/ppermute | solution.py:76
  92.1 6.9 %collective-permute-start.11 = (bf16[16,3584]{1,0:T(8,128)(2,1)S(1)}, bf16[16,3584]{1,0:T(8,128)(2,1)S(1)}, u32[]{:S(2)}, u32[]{:S(2)}) collective-permute-start(bf16[16,3584]{1,0:T(8,128)(2,1)S(1)} %get-tuple-element.56), channel_id=1, source_target_pairs={{10,0},{11,1},{8,2},{9,3},{14,4},{15,5},{12,6},{13,7},{2,8},{3,9},... | collective-permute-start | bytes 344072 | tf_op jit(solution)/shard_map/ppermute | solution.py:76
  93.0 5.9 %collective-permute-start.9 = (bf16[16,3584]{1,0:T(8,128)(2,1)S(1)}, bf16[16,3584]{1,0:T(8,128)(2,1)S(1)}, u32[]{:S(2)}, u32[]{:S(2)}) collective-permute-start(bf16[16,3584]{1,0:T(8,128)(2,1)S(1)} %get-tuple-element.54), channel_id=1, source_target_pairs={{4,0},{5,1},{14,2},{15,3},{8,4},{9,5},{2,6},{3,7},{12,8},{13,9},{6... | collective-permute-start | bytes 344072 | tf_op jit(solution)/shard_map/ppermute | solution.py:76
  99.0 6.5 %collective-permute-start.12 = (bf16[32,3584]{1,0:T(8,128)(2,1)S(1)}, bf16[32,3584]{1,0:T(8,128)(2,1)S(1)}, u32[]{:S(2)}, u32[]{:S(2)}) collective-permute-start(bf16[32,3584]{1,0:T(8,128)(2,1)S(1)} %get-tuple-element.58), channel_id=1, source_target_pairs={{0,17},{1,16},{2,19},{3,18},{4,21},{5,20},{6,23},{7,22},{8,25},{9,... | collective-permute-start | bytes 688136 | tf_op jit(solution)/shard_map/ppermute | solution.py:76
  102.9 2.6 %copy-start.3 = (bf16[1,128,3584]{2,1,0:T(8,128)(2,1)S(1)}, bf16[1,128,3584]{2,1,0:T(8,128)(2,1)}, u32[]{:S(2)}) copy-start(bf16[1,128,3584]{2,1,0:T(8,128)(2,1)} %param.10) | copy-start | bytes 2752516
  102.9 2.6 %copy-start.6 = (bf16[128,128]{1,0:T(8,128)(2,1)S(1)}, bf16[128,128]{1,0:T(8,128)(2,1)}, u32[]{:S(2)}) copy-start(bf16[128,128]{1,0:T(8,128)(2,1)} %get-tuple-element.44.refs_1_) | copy-start | bytes 98308
  102.9 14.5 %collective-permute-start.26 = (bf16[128,1792]{1,0:T(8,128)(2,1)S(1)}, bf16[128,1792]{1,0:T(8,128)(2,1)S(1)}, u32[]{:S(2)}, u32[]{:S(2)}) collective-permute-start(bf16[128,1792]{1,0:T(8,128)(2,1)S(1)} %get-tuple-element.77), channel_id=1, source_target_pairs={{0,2},{1,3},{2,0},{3,1},{4,6},{5,7},{6,4},{7,5},{8,10},{9,11},{10,... | collective-permute-start | bytes 1376264 | tf_op jit(solution)/shard_map/ppermute | solution.py:76
  103.7 14.5 %collective-permute-start.24 = (bf16[128,1792]{1,0:T(8,128)(2,1)S(1)}, bf16[128,1792]{1,0:T(8,128)(2,1)S(1)}, u32[]{:S(2)}, u32[]{:S(2)}) collective-permute-start(bf16[128,1792]{1,0:T(8,128)(2,1)S(1)} %get-tuple-element.73), channel_id=1, source_target_pairs={{0,1},{1,0},{2,3},{3,2},{4,5},{5,4},{6,7},{7,6},{8,9},{9,8},{10,11... | collective-permute-start | bytes 1376264 | tf_op jit(solution)/shard_map/ppermute | solution.py:76
  105.9 38.6 %collective-permute-start.13 = (bf16[128,3584]{1,0:T(8,128)(2,1)S(1)}, bf16[128,3584]{1,0:T(8,128)(2,1)S(1)}, u32[]{:S(2)}, u32[]{:S(2)}) collective-permute-start(bf16[128,3584]{1,0:T(8,128)(2,1)S(1)} %shard_map.120), channel_id=1, source_target_pairs={{0,32},{1,33},{2,34},{3,35},{4,36},{5,37},{6,38},{7,39},{8,40},{9,... | collective-permute-start | bytes 2752520 | tf_op jit(solution)/shard_map/ppermute | solution.py:87
  117.5 7.4 %collective-permute-start.27 = (bf16[64,1792]{1,0:T(8,128)(2,1)S(1)}, bf16[64,1792]{1,0:T(8,128)(2,1)S(1)}, u32[]{:S(2)}, u32[]{:S(2)}) collective-permute-start(bf16[64,1792]{1,0:T(8,128)(2,1)S(1)} %get-tuple-element.79), channel_id=1, source_target_pairs={{0,1},{1,0},{2,3},{3,2},{4,5},{5,4},{6,7},{7,6},{8,9},{9,8},{10,11... | collective-permute-start | bytes 688136 | tf_op jit(solution)/shard_map/ppermute | solution.py:76
  118.3 6.7 %collective-permute-start.25 = (bf16[64,1792]{1,0:T(8,128)(2,1)S(1)}, bf16[64,1792]{1,0:T(8,128)(2,1)S(1)}, u32[]{:S(2)}, u32[]{:S(2)}) collective-permute-start(bf16[64,1792]{1,0:T(8,128)(2,1)S(1)} %get-tuple-element.75), channel_id=1, source_target_pairs={{0,2},{1,3},{2,0},{3,1},{4,6},{5,7},{6,4},{7,5},{8,10},{9,11},{10,... | collective-permute-start | bytes 688136 | tf_op jit(solution)/shard_map/ppermute | solution.py:76
  125.0 4.6 %collective-permute-start.28 = (bf16[16,3584]{1,0:T(8,128)(2,1)S(1)}, bf16[16,3584]{1,0:T(8,128)(2,1)S(1)}, u32[]{:S(2)}, u32[]{:S(2)}) collective-permute-start(bf16[16,3584]{1,0:T(8,128)(2,1)S(1)} %get-tuple-element.81), channel_id=1, source_target_pairs={{4,0},{5,1},{14,2},{15,3},{8,4},{9,5},{2,6},{3,7},{12,8},{13,9},{6... | collective-permute-start | bytes 344072 | tf_op jit(solution)/shard_map/ppermute | solution.py:76
  125.7 4.9 %collective-permute-start.29 = (bf16[16,3584]{1,0:T(8,128)(2,1)S(1)}, bf16[16,3584]{1,0:T(8,128)(2,1)S(1)}, u32[]{:S(2)}, u32[]{:S(2)}) collective-permute-start(bf16[16,3584]{1,0:T(8,128)(2,1)S(1)} %get-tuple-element.82), channel_id=1, source_target_pairs={{14,0},{15,1},{4,2},{5,3},{2,4},{3,5},{8,6},{9,7},{6,8},{7,9},{12,... | collective-permute-start | bytes 344072 | tf_op jit(solution)/shard_map/ppermute | solution.py:76
  127.0 6.8 %collective-permute-start.30 = (bf16[16,3584]{1,0:T(8,128)(2,1)S(1)}, bf16[16,3584]{1,0:T(8,128)(2,1)S(1)}, u32[]{:S(2)}, u32[]{:S(2)}) collective-permute-start(bf16[16,3584]{1,0:T(8,128)(2,1)S(1)} %get-tuple-element.83), channel_id=1, source_target_pairs={{10,0},{11,1},{8,2},{9,3},{14,4},{15,5},{12,6},{13,7},{2,8},{3,9},... | collective-permute-start | bytes 344072 | tf_op jit(solution)/shard_map/ppermute | solution.py:76
  133.8 14.3 %collective-permute-start.31 = (bf16[32,3584]{1,0:T(8,128)(2,1)S(1)}, bf16[32,3584]{1,0:T(8,128)(2,1)S(1)}, u32[]{:S(2)}, u32[]{:S(2)}) collective-permute-start(bf16[32,3584]{1,0:T(8,128)(2,1)S(1)} %get-tuple-element.84), channel_id=1, source_target_pairs={{32,0},{33,1},{34,2},{35,3},{36,4},{37,5},{38,6},{39,7},{40,8},{41... | collective-permute-start | bytes 688136 | tf_op jit(solution)/shard_map/ppermute | solution.py:87
  142.5 11.7 %collective-permute-start.32 = (bf16[32,3584]{1,0:T(8,128)(2,1)S(1)}, bf16[32,3584]{1,0:T(8,128)(2,1)S(1)}, u32[]{:S(2)}, u32[]{:S(2)}) collective-permute-start(bf16[32,3584]{1,0:T(8,128)(2,1)S(1)} %get-tuple-element.85), channel_id=1, source_target_pairs={{32,17},{33,16},{34,19},{35,18},{36,21},{37,20},{38,23},{39,22},{4... | collective-permute-start | bytes 688136 | tf_op jit(solution)/shard_map/ppermute | solution.py:87

commit v3 on v2

--- a/solution.py
+++ b/solution.py
@@ -196,17 +196,15 @@
 
 
 def grads_body(
-    rows_ref, wg_ref, wu_ref, sg_ref, su_ref, mine_ref, got_ref, gg_ref, gu_ref
+    sg_ref, su_ref, sgx_ref, sux_ref, mine_ref, got_ref, gg_ref, gu_ref
 ):
-    rows = rows_ref[...]
-    count = rows.shape[0]
-    sgx, sux = slopes(rows, wg_ref, wu_ref)
     mine = mine_ref[...]
     got = got_ref[...]
+    count = mine.shape[0]
     gg_ref[:count] = (mine * sg_ref[...]).astype(BF16)
-    gg_ref[count:] = (got * sgx).astype(BF16)
+    gg_ref[count:] = (got * sgx_ref[...]).astype(BF16)
     gu_ref[:count] = (mine * su_ref[...]).astype(BF16)
-    gu_ref[count:] = (got * sux).astype(BF16)
+    gu_ref[count:] = (got * sux_ref[...]).astype(BF16)
 
 
 def back_x_body(gg_ref, gu_ref, wg_ref, wu_ref, keep_ref, send_ref):
@@ -234,6 +232,11 @@
     rows = jnp.concatenate([own_ref[...], far_ref[...]], axis=0)
     total = dot(comb_ref[...], jnp.concatenate([rows, rows], axis=0))
     out_ref[...] = (base_ref[...].astype(F32) + total).astype(BF16)
+
+
+def marked_body(base_ref, comb_ref, own_ref, far_ref, out_ref, mark_ref):
+    combine_body(base_ref, comb_ref, own_ref, far_ref, out_ref)
+    mark_ref[...] = jnp.zeros_like(mark_ref)
 
 
 def back_call(body, gg, gu, wg, wu, index, chunks):
@@ -291,28 +294,29 @@
         smem=(0,),
         limit=60,
     )
+    got = move(far, ACROSS_XHI)
     bown, bfar, bcomb = call(
         pack_body,
         [shape(2 * HALF, width)] * 2 + [table],
         [where, bwd_ids[0].T, bwd_score[0].T, bwd_in[0], bwd_cot[0]],
         smem=(0,),
         limit=60,
-        after=(far,),
-    )
-    bbase = relay(bwd_cot[0], STAY, -1)
-    bcomb = relay(bcomb, STAY, -1)
-    blocks = call(weave_body, [shape(BLOCK, width)] * PAIRS, [own, move(far, ACROSS_XHI)])
+        after=(got,),
+    )
+    blocks = call(weave_body, [shape(BLOCK, width)] * PAIRS, [own, got])
     fy = jnp.concatenate(shifts(blocks, False), axis=0)
     bblocks = call(
         weave_body,
         [shape(2 * BLOCK, width)] * PAIRS,
         [bown, move(bfar, ACROSS_XHI)],
-        after=(fy, bcomb),
+        after=(fy,),
     )
     fy = jnp.concatenate([fy, move(fy, Z_PAIR)], axis=0)
     fyx = move(fy, DP_PAIR)
     (mine,) = call(hidden_body, [shape(rows, hid)], [fy, wg, wu], proj)
 
+    bbase = relay(join([bwd_cot[0]], after=(mine,)), STAY, -1)
+    bcomb = relay(join([bcomb], after=(mine,)), STAY, -1)
     parts = shifts(bblocks, False)
     by = jnp.concatenate([p[:BLOCK] for p in parts], axis=0)
     cy = jnp.concatenate([p[BLOCK:] for p in parts], axis=0)
@@ -326,19 +330,26 @@
     keep, send = call(
         down_body, [shape(HOME, width, F32), shape(HOME, width)], [mine, theirs, wd, wdp], proj
     )
-    blocks = call(finish_body, [shape(BLOCK, width)] * PAIRS, [keep, move(send, Z_PAIR)])
-    own, far = call(part_body, [shape(HALF, width)] * 2, shifts(blocks, True))
-    far = move(far, ACROSS_XHI)
-    (fwd_out,) = call(combine_body, [shape(tokens, width)], [fwd_in[0], fcomb, own, far])
-    fwd_out = relay(fwd_out, STAY, 1)
-
+    fgot = move(send, Z_PAIR)
+    blocks = call(finish_body, [shape(BLOCK, width)] * PAIRS, [keep, fgot])
+    fin = blocks[0]
+    blocks = shifts(blocks, True)
     sg, su = call(
-        slope_body, [shape(rows, hid, F32)] * 2, [by, wg, wu], proj, after=(bbase,)
+        slope_body, [shape(rows, hid, F32)] * 2, [by, wg, wu], proj, after=(bcomb,)
     )
     gh, gh_send = call(grad_hidden_body, [shape(rows, hid, F32)] * 2, [cy, wd, wdp], proj)
     gh_got = move(gh_send, DP_PAIR)
+    fbase = relay(join([fwd_in[0]], after=(gh_send,)), STAY, 1)
+    fcomb = relay(join([fcomb], after=(gh_send,)), STAY, 1)
+    sgx, sux = call(
+        slope_body,
+        [shape(rows, hid, F32)] * 2,
+        [byx, wg, wu],
+        proj,
+        after=(fin, bbase, fcomb),
+    )
     gg, gu = call(
-        grads_body, [shape(2 * rows, hid)] * 2, [byx, wg, wu, sg, su, gh, gh_got], proj
+        grads_body, [shape(2 * rows, hid)] * 2, [sg, su, sgx, sux, gh, gh_got]
     )
     half = width // 2
     fold = [shape(HOME, half, F32), shape(HOME, half)]
@@ -347,13 +358,28 @@
     xgot, zgot = move(xsend, DP_PAIR), move(zsend, Z_PAIR)
     xkeep, xsend = call(fold_body, fold, [xkeep, xgot])
     zkeep, zsend = call(fold_body, fold, [zkeep, zgot])
+    own, far = call(
+        part_body, [shape(HALF, width)] * 2, blocks, after=(xsend, zsend)
+    )
+    own, far = relay(own, STAY, 1), relay(far, ACROSS_XHI, 1)
+    fwd_out, mark = call(
+        marked_body,
+        [shape(tokens, width), shape(8, 128, F32)],
+        [fbase, fcomb, own, far],
+    )
+    bbase = join([bbase], after=(xkeep, zkeep))
     xgot, zgot = move(xsend, Z_PAIR), move(zsend, DP_PAIR)
     blocks = call(
         finish_body, [shape(BLOCK, width)] * PAIRS, [xkeep, xgot, zkeep, zgot]
     )
     own, far = call(part_body, [shape(HALF, width)] * 2, shifts(blocks, True))
     own, far = relay(own, STAY, -1), relay(far, ACROSS_XHI, -1)
-    (bwd_out,) = call(combine_body, [shape(tokens, width)], [bbase, bcomb, own, far])
+    (bwd_out,) = call(
+        combine_body,
+        [shape(tokens, width)],
+        [bbase, bcomb, own, far],
+        after=(mark,),
+    )
     return fwd_out[None], bwd_out[None]
 
 

time: 157 us -> 153 us (0.975)
  waiting for transfers between devices: 63.8 us -> 47.2 us
  starting transfers between devices: 76.7 us -> 86.2 us
  Pallas kernels: 13.7 us -> 15.8 us
    ppermute x28 -> x27, waiting for transfers between devices: 54 us -> 36.8 us  [move(): return lax.ppermute(value, ('expert', 'dp'), pairs)]
    ppermute x5 -> x8, starting transfers between devices: 31.6 us -> 40.9 us  [relay(): return lax.ppermute(value, ('pipe', 'expert', 'dp'), full)]
    pallas_call x19 -> x25, Pallas kernels: 12.3 us -> 14.5 us  [call(): pl.pallas_call(run, out_shape=tuple(outs), in_specs=specs, out_specs=tupl...]
    ppermute x5 -> x8, waiting for transfers between devices: 9.76 us -> 10.3 us  [relay(): return lax.ppermute(value, ('pipe', 'expert', 'dp'), full)]
    ppermute x28 -> x27, starting transfers between devices: 45.1 us -> 45.3 us  [move(): return lax.ppermute(value, ('expert', 'dp'), pairs)]
  transfers between devices with their start and end apart: 33 -> 35, of which waited for: 15 -> 12; matrix products, arithmetic and copies ran while one was open for 0% -> 0% of each run, Pallas kernels for 6% -> 7%
where the time goes in v3:
time: 153 us
  starting transfers between devices  86.2 us (56%)
  waiting for transfers between devices  47.2 us (31%)
  Pallas kernels  15.8 us (10%)
  local copies, waits for them, and re-layouts  2.31 us (2%)
    ppermute x27, starting transfers between devices, move(): return lax.ppermute(value, ('expert', 'dp'), pairs)  45.3 us
    ppermute x8, starting transfers between devices, relay(): return lax.ppermute(value, ('pipe', 'expert', 'dp'), full)  40.9 us
    ppermute x27, waiting for transfers between devices, move(): return lax.ppermute(value, ('expert', 'dp'), pairs)  36.8 us
    pallas_call x25, Pallas kernels, call(): pl.pallas_call(run, out_shape=tuple(outs), in_specs=specs, out_specs=tupl...  14.5 us
    ppermute x8, waiting for transfers between devices, relay(): return lax.ppermute(value, ('pipe', 'expert', 'dp'), full)  10.3 us
  transfers between devices with their start and end apart: 35, of which 12 were waited for; matrix products, arithmetic and copies ran while one was open for 0% of the time, Pallas kernels for 7%

profile of v3, /device:TPU:1, one launch (start us, length us, event | category | flops | bytes accessed | tf_op | source)
XLA Modules:
  0.0 152.7 jit_solution(7234996208556800037)
XLA Ops:
  0.6 2.4 %shard_map.113 = (bf16[32,3584]{1,0:T(8,128)(2,1)}, bf16[32,3584]{1,0:T(8,128)(2,1)}, bf16[128,128]{1,0:T(8,128)(2,1)}) custom-call(s32[1]{0:T(128)} %bitcast.1.refs_0_, s32[8,128]{1,0:T(8,128)} %bitcast.42, f32[8,128]{1,0:T(8,128)} %bitcast.43, bf16[128,3584]{1,0:T(8,128)(2,1)} %bitcast.38), custom_call_target="tpu_custom_call" | custom-call | bytes 1417220 | tf_op jit(solution)/shard_map/pallas_call | solution.py:30
  3.0 3.3 %collective-permute-start = (bf16[32,3584]{1,0:T(8,128)(2,1)}, bf16[32,3584]{1,0:T(8,128)(2,1)S(1)}, u32[]{:S(2)}, u32[]{:S(2)}) collective-permute-start(bf16[32,3584]{1,0:T(8,128)(2,1)} %get-tuple-element.48), channel_id=1, source_target_pairs={{0,17},{1,16},{2,19},{3,18},{4,21},{5,20},{6,23},{7,22},{8,25},{9,... | collective-permute-start | bytes 688136 | tf_op jit(solution)/shard_map/ppermute | solution.py:76
  6.3 4.6 %collective-permute-done.refs_5_.refs_1_ = bf16[32,3584]{1,0:T(8,128)(2,1)S(1)} collective-permute-done((bf16[32,3584]{1,0:T(8,128)(2,1)}, bf16[32,3584]{1,0:T(8,128)(2,1)S(1)}, u32[]{:S(2)}, u32[]{:S(2)}) %collective-permute-start) | collective-permute-done | bytes 229408 | tf_op jit(solution)/shard_map/ppermute | solution.py:76
  10.9 1.0 copy-done.7
  12.0 3.9 %collective-permute-start.2 = (bf16[16,3584]{1,0:T(8,128)(2,1)S(1)}, bf16[16,3584]{1,0:T(8,128)(2,1)S(1)}, u32[]{:S(2)}, u32[]{:S(2)}) collective-permute-start(bf16[16,3584]{1,0:T(8,128)(2,1)S(1)} %get-tuple-element.53), channel_id=1, source_target_pairs={{0,4},{1,5},{2,14},{3,15},{4,8},{5,9},{6,2},{7,3},{8,12},{9,13},{1... | collective-permute-start | bytes 344072 | tf_op jit(solution)/shard_map/ppermute | solution.py:76
  15.9 3.8 %collective-permute-start.3 = (bf16[16,3584]{1,0:T(8,128)(2,1)S(1)}, bf16[16,3584]{1,0:T(8,128)(2,1)S(1)}, u32[]{:S(2)}, u32[]{:S(2)}) collective-permute-start(bf16[16,3584]{1,0:T(8,128)(2,1)S(1)} %get-tuple-element.54), channel_id=1, source_target_pairs={{0,14},{1,15},{2,4},{3,5},{4,2},{5,3},{6,8},{7,9},{8,6},{9,7},{10,... | collective-permute-start | bytes 344072 | tf_op jit(solution)/shard_map/ppermute | solution.py:76
  20.2 3.0 %shard_map.114 = (bf16[64,3584]{1,0:T(8,128)(2,1)}, bf16[64,3584]{1,0:T(8,128)(2,1)}, bf16[128,128]{1,0:T(8,128)(2,1)}) custom-call(s32[1]{0:T(128)} %bitcast.1.refs_0_, s32[8,128]{1,0:T(8,128)} %bitcast.44, f32[8,128]{1,0:T(8,128)} %bitcast.45, bf16[128,3584]{1,0:T(8,128)(2,1)} %bitcast.40, bf16[128,3584]{1,0:T(8,128)(2,1)} %bitcast.36, ...), custom_call_target="tpu_custom_call" | custom-call | bytes 2793476 | tf_op jit(solution)/shard_map/pallas_call | solution.py:30
  23.2 2.5 %collective-permute-start.1 = (bf16[64,3584]{1,0:T(8,128)(2,1)}, bf16[64,3584]{1,0:T(8,128)(2,1)S(1)}, u32[]{:S(2)}, u32[]{:S(2)}) collective-permute-start(bf16[64,3584]{1,0:T(8,128)(2,1)} %get-tuple-element.50), channel_id=1, source_target_pairs={{0,17},{1,16},{2,19},{3,18},{4,21},{5,20},{6,23},{7,22},{8,25},{9,... | collective-permute-start | bytes 1376264 | tf_op jit(solution)/shard_map/ppermute | solution.py:76
  25.7 3.1 %collective-permute-done.4 = bf16[16,3584]{1,0:T(8,128)(2,1)S(1)} collective-permute-done((bf16[16,3584]{1,0:T(8,128)(2,1)S(1)}, bf16[16,3584]{1,0:T(8,128)(2,1)S(1)}, u32[]{:S(2)}, u32[]{:S(2)}) %collective-permute-start.4) | collective-permute-done | bytes 114720 | tf_op jit(solution)/shard_map/ppermute | solution.py:76
  28.8 2.1 %collective-permute-start.12 = (bf16[64,3584]{1,0:T(8,128)(2,1)S(1)}, bf16[64,3584]{1,0:T(8,128)(2,1)S(1)}, u32[]{:S(2)}, u32[]{:S(2)}) collective-permute-start(bf16[64,3584]{1,0:T(8,128)(2,1)S(1)} %get-tuple-element.107.refs_2_), channel_id=1, source_target_pairs={{0,2},{1,3},{2,0},{3,1},{4,6},{5,7},{6,4},{7,5},{8,10},{9,11},{10,... | collective-permute-start | bytes 1376264 | tf_op jit(solution)/shard_map/ppermute | solution.py:76
  31.0 3.5 %collective-permute-done.1.refs_1_ = bf16[64,3584]{1,0:T(8,128)(2,1)S(1)} collective-permute-done((bf16[64,3584]{1,0:T(8,128)(2,1)}, bf16[64,3584]{1,0:T(8,128)(2,1)S(1)}, u32[]{:S(2)}, u32[]{:S(2)}) %collective-permute-start.1) | collective-permute-done | bytes 458784 | tf_op jit(solution)/shard_map/ppermute | solution.py:76
  34.5 1.0 copy-done.6
  35.6 1.6 %collective-permute-start.5 = (bf16[32,3584]{1,0:T(8,128)(2,1)S(1)}, bf16[32,3584]{1,0:T(8,128)(2,1)S(1)}, u32[]{:S(2)}, u32[]{:S(2)}) collective-permute-start(bf16[32,3584]{1,0:T(8,128)(2,1)S(1)} %get-tuple-element.57), channel_id=1, source_target_pairs={{0,4},{1,5},{2,14},{3,15},{4,8},{5,9},{6,2},{7,3},{8,12},{9,13},{1... | collective-permute-start | bytes 688136 | tf_op jit(solution)/shard_map/ppermute | solution.py:76
  37.2 2.4 %collective-permute-start.6 = (bf16[32,3584]{1,0:T(8,128)(2,1)S(1)}, bf16[32,3584]{1,0:T(8,128)(2,1)S(1)}, u32[]{:S(2)}, u32[]{:S(2)}) collective-permute-start(bf16[32,3584]{1,0:T(8,128)(2,1)S(1)} %get-tuple-element.58), channel_id=1, source_target_pairs={{0,14},{1,15},{2,4},{3,5},{4,2},{5,3},{6,8},{7,9},{8,6},{9,7},{10,... | collective-permute-start | bytes 688136 | tf_op jit(solution)/shard_map/ppermute | solution.py:76
  39.6 0.8 collective-permute-start.7
  40.6 8.3 %collective-permute-done.5 = bf16[32,3584]{1,0:T(8,128)(2,1)S(1)} collective-permute-done((bf16[32,3584]{1,0:T(8,128)(2,1)S(1)}, bf16[32,3584]{1,0:T(8,128)(2,1)S(1)}, u32[]{:S(2)}, u32[]{:S(2)}) %collective-permute-start.5) | collective-permute-done | bytes 229408 | tf_op jit(solution)/shard_map/ppermute | solution.py:76
  49.0 9.2 %collective-permute-done.7 = bf16[32,3584]{1,0:T(8,128)(2,1)S(1)} collective-permute-done((bf16[32,3584]{1,0:T(8,128)(2,1)S(1)}, bf16[32,3584]{1,0:T(8,128)(2,1)S(1)}, u32[]{:S(2)}, u32[]{:S(2)}) %collective-permute-start.7) | collective-permute-done | bytes 229408 | tf_op jit(solution)/shard_map/ppermute | solution.py:76
  58.4 1.5 %collective-permute-start.8 = (bf16[64,3584]{1,0:T(8,128)(2,1)S(1)}, bf16[64,3584]{1,0:T(8,128)(2,1)S(1)}, u32[]{:S(2)}, u32[]{:S(2)}) collective-permute-start(bf16[64,3584]{1,0:T(8,128)(2,1)S(1)} %pad_maximum_fusion), channel_id=1, source_target_pairs={{0,2},{1,3},{2,0},{3,1},{4,6},{5,7},{6,4},{7,5},{8,10},{9,11},{10,... | collective-permute-start | bytes 1376264 | tf_op jit(solution)/shard_map/ppermute | solution.py:76
  60.6 6.1 %collective-permute-done.13.refs_0_ = bf16[128,3584]{1,0:T(8,128)(2,1)S(1)} collective-permute-done((bf16[128,3584]{1,0:T(8,128)(2,1)S(1)}, bf16[128,3584]{1,0:T(8,128)(2,1)S(1)}, u32[]{:S(2)}, u32[]{:S(2)}) %collective-permute-start.13) | collective-permute-done | bytes 917536 | tf_op jit(solution)/shard_map/ppermute | solution.py:76
  66.8 0.7 shard_map.121
  67.7 4.1 %collective-permute-start.22 = (bf16[128,3584]{1,0:T(8,128)(2,1)S(1)}, bf16[128,3584]{1,0:T(8,128)(2,1)S(1)}, u32[]{:S(2)}, u32[]{:S(2)}) collective-permute-start(bf16[128,3584]{1,0:T(8,128)(2,1)S(1)} %shard_map.127), channel_id=1, source_target_pairs={{32,0},{33,1},{34,2},{35,3},{36,4},{37,5},{38,6},{39,7},{40,8},{41... | collective-permute-start | bytes 2752520 | tf_op jit(solution)/shard_map/ppermute | solution.py:87
  71.9 1.4 collective-permute-start.21
  74.0 1.9 %collective-permute-start.15 = (bf16[64,3584]{1,0:T(8,128)(2,1)S(1)}, bf16[64,3584]{1,0:T(8,128)(2,1)S(1)}, u32[]{:S(2)}, u32[]{:S(2)}) collective-permute-start(bf16[64,3584]{1,0:T(8,128)(2,1)S(1)} %get-tuple-element.63), channel_id=1, source_target_pairs={{0,2},{1,3},{2,0},{3,1},{4,6},{5,7},{6,4},{7,5},{8,10},{9,11},{10,... | collective-permute-start | bytes 1376264 | tf_op jit(solution)/shard_map/ppermute | solution.py:76
  75.9 1.2 collective-permute-done.8
  77.1 1.3 shard_map.117
  78.5 9.6 %collective-permute-start.20 = (bf16[128,128]{1,0:T(8,128)(2,1)S(1)}, bf16[128,128]{1,0:T(8,128)(2,1)S(1)}, u32[]{:S(2)}, u32[]{:S(2)}) collective-permute-start(bf16[128,128]{1,0:T(8,128)(2,1)S(1)} %shard_map.125), channel_id=1, source_target_pairs={{32,0},{33,1},{34,2},{35,3},{36,4},{37,5},{38,6},{39,7},{40,8},{41... | collective-permute-start | bytes 98312 | tf_op jit(solution)/shard_map/ppermute | solution.py:87
  88.1 3.1 %collective-permute-done.20.refs_3_.refs_1_ = bf16[128,128]{1,0:T(8,128)(2,1)S(1)} collective-permute-done((bf16[128,128]{1,0:T(8,128)(2,1)S(1)}, bf16[128,128]{1,0:T(8,128)(2,1)S(1)}, u32[]{:S(2)}, u32[]{:S(2)}) %collective-permute-start.20) | collective-permute-done | bytes 32800 | tf_op jit(solution)/shard_map/ppermute | solution.py:87
  91.3 1.9 %collective-permute-start.11 = (bf16[128,128]{1,0:T(8,128)(2,1)S(1)}, bf16[128,128]{1,0:T(8,128)(2,1)S(1)}, u32[]{:S(2)}, u32[]{:S(2)}) collective-permute-start(bf16[128,128]{1,0:T(8,128)(2,1)S(1)} %shard_map.119), channel_id=1, source_target_pairs={{0,32},{1,33},{2,34},{3,35},{4,36},{5,37},{6,38},{7,39},{8,40},{9,... | collective-permute-start | bytes 98312 | tf_op jit(solution)/shard_map/ppermute | solution.py:87
  93.2 0.7 shard_map.126
  94.3 1.8 %shard_map.128 = (f32[128,256]{1,0:T(8,128)S(1)}, f32[128,256]{1,0:T(8,128)S(1)}) custom-call(bf16[128,3584]{1,0:T(8,128)(2,1)} %collective-permute-done.21.refs_0_, bf16[3584,256]{1,0:T(8,128)(2,1)S(1)} %bitcast.24, bf16[3584,256]{1,0:T(8,128)(2,1)S(1)} %bitcast.30, bf16[16,3584]{1,0:T(8,128)(2,1)S(1)} %get-tuple-element.64.refs_3_.refs_0_, ...), custom_call_target="tpu_custom_call" | custom-call | flops 469762048 | bytes 4849664 | tf_op jit(solution)/shard_map/pallas_call | solution.py:30
  96.3 0.7 shard_map.132
  97.1 0.7 shard_map.130
  97.7 1.9 %collective-permute-start.24 = (bf16[128,1792]{1,0:T(8,128)(2,1)S(1)}, bf16[128,1792]{1,0:T(8,128)(2,1)S(1)}, u32[]{:S(2)}, u32[]{:S(2)}) collective-permute-start(bf16[128,1792]{1,0:T(8,128)(2,1)S(1)} %get-tuple-element.77), channel_id=1, source_target_pairs={{0,1},{1,0},{2,3},{3,2},{4,5},{5,4},{6,7},{7,6},{8,9},{9,8},{10,11... | collective-permute-start | bytes 1376264 | tf_op jit(solution)/shard_map/ppermute | solution.py:76
  99.7 6.7 %collective-permute-start.10 = (bf16[128,3584]{1,0:T(8,128)(2,1)S(1)}, bf16[128,3584]{1,0:T(8,128)(2,1)S(1)}, u32[]{:S(2)}, u32[]{:S(2)}) collective-permute-start(bf16[128,3584]{1,0:T(8,128)(2,1)S(1)} %shard_map.118), channel_id=1, source_target_pairs={{0,32},{1,33},{2,34},{3,35},{4,36},{5,37},{6,38},{7,39},{8,40},{9,... | collective-permute-start | bytes 2752520 | tf_op jit(solution)/shard_map/ppermute | solution.py:87
  106.4 0.7 collective-permute-done.25.refs_1_
  107.2 2.2 %collective-permute-start.29 = (bf16[64,1792]{1,0:T(8,128)(2,1)S(1)}, bf16[64,1792]{1,0:T(8,128)(2,1)S(1)}, u32[]{:S(2)}, u32[]{:S(2)}) collective-permute-start(bf16[64,1792]{1,0:T(8,128)(2,1)S(1)} %get-tuple-element.81.refs_5_), channel_id=1, source_target_pairs={{0,1},{1,0},{2,3},{3,2},{4,5},{5,4},{6,7},{7,6},{8,9},{9,8},{10,11... | collective-permute-start | bytes 688136 | tf_op jit(solution)/shard_map/ppermute | solution.py:76
  109.7 6.2 %collective-permute-start.16 = (bf16[16,3584]{1,0:T(8,128)(2,1)S(1)}, bf16[16,3584]{1,0:T(8,128)(2,1)S(1)}, u32[]{:S(2)}, u32[]{:S(2)}) collective-permute-start(bf16[16,3584]{1,0:T(8,128)(2,1)S(1)} %get-tuple-element.65), channel_id=1, source_target_pairs={{4,0},{5,1},{14,2},{15,3},{8,4},{9,5},{2,6},{3,7},{12,8},{13,9},{6... | collective-permute-start | bytes 344072 | tf_op jit(solution)/shard_map/ppermute | solution.py:76
  116.0 4.3 %collective-permute-start.18 = (bf16[16,3584]{1,0:T(8,128)(2,1)S(1)}, bf16[16,3584]{1,0:T(8,128)(2,1)S(1)}, u32[]{:S(2)}, u32[]{:S(2)}) collective-permute-start(bf16[16,3584]{1,0:T(8,128)(2,1)S(1)} %get-tuple-element.67), channel_id=1, source_target_pairs={{10,0},{11,1},{8,2},{9,3},{14,4},{15,5},{12,6},{13,7},{2,8},{3,9},... | collective-permute-start | bytes 344072 | tf_op jit(solution)/shard_map/ppermute | solution.py:76
  120.7 2.9 %collective-permute-start.31 = (bf16[16,3584]{1,0:T(8,128)(2,1)S(1)}, bf16[16,3584]{1,0:T(8,128)(2,1)S(1)}, u32[]{:S(2)}, u32[]{:S(2)}) collective-permute-start(bf16[16,3584]{1,0:T(8,128)(2,1)S(1)} %get-tuple-element.89), channel_id=1, source_target_pairs={{14,0},{15,1},{4,2},{5,3},{2,4},{3,5},{8,6},{9,7},{6,8},{7,9},{12,... | collective-permute-start | bytes 344072 | tf_op jit(solution)/shard_map/ppermute | solution.py:76
  123.6 0.9 collective-permute-start.32
  124.5 9.3 %collective-permute-start.26 = (bf16[32,3584]{1,0:T(8,128)(2,1)S(1)}, bf16[32,3584]{1,0:T(8,128)(2,1)S(1)}, u32[]{:S(2)}, u32[]{:S(2)}) collective-permute-start(bf16[32,3584]{1,0:T(8,128)(2,1)S(1)} %get-tuple-element.82), channel_id=1, source_target_pairs={{0,32},{1,33},{2,34},{3,35},{4,36},{5,37},{6,38},{7,39},{8,40},{9,... | collective-permute-start | bytes 688136 | tf_op jit(solution)/shard_map/ppermute | solution.py:87
  133.8 3.7 %collective-permute-start.27 = (bf16[32,3584]{1,0:T(8,128)(2,1)S(1)}, bf16[32,3584]{1,0:T(8,128)(2,1)S(1)}, u32[]{:S(2)}, u32[]{:S(2)}) collective-permute-start(bf16[32,3584]{1,0:T(8,128)(2,1)S(1)} %get-tuple-element.83), channel_id=1, source_target_pairs={{0,49},{1,48},{2,51},{3,50},{4,53},{5,52},{6,55},{7,54},{8,57},{9,... | collective-permute-start | bytes 688136 | tf_op jit(solution)/shard_map/ppermute | solution.py:87
  137.6 2.6 %collective-permute-start.33 = (bf16[32,3584]{1,0:T(8,128)(2,1)S(1)}, bf16[32,3584]{1,0:T(8,128)(2,1)S(1)}, u32[]{:S(2)}, u32[]{:S(2)}) collective-permute-start(bf16[32,3584]{1,0:T(8,128)(2,1)S(1)} %get-tuple-element.91), channel_id=1, source_target_pairs={{32,0},{33,1},{34,2},{35,3},{36,4},{37,5},{38,6},{39,7},{40,8},{41... | collective-permute-start | bytes 688136 | tf_op jit(solution)/shard_map/ppermute | solution.py:87
  140.1 3.0 %collective-permute-start.34 = (bf16[32,3584]{1,0:T(8,128)(2,1)S(1)}, bf16[32,3584]{1,0:T(8,128)(2,1)S(1)}, u32[]{:S(2)}, u32[]{:S(2)}) collective-permute-start(bf16[32,3584]{1,0:T(8,128)(2,1)S(1)} %get-tuple-element.92), channel_id=1, source_target_pairs={{32,17},{33,16},{34,19},{35,18},{36,21},{37,20},{38,23},{39,22},{4... | collective-permute-start | bytes 688136 | tf_op jit(solution)/shard_map/ppermute | solution.py:87
  143.3 1.2 collective-permute-done.27.refs_3_
  144.5 1.3 shard_map.135
  145.8 5.6 %collective-permute-done.34.refs_3_ = bf16[32,3584]{1,0:T(8,128)(2,1)S(1)} collective-permute-done((bf16[32,3584]{1,0:T(8,128)(2,1)S(1)}, bf16[32,3584]{1,0:T(8,128)(2,1)S(1)}, u32[]{:S(2)}, u32[]{:S(2)}) %collective-permute-start.34) | collective-permute-done | bytes 229408 | tf_op jit(solution)/shard_map/ppermute | solution.py:87
  151.4 1.3 shard_map.139
  (81 shorter events, 4.5 us)
Async XLA Ops:
  3.0 7.9 %collective-permute-start = (bf16[32,3584]{1,0:T(8,128)(2,1)}, bf16[32,3584]{1,0:T(8,128)(2,1)S(1)}, u32[]{:S(2)}, u32[]{:S(2)}) collective-permute-start(bf16[32,3584]{1,0:T(8,128)(2,1)} %get-tuple-element.48), channel_id=1, source_target_pairs={{0,17},{1,16},{2,19},{3,18},{4,21},{5,20},{6,23},{7,22},{8,25},{9,... | collective-permute-start | bytes 688136 | tf_op jit(solution)/shard_map/ppermute | solution.py:76
  6.3 67.0 %collective-permute-start.9 = (bf16[256,3584]{1,0:T(8,128)(2,1)}, bf16[256,3584]{1,0:T(8,128)(2,1)S(1)}, u32[]{:S(2)}, u32[]{:S(2)}) collective-permute-start(bf16[256,3584]{1,0:T(8,128)(2,1)} %bitcast.33), channel_id=1, source_target_pairs={{0,1},{1,0},{2,3},{3,2},{4,5},{5,4},{6,7},{7,6},{8,9},{9,8},{10,11... | collective-permute-start | bytes 5505032 | tf_op jit(solution)/shard_map/ppermute | solution.py:76
  10.9 9.3 %copy-start.5 = (bf16[32,3584]{1,0:T(8,128)(2,1)}, bf16[32,3584]{1,0:T(8,128)(2,1)S(1)}, u32[]{:S(2)}) copy-start(bf16[32,3584]{1,0:T(8,128)(2,1)S(1)} %collective-permute-done.refs_5_.refs_1_) | copy-start | bytes 688132
  10.9 1.0 copy-start.7
  12.0 13.7 %collective-permute-start.2 = (bf16[16,3584]{1,0:T(8,128)(2,1)S(1)}, bf16[16,3584]{1,0:T(8,128)(2,1)S(1)}, u32[]{:S(2)}, u32[]{:S(2)}) collective-permute-start(bf16[16,3584]{1,0:T(8,128)(2,1)S(1)} %get-tuple-element.53), channel_id=1, source_target_pairs={{0,4},{1,5},{2,14},{3,15},{4,8},{5,9},{6,2},{7,3},{8,12},{9,13},{1... | collective-permute-start | bytes 344072 | tf_op jit(solution)/shard_map/ppermute | solution.py:76
  15.9 9.8 %collective-permute-start.3 = (bf16[16,3584]{1,0:T(8,128)(2,1)S(1)}, bf16[16,3584]{1,0:T(8,128)(2,1)S(1)}, u32[]{:S(2)}, u32[]{:S(2)}) collective-permute-start(bf16[16,3584]{1,0:T(8,128)(2,1)S(1)} %get-tuple-element.54), channel_id=1, source_target_pairs={{0,14},{1,15},{2,4},{3,5},{4,2},{5,3},{6,8},{7,9},{8,6},{9,7},{10,... | collective-permute-start | bytes 344072 | tf_op jit(solution)/shard_map/ppermute | solution.py:76
  19.6 9.2 %collective-permute-start.4 = (bf16[16,3584]{1,0:T(8,128)(2,1)S(1)}, bf16[16,3584]{1,0:T(8,128)(2,1)S(1)}, u32[]{:S(2)}, u32[]{:S(2)}) collective-permute-start(bf16[16,3584]{1,0:T(8,128)(2,1)S(1)} %get-tuple-element.55), channel_id=1, source_target_pairs={{0,10},{1,11},{2,8},{3,9},{4,14},{5,15},{6,12},{7,13},{8,2},{9,3},... | collective-permute-start | bytes 344072 | tf_op jit(solution)/shard_map/ppermute | solution.py:76
  23.2 11.3 %collective-permute-start.1 = (bf16[64,3584]{1,0:T(8,128)(2,1)}, bf16[64,3584]{1,0:T(8,128)(2,1)S(1)}, u32[]{:S(2)}, u32[]{:S(2)}) collective-permute-start(bf16[64,3584]{1,0:T(8,128)(2,1)} %get-tuple-element.50), channel_id=1, source_target_pairs={{0,17},{1,16},{2,19},{3,18},{4,21},{5,20},{6,23},{7,22},{8,25},{9,... | collective-permute-start | bytes 1376264 | tf_op jit(solution)/shard_map/ppermute | solution.py:76
  28.8 11.6 %collective-permute-start.12 = (bf16[64,3584]{1,0:T(8,128)(2,1)S(1)}, bf16[64,3584]{1,0:T(8,128)(2,1)S(1)}, u32[]{:S(2)}, u32[]{:S(2)}) collective-permute-start(bf16[64,3584]{1,0:T(8,128)(2,1)S(1)} %get-tuple-element.107.refs_2_), channel_id=1, source_target_pairs={{0,2},{1,3},{2,0},{3,1},{4,6},{5,7},{6,4},{7,5},{8,10},{9,11},{10,... | collective-permute-start | bytes 1376264 | tf_op jit(solution)/shard_map/ppermute | solution.py:76
  34.5 1.0 copy-start.6
  35.6 13.4 %collective-permute-start.5 = (bf16[32,3584]{1,0:T(8,128)(2,1)S(1)}, bf16[32,3584]{1,0:T(8,128)(2,1)S(1)}, u32[]{:S(2)}, u32[]{:S(2)}) collective-permute-start(bf16[32,3584]{1,0:T(8,128)(2,1)S(1)} %get-tuple-element.57), channel_id=1, source_target_pairs={{0,4},{1,5},{2,14},{3,15},{4,8},{5,9},{6,2},{7,3},{8,12},{9,13},{1... | collective-permute-start | bytes 688136 | tf_op jit(solution)/shard_map/ppermute | solution.py:76
  37.2 11.8 %collective-permute-start.6 = (bf16[32,3584]{1,0:T(8,128)(2,1)S(1)}, bf16[32,3584]{1,0:T(8,128)(2,1)S(1)}, u32[]{:S(2)}, u32[]{:S(2)}) collective-permute-start(bf16[32,3584]{1,0:T(8,128)(2,1)S(1)} %get-tuple-element.58), channel_id=1, source_target_pairs={{0,14},{1,15},{2,4},{3,5},{4,2},{5,3},{6,8},{7,9},{8,6},{9,7},{10,... | collective-permute-start | bytes 688136 | tf_op jit(solution)/shard_map/ppermute | solution.py:76
  39.6 18.7 %collective-permute-start.7 = (bf16[32,3584]{1,0:T(8,128)(2,1)S(1)}, bf16[32,3584]{1,0:T(8,128)(2,1)S(1)}, u32[]{:S(2)}, u32[]{:S(2)}) collective-permute-start(bf16[32,3584]{1,0:T(8,128)(2,1)S(1)} %get-tuple-element.59), channel_id=1, source_target_pairs={{0,10},{1,11},{2,8},{3,9},{4,14},{5,15},{6,12},{7,13},{8,2},{9,3},... | collective-permute-start | bytes 688136 | tf_op jit(solution)/shard_map/ppermute | solution.py:76
  40.4 19.5 %copy-start.1 = (bf16[1,3584,256]{2,1,0:T(8,128)(2,1)S(1)}, bf16[1,3584,256]{2,1,0:T(8,128)(2,1)}, u32[]{:S(2)}) copy-start(bf16[1,3584,256]{2,1,0:T(8,128)(2,1)} %param.18) | copy-start | bytes 5505028
  40.5 19.5 %copy-start = (bf16[1,3584,256]{2,1,0:T(8,128)(2,1)S(1)}, bf16[1,3584,256]{2,1,0:T(8,128)(2,1)}, u32[]{:S(2)}) copy-start(bf16[1,3584,256]{2,1,0:T(8,128)(2,1)} %param.17) | copy-start | bytes 5505028
  40.5 26.3 %collective-permute-start.13 = (bf16[128,3584]{1,0:T(8,128)(2,1)S(1)}, bf16[128,3584]{1,0:T(8,128)(2,1)S(1)}, u32[]{:S(2)}, u32[]{:S(2)}) collective-permute-start(bf16[128,3584]{1,0:T(8,128)(2,1)S(1)} %constant_dynamic-update-slice_fusion.9.refs_0_), channel_id=1, source_target_pairs={{0,1},{1,0},{2,3},{3,2},{4,5},{5,4},{6,7},{7,6},{8,9},{9,8},{10,11... | collective-permute-start | bytes 2752520 | tf_op jit(solution)/shard_map/ppermute | solution.py:76
  58.3 13.5 %collective-permute-start.19 = (bf16[64,3584]{1,0:T(8,128)(2,1)S(1)}, bf16[64,3584]{1,0:T(8,128)(2,1)S(1)}, u32[]{:S(2)}, u32[]{:S(2)}) collective-permute-start(bf16[64,3584]{1,0:T(8,128)(2,1)S(1)} %pad_maximum_fusion.1.refs_0_), channel_id=1, source_target_pairs={{0,2},{1,3},{2,0},{3,1},{4,6},{5,7},{6,4},{7,5},{8,10},{9,11},{10,... | collective-permute-start | bytes 1376264 | tf_op jit(solution)/shard_map/ppermute | solution.py:76
  58.4 18.6 %collective-permute-start.8 = (bf16[64,3584]{1,0:T(8,128)(2,1)S(1)}, bf16[64,3584]{1,0:T(8,128)(2,1)S(1)}, u32[]{:S(2)}, u32[]{:S(2)}) collective-permute-start(bf16[64,3584]{1,0:T(8,128)(2,1)S(1)} %pad_maximum_fusion), channel_id=1, source_target_pairs={{0,2},{1,3},{2,0},{3,1},{4,6},{5,7},{6,4},{7,5},{8,10},{9,11},{10,... | collective-permute-start | bytes 1376264 | tf_op jit(solution)/shard_map/ppermute | solution.py:76
  60.6 7.0 %copy-start.3 = (bf16[1,128,3584]{2,1,0:T(8,128)(2,1)S(1)}, bf16[1,128,3584]{2,1,0:T(8,128)(2,1)}, u32[]{:S(2)}) copy-start(bf16[1,128,3584]{2,1,0:T(8,128)(2,1)} %param.16) | copy-start | bytes 2752516
  67.4 5.9 %copy-start.2 = (bf16[1,256,3584]{2,1,0:T(8,128)(2,1)S(1)}, bf16[1,256,3584]{2,1,0:T(8,128)(2,1)}, u32[]{:S(2)}) copy-start(bf16[1,256,3584]{2,1,0:T(8,128)(2,1)} %param.19) | copy-start | bytes 5505028
  67.4 4.4 %collective-permute-start.14 = (bf16[128,256]{1,0:T(8,128)(2,1)S(1)}, bf16[128,256]{1,0:T(8,128)(2,1)S(1)}, u32[]{:S(2)}, u32[]{:S(2)}) collective-permute-start(bf16[128,256]{1,0:T(8,128)(2,1)S(1)} %shard_map.121), channel_id=1, source_target_pairs={{0,1},{1,0},{2,3},{3,2},{4,5},{5,4},{6,7},{7,6},{8,9},{9,8},{10,11... | collective-permute-start | bytes 196616 | tf_op jit(solution)/shard_map/ppermute | solution.py:76
  67.7 26.3 %collective-permute-start.22 = (bf16[128,3584]{1,0:T(8,128)(2,1)S(1)}, bf16[128,3584]{1,0:T(8,128)(2,1)S(1)}, u32[]{:S(2)}, u32[]{:S(2)}) collective-permute-start(bf16[128,3584]{1,0:T(8,128)(2,1)S(1)} %shard_map.127), channel_id=1, source_target_pairs={{32,0},{33,1},{34,2},{35,3},{36,4},{37,5},{38,6},{39,7},{40,8},{41... | collective-permute-start | bytes 2752520 | tf_op jit(solution)/shard_map/ppermute | solution.py:87
  71.9 22.5 %collective-permute-start.21 = (bf16[128,3584]{1,0:T(8,128)(2,1)S(1)}, bf16[128,3584]{1,0:T(8,128)(2,1)}, u32[]{:S(2)}, u32[]{:S(2)}) collective-permute-start(bf16[128,3584]{1,0:T(8,128)(2,1)S(1)} %shard_map.124.refs_0_), channel_id=1, source_target_pairs={{0,1},{1,0},{2,3},{3,2},{4,5},{5,4},{6,7},{7,6},{8,9},{9,8},{10,11... | collective-permute-start | bytes 2752520 | tf_op jit(solution)/shard_map/ppermute | solution.py:76
  74.0 19.9 %collective-permute-start.15 = (bf16[64,3584]{1,0:T(8,128)(2,1)S(1)}, bf16[64,3584]{1,0:T(8,128)(2,1)S(1)}, u32[]{:S(2)}, u32[]{:S(2)}) collective-permute-start(bf16[64,3584]{1,0:T(8,128)(2,1)S(1)} %get-tuple-element.63), channel_id=1, source_target_pairs={{0,2},{1,3},{2,0},{3,1},{4,6},{5,7},{6,4},{7,5},{8,10},{9,11},{10,... | collective-permute-start | bytes 1376264 | tf_op jit(solution)/shard_map/ppermute | solution.py:76
  77.1 1.4 copy-start.9
  77.1 11.0 %copy-start.8 = (bf16[128,128]{1,0:T(8,128)(2,1)S(1)}, bf16[128,128]{1,0:T(8,128)(2,1)}, u32[]{:S(2)}) copy-start(bf16[128,128]{1,0:T(8,128)(2,1)} %get-tuple-element.61.refs_0_) | copy-start | bytes 98308
  78.4 17.8 %collective-permute-start.23 = (f32[128,256]{1,0:T(8,128)S(1)}, f32[128,256]{1,0:T(8,128)S(1)}, u32[]{:S(2)}, u32[]{:S(2)}) collective-permute-start(f32[128,256]{1,0:T(8,128)S(1)} %get-tuple-element.60.refs_1_), channel_id=1, source_target_pairs={{0,1},{1,0},{2,3},{3,2},{4,5},{5,4},{6,7},{7,6},{8,9},{9,8},{10,11... | collective-permute-start | bytes 393224 | tf_op jit(solution)/shard_map/ppermute | solution.py:76
  78.5 12.7 %collective-permute-start.20 = (bf16[128,128]{1,0:T(8,128)(2,1)S(1)}, bf16[128,128]{1,0:T(8,128)(2,1)S(1)}, u32[]{:S(2)}, u32[]{:S(2)}) collective-permute-start(bf16[128,128]{1,0:T(8,128)(2,1)S(1)} %shard_map.125), channel_id=1, source_target_pairs={{32,0},{33,1},{34,2},{35,3},{36,4},{37,5},{38,6},{39,7},{40,8},{41... | collective-permute-start | bytes 98312 | tf_op jit(solution)/shard_map/ppermute | solution.py:87
  91.3 3.1 %collective-permute-start.11 = (bf16[128,128]{1,0:T(8,128)(2,1)S(1)}, bf16[128,128]{1,0:T(8,128)(2,1)S(1)}, u32[]{:S(2)}, u32[]{:S(2)}) collective-permute-start(bf16[128,128]{1,0:T(8,128)(2,1)S(1)} %shard_map.119), channel_id=1, source_target_pairs={{0,32},{1,33},{2,34},{3,35},{4,36},{5,37},{6,38},{7,39},{8,40},{9,... | collective-permute-start | bytes 98312 | tf_op jit(solution)/shard_map/ppermute | solution.py:87
  96.9 2.7 %copy-start.4 = (bf16[1,128,3584]{2,1,0:T(8,128)(2,1)S(1)}, bf16[1,128,3584]{2,1,0:T(8,128)(2,1)}, u32[]{:S(2)}) copy-start(bf16[1,128,3584]{2,1,0:T(8,128)(2,1)} %param.10) | copy-start | bytes 2752516
  96.9 10.2 %collective-permute-start.25 = (bf16[128,1792]{1,0:T(8,128)(2,1)S(1)}, bf16[128,1792]{1,0:T(8,128)(2,1)S(1)}, u32[]{:S(2)}, u32[]{:S(2)}) collective-permute-start(bf16[128,1792]{1,0:T(8,128)(2,1)S(1)} %get-tuple-element.80), channel_id=1, source_target_pairs={{0,2},{1,3},{2,0},{3,1},{4,6},{5,7},{6,4},{7,5},{8,10},{9,11},{10,... | collective-permute-start | bytes 1376264 | tf_op jit(solution)/shard_map/ppermute | solution.py:76
  97.7 11.6 %collective-permute-start.24 = (bf16[128,1792]{1,0:T(8,128)(2,1)S(1)}, bf16[128,1792]{1,0:T(8,128)(2,1)S(1)}, u32[]{:S(2)}, u32[]{:S(2)}) collective-permute-start(bf16[128,1792]{1,0:T(8,128)(2,1)S(1)} %get-tuple-element.77), channel_id=1, source_target_pairs={{0,1},{1,0},{2,3},{3,2},{4,5},{5,4},{6,7},{7,6},{8,9},{9,8},{10,11... | collective-permute-start | bytes 1376264 | tf_op jit(solution)/shard_map/ppermute | solution.py:76
  99.7 43.6 %collective-permute-start.10 = (bf16[128,3584]{1,0:T(8,128)(2,1)S(1)}, bf16[128,3584]{1,0:T(8,128)(2,1)S(1)}, u32[]{:S(2)}, u32[]{:S(2)}) collective-permute-start(bf16[128,3584]{1,0:T(8,128)(2,1)S(1)} %shard_map.118), channel_id=1, source_target_pairs={{0,32},{1,33},{2,34},{3,35},{4,36},{5,37},{6,38},{7,39},{8,40},{9,... | collective-permute-start | bytes 2752520 | tf_op jit(solution)/shard_map/ppermute | solution.py:87
  107.2 8.8 %collective-permute-start.29 = (bf16[64,1792]{1,0:T(8,128)(2,1)S(1)}, bf16[64,1792]{1,0:T(8,128)(2,1)S(1)}, u32[]{:S(2)}, u32[]{:S(2)}) collective-permute-start(bf16[64,1792]{1,0:T(8,128)(2,1)S(1)} %get-tuple-element.81.refs_5_), channel_id=1, source_target_pairs={{0,1},{1,0},{2,3},{3,2},{4,5},{5,4},{6,7},{7,6},{8,9},{9,8},{10,11... | collective-permute-start | bytes 688136 | tf_op jit(solution)/shard_map/ppermute | solution.py:76
  109.5 10.8 %collective-permute-start.28 = (bf16[64,1792]{1,0:T(8,128)(2,1)S(1)}, bf16[64,1792]{1,0:T(8,128)(2,1)S(1)}, u32[]{:S(2)}, u32[]{:S(2)}) collective-permute-start(bf16[64,1792]{1,0:T(8,128)(2,1)S(1)} %get-tuple-element.78.refs_4_), channel_id=1, source_target_pairs={{0,2},{1,3},{2,0},{3,1},{4,6},{5,7},{6,4},{7,5},{8,10},{9,11},{10,... | collective-permute-start | bytes 688136 | tf_op jit(solution)/shard_map/ppermute | solution.py:76
  109.7 10.9 %collective-permute-start.16 = (bf16[16,3584]{1,0:T(8,128)(2,1)S(1)}, bf16[16,3584]{1,0:T(8,128)(2,1)S(1)}, u32[]{:S(2)}, u32[]{:S(2)}) collective-permute-start(bf16[16,3584]{1,0:T(8,128)(2,1)S(1)} %get-tuple-element.65), channel_id=1, source_target_pairs={{4,0},{5,1},{14,2},{15,3},{8,4},{9,5},{2,6},{3,7},{12,8},{13,9},{6... | collective-permute-start | bytes 344072 | tf_op jit(solution)/shard_map/ppermute | solution.py:76
  116.0 7.6 %collective-permute-start.17 = (bf16[16,3584]{1,0:T(8,128)(2,1)S(1)}, bf16[16,3584]{1,0:T(8,128)(2,1)S(1)}, u32[]{:S(2)}, u32[]{:S(2)}) collective-permute-start(bf16[16,3584]{1,0:T(8,128)(2,1)S(1)} %get-tuple-element.66), channel_id=1, source_target_pairs={{14,0},{15,1},{4,2},{5,3},{2,4},{3,5},{8,6},{9,7},{6,8},{7,9},{12,... | collective-permute-start | bytes 344072 | tf_op jit(solution)/shard_map/ppermute | solution.py:76
  116.0 8.5 %collective-permute-start.18 = (bf16[16,3584]{1,0:T(8,128)(2,1)S(1)}, bf16[16,3584]{1,0:T(8,128)(2,1)S(1)}, u32[]{:S(2)}, u32[]{:S(2)}) collective-permute-start(bf16[16,3584]{1,0:T(8,128)(2,1)S(1)} %get-tuple-element.67), channel_id=1, source_target_pairs={{10,0},{11,1},{8,2},{9,3},{14,4},{15,5},{12,6},{13,7},{2,8},{3,9},... | collective-permute-start | bytes 344072 | tf_op jit(solution)/shard_map/ppermute | solution.py:76
  120.4 13.4 %collective-permute-start.30 = (bf16[16,3584]{1,0:T(8,128)(2,1)S(1)}, bf16[16,3584]{1,0:T(8,128)(2,1)S(1)}, u32[]{:S(2)}, u32[]{:S(2)}) collective-permute-start(bf16[16,3584]{1,0:T(8,128)(2,1)S(1)} %get-tuple-element.88), channel_id=1, source_target_pairs={{4,0},{5,1},{14,2},{15,3},{8,4},{9,5},{2,6},{3,7},{12,8},{13,9},{6... | collective-permute-start | bytes 344072 | tf_op jit(solution)/shard_map/ppermute | solution.py:76
  120.7 16.8 %collective-permute-start.31 = (bf16[16,3584]{1,0:T(8,128)(2,1)S(1)}, bf16[16,3584]{1,0:T(8,128)(2,1)S(1)}, u32[]{:S(2)}, u32[]{:S(2)}) collective-permute-start(bf16[16,3584]{1,0:T(8,128)(2,1)S(1)} %get-tuple-element.89), channel_id=1, source_target_pairs={{14,0},{15,1},{4,2},{5,3},{2,4},{3,5},{8,6},{9,7},{6,8},{7,9},{12,... | collective-permute-start | bytes 344072 | tf_op jit(solution)/shard_map/ppermute | solution.py:76
  123.6 13.9 %collective-permute-start.32 = (bf16[16,3584]{1,0:T(8,128)(2,1)S(1)}, bf16[16,3584]{1,0:T(8,128)(2,1)S(1)}, u32[]{:S(2)}, u32[]{:S(2)}) collective-permute-start(bf16[16,3584]{1,0:T(8,128)(2,1)S(1)} %get-tuple-element.90), channel_id=1, source_target_pairs={{10,0},{11,1},{8,2},{9,3},{14,4},{15,5},{12,6},{13,7},{2,8},{3,9},... | collective-permute-start | bytes 344072 | tf_op jit(solution)/shard_map/ppermute | solution.py:76
  124.5 18.8 %collective-permute-start.26 = (bf16[32,3584]{1,0:T(8,128)(2,1)S(1)}, bf16[32,3584]{1,0:T(8,128)(2,1)S(1)}, u32[]{:S(2)}, u32[]{:S(2)}) collective-permute-start(bf16[32,3584]{1,0:T(8,128)(2,1)S(1)} %get-tuple-element.82), channel_id=1, source_target_pairs={{0,32},{1,33},{2,34},{3,35},{4,36},{5,37},{6,38},{7,39},{8,40},{9,... | collective-permute-start | bytes 688136 | tf_op jit(solution)/shard_map/ppermute | solution.py:87
  133.8 10.7 %collective-permute-start.27 = (bf16[32,3584]{1,0:T(8,128)(2,1)S(1)}, bf16[32,3584]{1,0:T(8,128)(2,1)S(1)}, u32[]{:S(2)}, u32[]{:S(2)}) collective-permute-start(bf16[32,3584]{1,0:T(8,128)(2,1)S(1)} %get-tuple-element.83), channel_id=1, source_target_pairs={{0,49},{1,48},{2,51},{3,50},{4,53},{5,52},{6,55},{7,54},{8,57},{9,... | collective-permute-start | bytes 688136 | tf_op jit(solution)/shard_map/ppermute | solution.py:87
  137.6 8.2 %collective-permute-start.33 = (bf16[32,3584]{1,0:T(8,128)(2,1)S(1)}, bf16[32,3584]{1,0:T(8,128)(2,1)S(1)}, u32[]{:S(2)}, u32[]{:S(2)}) collective-permute-start(bf16[32,3584]{1,0:T(8,128)(2,1)S(1)} %get-tuple-element.91), channel_id=1, source_target_pairs={{32,0},{33,1},{34,2},{35,3},{36,4},{37,5},{38,6},{39,7},{40,8},{41... | collective-permute-start | bytes 688136 | tf_op jit(solution)/shard_map/ppermute | solution.py:87
  140.1 11.2 %collective-permute-start.34 = (bf16[32,3584]{1,0:T(8,128)(2,1)S(1)}, bf16[32,3584]{1,0:T(8,128)(2,1)S(1)}, u32[]{:S(2)}, u32[]{:S(2)}) collective-permute-start(bf16[32,3584]{1,0:T(8,128)(2,1)S(1)} %get-tuple-element.92), channel_id=1, source_target_pairs={{32,17},{33,16},{34,19},{35,18},{36,21},{37,20},{38,23},{39,22},{4... | collective-permute-start | bytes 688136 | tf_op jit(solution)/shard_map/ppermute | solution.py:87

commit v4 on v3

--- a/solution.py
+++ b/solution.py
@@ -1,3 +1,5 @@
+import functools
+
 import jax
 import jax.numpy as jnp
 from jax import lax
@@ -150,6 +152,12 @@
     far_ref[...] = jnp.concatenate([b[CAP:] for b in blocks], axis=0).astype(BF16)
 
 
+def side_body(side, b0, b1, b2, b3, out_ref):
+    rows = slice(side * CAP, (side + 1) * CAP)
+    blocks = [b[...].astype(F32)[rows] for b in (b0, b1, b2, b3)]
+    out_ref[...] = jnp.concatenate(blocks, axis=0).astype(BF16)
+
+
 def join_body(*refs):
     refs[-1][...] = jnp.concatenate([r[...] for r in refs[:-1]], axis=0)
 
@@ -192,14 +200,14 @@
 def grad_hidden_body(rows_ref, wd_ref, wdp_ref, mine_ref, send_ref):
     rows = rows_ref[...]
     mine_ref[...] = dot_t(rows, wd_ref[...])
-    send_ref[...] = dot_t(rows, wdp_ref[...])
+    send_ref[...] = dot_t(rows, wdp_ref[...]).astype(BF16)
 
 
 def grads_body(
     sg_ref, su_ref, sgx_ref, sux_ref, mine_ref, got_ref, gg_ref, gu_ref
 ):
     mine = mine_ref[...]
-    got = got_ref[...]
+    got = got_ref[...].astype(F32)
     count = mine.shape[0]
     gg_ref[:count] = (mine * sg_ref[...]).astype(BF16)
     gg_ref[count:] = (got * sgx_ref[...]).astype(BF16)
@@ -337,7 +345,12 @@
     sg, su = call(
         slope_body, [shape(rows, hid, F32)] * 2, [by, wg, wu], proj, after=(bcomb,)
     )
-    gh, gh_send = call(grad_hidden_body, [shape(rows, hid, F32)] * 2, [cy, wd, wdp], proj)
+    gh, gh_send = call(
+        grad_hidden_body,
+        [shape(rows, hid, F32), shape(rows, hid)],
+        [cy, wd, wdp],
+        proj,
+    )
     gh_got = move(gh_send, DP_PAIR)
     fbase = relay(join([fwd_in[0]], after=(gh_send,)), STAY, 1)
     fcomb = relay(join([fcomb], after=(gh_send,)), STAY, 1)
@@ -372,8 +385,12 @@
     blocks = call(
         finish_body, [shape(BLOCK, width)] * PAIRS, [xkeep, xgot, zkeep, zgot]
     )
-    own, far = call(part_body, [shape(HALF, width)] * 2, shifts(blocks, True))
-    own, far = relay(own, STAY, -1), relay(far, ACROSS_XHI, -1)
+    blocks = shifts(blocks, True)
+    (far,) = call(functools.partial(side_body, 1), [shape(HALF, width)], blocks)
+    (own,) = call(
+        functools.partial(side_body, 0), [shape(HALF, width)], blocks, after=(far,)
+    )
+    far, own = relay(far, ACROSS_XHI, -1), relay(own, STAY, -1)
     (bwd_out,) = call(
         combine_body,
         [shape(tokens, width)],

time: 153 us -> 153 us (level)
  starting transfers between devices: 86.2 us -> 84.5 us
    ppermute x8, starting transfers between devices: 40.9 us -> 35.7 us  [relay(): return lax.ppermute(value, ('pipe', 'expert', 'dp'), full)]
    ppermute x27, starting transfers between devices: 45.3 us -> 48.8 us  [move(): return lax.ppermute(value, ('expert', 'dp'), pairs)]
    ppermute x27, waiting for transfers between devices: 36.8 us -> 39.1 us  [move(): return lax.ppermute(value, ('expert', 'dp'), pairs)]
    pallas_call x25 -> x26, Pallas kernels: 14.5 us -> 14.5 us  [call(): pl.pallas_call(run, out_shape=tuple(outs), in_specs=specs, out_specs=tupl...]
where the time goes in v4:
time: 153 us; the launch traced here: 152 us
  starting transfers between devices  84.5 us (55%)
  waiting for transfers between devices  48.2 us (32%)
  Pallas kernels  15.8 us (10%)
  local copies, waits for them, and re-layouts  2.31 us (2%)
    ppermute x27, starting transfers between devices, move(): return lax.ppermute(value, ('expert', 'dp'), pairs)  48.8 us
    ppermute x27, waiting for transfers between devices, move(): return lax.ppermute(value, ('expert', 'dp'), pairs)  39.1 us
    ppermute x8, starting transfers between devices, relay(): return lax.ppermute(value, ('pipe', 'expert', 'dp'), full)  35.7 us
    pallas_call x26, Pallas kernels, call(): pl.pallas_call(run, out_shape=tuple(outs), in_specs=specs, out_specs=tupl...  14.5 us
    ppermute x8, waiting for transfers between devices, relay(): return lax.ppermute(value, ('pipe', 'expert', 'dp'), full)  9.1 us
  transfers between devices with their start and end apart: 35, of which 12 were waited for; matrix products, arithmetic and copies ran while one was open for 0% of the time, Pallas kernels for 7%

profile of v4, /device:TPU:1, one launch (start us, length us, event | category | flops | bytes accessed | tf_op | source)
XLA Modules:
  0.0 152.1 jit_solution(16957972123669983391)
XLA Ops:
  0.6 2.4 %shard_map.113 = (bf16[32,3584]{1,0:T(8,128)(2,1)}, bf16[32,3584]{1,0:T(8,128)(2,1)}, bf16[128,128]{1,0:T(8,128)(2,1)}) custom-call(s32[1]{0:T(128)} %bitcast.1.refs_0_, s32[8,128]{1,0:T(8,128)} %bitcast.42, f32[8,128]{1,0:T(8,128)} %bitcast.43, bf16[128,3584]{1,0:T(8,128)(2,1)} %bitcast.38), custom_call_target="tpu_custom_call" | custom-call | bytes 1417220 | tf_op jit(solution)/shard_map/pallas_call | solution.py:32
  3.0 3.3 %collective-permute-start = (bf16[32,3584]{1,0:T(8,128)(2,1)}, bf16[32,3584]{1,0:T(8,128)(2,1)S(1)}, u32[]{:S(2)}, u32[]{:S(2)}) collective-permute-start(bf16[32,3584]{1,0:T(8,128)(2,1)} %get-tuple-element.46), channel_id=1, source_target_pairs={{0,17},{1,16},{2,19},{3,18},{4,21},{5,20},{6,23},{7,22},{8,25},{9,... | collective-permute-start | bytes 688136 | tf_op jit(solution)/shard_map/ppermute | solution.py:78
  6.3 4.6 %collective-permute-done.refs_5_.refs_1_ = bf16[32,3584]{1,0:T(8,128)(2,1)S(1)} collective-permute-done((bf16[32,3584]{1,0:T(8,128)(2,1)}, bf16[32,3584]{1,0:T(8,128)(2,1)S(1)}, u32[]{:S(2)}, u32[]{:S(2)}) %collective-permute-start) | collective-permute-done | bytes 229408 | tf_op jit(solution)/shard_map/ppermute | solution.py:78
  10.9 1.0 copy-done.7
  12.0 3.9 %collective-permute-start.2 = (bf16[16,3584]{1,0:T(8,128)(2,1)S(1)}, bf16[16,3584]{1,0:T(8,128)(2,1)S(1)}, u32[]{:S(2)}, u32[]{:S(2)}) collective-permute-start(bf16[16,3584]{1,0:T(8,128)(2,1)S(1)} %get-tuple-element.51), channel_id=1, source_target_pairs={{0,4},{1,5},{2,14},{3,15},{4,8},{5,9},{6,2},{7,3},{8,12},{9,13},{1... | collective-permute-start | bytes 344072 | tf_op jit(solution)/shard_map/ppermute | solution.py:78
  15.9 3.8 %collective-permute-start.3 = (bf16[16,3584]{1,0:T(8,128)(2,1)S(1)}, bf16[16,3584]{1,0:T(8,128)(2,1)S(1)}, u32[]{:S(2)}, u32[]{:S(2)}) collective-permute-start(bf16[16,3584]{1,0:T(8,128)(2,1)S(1)} %get-tuple-element.52), channel_id=1, source_target_pairs={{0,14},{1,15},{2,4},{3,5},{4,2},{5,3},{6,8},{7,9},{8,6},{9,7},{10,... | collective-permute-start | bytes 344072 | tf_op jit(solution)/shard_map/ppermute | solution.py:78
  20.2 3.0 %shard_map.114 = (bf16[64,3584]{1,0:T(8,128)(2,1)}, bf16[64,3584]{1,0:T(8,128)(2,1)}, bf16[128,128]{1,0:T(8,128)(2,1)}) custom-call(s32[1]{0:T(128)} %bitcast.1.refs_0_, s32[8,128]{1,0:T(8,128)} %bitcast.44, f32[8,128]{1,0:T(8,128)} %bitcast.45, bf16[128,3584]{1,0:T(8,128)(2,1)} %bitcast.40, bf16[128,3584]{1,0:T(8,128)(2,1)} %bitcast.36, ...), custom_call_target="tpu_custom_call" | custom-call | bytes 2793476 | tf_op jit(solution)/shard_map/pallas_call | solution.py:32
  23.2 2.5 %collective-permute-start.1 = (bf16[64,3584]{1,0:T(8,128)(2,1)}, bf16[64,3584]{1,0:T(8,128)(2,1)S(1)}, u32[]{:S(2)}, u32[]{:S(2)}) collective-permute-start(bf16[64,3584]{1,0:T(8,128)(2,1)} %get-tuple-element.48), channel_id=1, source_target_pairs={{0,17},{1,16},{2,19},{3,18},{4,21},{5,20},{6,23},{7,22},{8,25},{9,... | collective-permute-start | bytes 1376264 | tf_op jit(solution)/shard_map/ppermute | solution.py:78
  25.7 3.1 %collective-permute-done.4 = bf16[16,3584]{1,0:T(8,128)(2,1)S(1)} collective-permute-done((bf16[16,3584]{1,0:T(8,128)(2,1)S(1)}, bf16[16,3584]{1,0:T(8,128)(2,1)S(1)}, u32[]{:S(2)}, u32[]{:S(2)}) %collective-permute-start.4) | collective-permute-done | bytes 114720 | tf_op jit(solution)/shard_map/ppermute | solution.py:78
  28.8 2.1 %collective-permute-start.12 = (bf16[64,3584]{1,0:T(8,128)(2,1)S(1)}, bf16[64,3584]{1,0:T(8,128)(2,1)S(1)}, u32[]{:S(2)}, u32[]{:S(2)}) collective-permute-start(bf16[64,3584]{1,0:T(8,128)(2,1)S(1)} %get-tuple-element.103.refs_2_), channel_id=1, source_target_pairs={{0,2},{1,3},{2,0},{3,1},{4,6},{5,7},{6,4},{7,5},{8,10},{9,11},{10,... | collective-permute-start | bytes 1376264 | tf_op jit(solution)/shard_map/ppermute | solution.py:78
  31.0 3.5 %collective-permute-done.1.refs_1_ = bf16[64,3584]{1,0:T(8,128)(2,1)S(1)} collective-permute-done((bf16[64,3584]{1,0:T(8,128)(2,1)}, bf16[64,3584]{1,0:T(8,128)(2,1)S(1)}, u32[]{:S(2)}, u32[]{:S(2)}) %collective-permute-start.1) | collective-permute-done | bytes 458784 | tf_op jit(solution)/shard_map/ppermute | solution.py:78
  34.5 1.0 copy-done.6
  35.6 1.6 %collective-permute-start.5 = (bf16[32,3584]{1,0:T(8,128)(2,1)S(1)}, bf16[32,3584]{1,0:T(8,128)(2,1)S(1)}, u32[]{:S(2)}, u32[]{:S(2)}) collective-permute-start(bf16[32,3584]{1,0:T(8,128)(2,1)S(1)} %get-tuple-element.55), channel_id=1, source_target_pairs={{0,4},{1,5},{2,14},{3,15},{4,8},{5,9},{6,2},{7,3},{8,12},{9,13},{1... | collective-permute-start | bytes 688136 | tf_op jit(solution)/shard_map/ppermute | solution.py:78
  37.2 2.4 %collective-permute-start.6 = (bf16[32,3584]{1,0:T(8,128)(2,1)S(1)}, bf16[32,3584]{1,0:T(8,128)(2,1)S(1)}, u32[]{:S(2)}, u32[]{:S(2)}) collective-permute-start(bf16[32,3584]{1,0:T(8,128)(2,1)S(1)} %get-tuple-element.56), channel_id=1, source_target_pairs={{0,14},{1,15},{2,4},{3,5},{4,2},{5,3},{6,8},{7,9},{8,6},{9,7},{10,... | collective-permute-start | bytes 688136 | tf_op jit(solution)/shard_map/ppermute | solution.py:78
  39.6 0.8 collective-permute-start.7
  40.6 0.7 shard_map.120.refs_3_.refs_0_.refs_1_
  41.3 7.7 %collective-permute-done.5 = bf16[32,3584]{1,0:T(8,128)(2,1)S(1)} collective-permute-done((bf16[32,3584]{1,0:T(8,128)(2,1)S(1)}, bf16[32,3584]{1,0:T(8,128)(2,1)S(1)}, u32[]{:S(2)}, u32[]{:S(2)}) %collective-permute-start.5) | collective-permute-done | bytes 229408 | tf_op jit(solution)/shard_map/ppermute | solution.py:78
  49.0 9.2 %collective-permute-done.7 = bf16[32,3584]{1,0:T(8,128)(2,1)S(1)} collective-permute-done((bf16[32,3584]{1,0:T(8,128)(2,1)S(1)}, bf16[32,3584]{1,0:T(8,128)(2,1)S(1)}, u32[]{:S(2)}, u32[]{:S(2)}) %collective-permute-start.7) | collective-permute-done | bytes 229408 | tf_op jit(solution)/shard_map/ppermute | solution.py:78
  58.4 1.5 %collective-permute-start.8 = (bf16[64,3584]{1,0:T(8,128)(2,1)S(1)}, bf16[64,3584]{1,0:T(8,128)(2,1)S(1)}, u32[]{:S(2)}, u32[]{:S(2)}) collective-permute-start(bf16[64,3584]{1,0:T(8,128)(2,1)S(1)} %pad_maximum_fusion), channel_id=1, source_target_pairs={{0,2},{1,3},{2,0},{3,1},{4,6},{5,7},{6,4},{7,5},{8,10},{9,11},{10,... | collective-permute-start | bytes 1376264 | tf_op jit(solution)/shard_map/ppermute | solution.py:78
  60.0 6.8 %collective-permute-done.13.refs_0_ = bf16[128,3584]{1,0:T(8,128)(2,1)S(1)} collective-permute-done((bf16[128,3584]{1,0:T(8,128)(2,1)S(1)}, bf16[128,3584]{1,0:T(8,128)(2,1)S(1)}, u32[]{:S(2)}, u32[]{:S(2)}) %collective-permute-start.13) | collective-permute-done | bytes 917536 | tf_op jit(solution)/shard_map/ppermute | solution.py:78
  67.7 4.1 %collective-permute-start.22 = (bf16[128,3584]{1,0:T(8,128)(2,1)S(1)}, bf16[128,3584]{1,0:T(8,128)(2,1)S(1)}, u32[]{:S(2)}, u32[]{:S(2)}) collective-permute-start(bf16[128,3584]{1,0:T(8,128)(2,1)S(1)} %shard_map.127), channel_id=1, source_target_pairs={{32,0},{33,1},{34,2},{35,3},{36,4},{37,5},{38,6},{39,7},{40,8},{41... | collective-permute-start | bytes 2752520 | tf_op jit(solution)/shard_map/ppermute | solution.py:89
  71.9 1.4 collective-permute-start.21
  73.3 3.8 %collective-permute-start.20 = (bf16[128,128]{1,0:T(8,128)(2,1)S(1)}, bf16[128,128]{1,0:T(8,128)(2,1)S(1)}, u32[]{:S(2)}, u32[]{:S(2)}) collective-permute-start(bf16[128,128]{1,0:T(8,128)(2,1)S(1)} %shard_map.125), channel_id=1, source_target_pairs={{32,0},{33,1},{34,2},{35,3},{36,4},{37,5},{38,6},{39,7},{40,8},{41... | collective-permute-start | bytes 98312 | tf_op jit(solution)/shard_map/ppermute | solution.py:89
  77.8 2.0 %collective-permute-start.15 = (bf16[64,3584]{1,0:T(8,128)(2,1)S(1)}, bf16[64,3584]{1,0:T(8,128)(2,1)S(1)}, u32[]{:S(2)}, u32[]{:S(2)}) collective-permute-start(bf16[64,3584]{1,0:T(8,128)(2,1)S(1)} %get-tuple-element.61), channel_id=1, source_target_pairs={{0,2},{1,3},{2,0},{3,1},{4,6},{5,7},{6,4},{7,5},{8,10},{9,11},{10,... | collective-permute-start | bytes 1376264 | tf_op jit(solution)/shard_map/ppermute | solution.py:78
  79.8 1.3 shard_map.117
  81.1 1.8 %collective-permute-start.23 = (bf16[128,256]{1,0:T(8,128)(2,1)S(1)}, bf16[128,256]{1,0:T(8,128)(2,1)S(1)}, u32[]{:S(2)}, u32[]{:S(2)}) collective-permute-start(bf16[128,256]{1,0:T(8,128)(2,1)S(1)} %get-tuple-element.58.refs_1_), channel_id=1, source_target_pairs={{0,1},{1,0},{2,3},{3,2},{4,5},{5,4},{6,7},{7,6},{8,9},{9,8},{10,11... | collective-permute-start | bytes 196616 | tf_op jit(solution)/shard_map/ppermute | solution.py:78
  82.9 1.9 %collective-permute-done.20.refs_3_.refs_1_ = bf16[128,128]{1,0:T(8,128)(2,1)S(1)} collective-permute-done((bf16[128,128]{1,0:T(8,128)(2,1)S(1)}, bf16[128,128]{1,0:T(8,128)(2,1)S(1)}, u32[]{:S(2)}, u32[]{:S(2)}) %collective-permute-start.20) | collective-permute-done | bytes 32800 | tf_op jit(solution)/shard_map/ppermute | solution.py:89
  84.8 1.9 %collective-permute-start.11 = (bf16[128,128]{1,0:T(8,128)(2,1)S(1)}, bf16[128,128]{1,0:T(8,128)(2,1)S(1)}, u32[]{:S(2)}, u32[]{:S(2)}) collective-permute-start(bf16[128,128]{1,0:T(8,128)(2,1)S(1)} %shard_map.119), channel_id=1, source_target_pairs={{0,32},{1,33},{2,34},{3,35},{4,36},{5,37},{6,38},{7,39},{8,40},{9,... | collective-permute-start | bytes 98312 | tf_op jit(solution)/shard_map/ppermute | solution.py:89
  86.7 0.7 shard_map.126
  87.4 3.3 %collective-permute-done.15.refs_1_ = bf16[64,3584]{1,0:T(8,128)(2,1)S(1)} collective-permute-done((bf16[64,3584]{1,0:T(8,128)(2,1)S(1)}, bf16[64,3584]{1,0:T(8,128)(2,1)S(1)}, u32[]{:S(2)}, u32[]{:S(2)}) %collective-permute-start.15) | collective-permute-done | bytes 458784 | tf_op jit(solution)/shard_map/ppermute | solution.py:78
  91.4 1.8 %shard_map.128 = (f32[128,256]{1,0:T(8,128)S(1)}, f32[128,256]{1,0:T(8,128)S(1)}) custom-call(bf16[128,3584]{1,0:T(8,128)(2,1)} %collective-permute-done.21.refs_0_, bf16[3584,256]{1,0:T(8,128)(2,1)S(1)} %bitcast.24, bf16[3584,256]{1,0:T(8,128)(2,1)S(1)} %bitcast.30, bf16[16,3584]{1,0:T(8,128)(2,1)S(1)} %get-tuple-element.62.refs_3_.refs_0_, ...), custom_call_target="tpu_custom_call" | custom-call | flops 469762048 | bytes 4849664 | tf_op jit(solution)/shard_map/pallas_call | solution.py:32
  93.3 0.7 shard_map.132
  94.0 1.6 %collective-permute-start.25 = (bf16[128,1792]{1,0:T(8,128)(2,1)S(1)}, bf16[128,1792]{1,0:T(8,128)(2,1)S(1)}, u32[]{:S(2)}, u32[]{:S(2)}) collective-permute-start(bf16[128,1792]{1,0:T(8,128)(2,1)S(1)} %get-tuple-element.78), channel_id=1, source_target_pairs={{0,2},{1,3},{2,0},{3,1},{4,6},{5,7},{6,4},{7,5},{8,10},{9,11},{10,... | collective-permute-start | bytes 1376264 | tf_op jit(solution)/shard_map/ppermute | solution.py:78
  95.6 0.7 shard_map.130
  96.3 2.4 %collective-permute-start.24 = (bf16[128,1792]{1,0:T(8,128)(2,1)S(1)}, bf16[128,1792]{1,0:T(8,128)(2,1)S(1)}, u32[]{:S(2)}, u32[]{:S(2)}) collective-permute-start(bf16[128,1792]{1,0:T(8,128)(2,1)S(1)} %get-tuple-element.75), channel_id=1, source_target_pairs={{0,1},{1,0},{2,3},{3,2},{4,5},{5,4},{6,7},{7,6},{8,9},{9,8},{10,11... | collective-permute-start | bytes 1376264 | tf_op jit(solution)/shard_map/ppermute | solution.py:78
  98.8 6.9 %collective-permute-start.10 = (bf16[128,3584]{1,0:T(8,128)(2,1)S(1)}, bf16[128,3584]{1,0:T(8,128)(2,1)S(1)}, u32[]{:S(2)}, u32[]{:S(2)}) collective-permute-start(bf16[128,3584]{1,0:T(8,128)(2,1)S(1)} %shard_map.118), channel_id=1, source_target_pairs={{0,32},{1,33},{2,34},{3,35},{4,36},{5,37},{6,38},{7,39},{8,40},{9,... | collective-permute-start | bytes 2752520 | tf_op jit(solution)/shard_map/ppermute | solution.py:89
  106.1 0.9 collective-permute-start.28
  107.0 7.6 %collective-permute-start.16 = (bf16[16,3584]{1,0:T(8,128)(2,1)S(1)}, bf16[16,3584]{1,0:T(8,128)(2,1)S(1)}, u32[]{:S(2)}, u32[]{:S(2)}) collective-permute-start(bf16[16,3584]{1,0:T(8,128)(2,1)S(1)} %get-tuple-element.63), channel_id=1, source_target_pairs={{4,0},{5,1},{14,2},{15,3},{8,4},{9,5},{2,6},{3,7},{12,8},{13,9},{6... | collective-permute-start | bytes 344072 | tf_op jit(solution)/shard_map/ppermute | solution.py:78
  114.6 4.9 %collective-permute-start.18 = (bf16[16,3584]{1,0:T(8,128)(2,1)S(1)}, bf16[16,3584]{1,0:T(8,128)(2,1)S(1)}, u32[]{:S(2)}, u32[]{:S(2)}) collective-permute-start(bf16[16,3584]{1,0:T(8,128)(2,1)S(1)} %get-tuple-element.65), channel_id=1, source_target_pairs={{10,0},{11,1},{8,2},{9,3},{14,4},{15,5},{12,6},{13,7},{2,8},{3,9},... | collective-permute-start | bytes 344072 | tf_op jit(solution)/shard_map/ppermute | solution.py:78
  119.6 3.1 %collective-permute-start.31 = (bf16[16,3584]{1,0:T(8,128)(2,1)S(1)}, bf16[16,3584]{1,0:T(8,128)(2,1)S(1)}, u32[]{:S(2)}, u32[]{:S(2)}) collective-permute-start(bf16[16,3584]{1,0:T(8,128)(2,1)S(1)} %get-tuple-element.87), channel_id=1, source_target_pairs={{14,0},{15,1},{4,2},{5,3},{2,4},{3,5},{8,6},{9,7},{6,8},{7,9},{12,... | collective-permute-start | bytes 344072 | tf_op jit(solution)/shard_map/ppermute | solution.py:78
  123.1 10.9 %collective-permute-start.26 = (bf16[32,3584]{1,0:T(8,128)(2,1)S(1)}, bf16[32,3584]{1,0:T(8,128)(2,1)S(1)}, u32[]{:S(2)}, u32[]{:S(2)}) collective-permute-start(bf16[32,3584]{1,0:T(8,128)(2,1)S(1)} %get-tuple-element.80), channel_id=1, source_target_pairs={{0,32},{1,33},{2,34},{3,35},{4,36},{5,37},{6,38},{7,39},{8,40},{9,... | collective-permute-start | bytes 688136 | tf_op jit(solution)/shard_map/ppermute | solution.py:89
  134.0 2.7 %collective-permute-start.27 = (bf16[32,3584]{1,0:T(8,128)(2,1)S(1)}, bf16[32,3584]{1,0:T(8,128)(2,1)S(1)}, u32[]{:S(2)}, u32[]{:S(2)}) collective-permute-start(bf16[32,3584]{1,0:T(8,128)(2,1)S(1)} %get-tuple-element.81), channel_id=1, source_target_pairs={{0,49},{1,48},{2,51},{3,50},{4,53},{5,52},{6,55},{7,54},{8,57},{9,... | collective-permute-start | bytes 688136 | tf_op jit(solution)/shard_map/ppermute | solution.py:89
  136.7 2.6 %collective-permute-start.33 = (bf16[32,3584]{1,0:T(8,128)(2,1)S(1)}, bf16[32,3584]{1,0:T(8,128)(2,1)S(1)}, u32[]{:S(2)}, u32[]{:S(2)}) collective-permute-start(bf16[32,3584]{1,0:T(8,128)(2,1)S(1)} %shard_map.139), channel_id=1, source_target_pairs={{32,0},{33,1},{34,2},{35,3},{36,4},{37,5},{38,6},{39,7},{40,8},{41... | collective-permute-start | bytes 688136 | tf_op jit(solution)/shard_map/ppermute | solution.py:89
  139.4 2.8 %collective-permute-start.34 = (bf16[32,3584]{1,0:T(8,128)(2,1)S(1)}, bf16[32,3584]{1,0:T(8,128)(2,1)S(1)}, u32[]{:S(2)}, u32[]{:S(2)}) collective-permute-start(bf16[32,3584]{1,0:T(8,128)(2,1)S(1)} %shard_map.138.refs_4_), channel_id=1, source_target_pairs={{32,17},{33,16},{34,19},{35,18},{36,21},{37,20},{38,23},{39,22},{4... | collective-permute-start | bytes 688136 | tf_op jit(solution)/shard_map/ppermute | solution.py:89
  142.3 3.0 %collective-permute-done.27.refs_3_ = bf16[32,3584]{1,0:T(8,128)(2,1)S(1)} collective-permute-done((bf16[32,3584]{1,0:T(8,128)(2,1)S(1)}, bf16[32,3584]{1,0:T(8,128)(2,1)S(1)}, u32[]{:S(2)}, u32[]{:S(2)}) %collective-permute-start.27) | collective-permute-done | bytes 229408 | tf_op jit(solution)/shard_map/ppermute | solution.py:89
  145.3 1.3 shard_map.135
  146.6 4.2 %collective-permute-done.34.refs_3_ = bf16[32,3584]{1,0:T(8,128)(2,1)S(1)} collective-permute-done((bf16[32,3584]{1,0:T(8,128)(2,1)S(1)}, bf16[32,3584]{1,0:T(8,128)(2,1)S(1)}, u32[]{:S(2)}, u32[]{:S(2)}) %collective-permute-start.34) | collective-permute-done | bytes 229408 | tf_op jit(solution)/shard_map/ppermute | solution.py:89
  150.8 1.3 shard_map.140
  (82 shorter events, 4.6 us)
Async XLA Ops:
  3.0 7.9 %collective-permute-start = (bf16[32,3584]{1,0:T(8,128)(2,1)}, bf16[32,3584]{1,0:T(8,128)(2,1)S(1)}, u32[]{:S(2)}, u32[]{:S(2)}) collective-permute-start(bf16[32,3584]{1,0:T(8,128)(2,1)} %get-tuple-element.46), channel_id=1, source_target_pairs={{0,17},{1,16},{2,19},{3,18},{4,21},{5,20},{6,23},{7,22},{8,25},{9,... | collective-permute-start | bytes 688136 | tf_op jit(solution)/shard_map/ppermute | solution.py:78
  6.3 70.8 %collective-permute-start.9 = (bf16[256,3584]{1,0:T(8,128)(2,1)}, bf16[256,3584]{1,0:T(8,128)(2,1)S(1)}, u32[]{:S(2)}, u32[]{:S(2)}) collective-permute-start(bf16[256,3584]{1,0:T(8,128)(2,1)} %bitcast.33), channel_id=1, source_target_pairs={{0,1},{1,0},{2,3},{3,2},{4,5},{5,4},{6,7},{7,6},{8,9},{9,8},{10,11... | collective-permute-start | bytes 5505032 | tf_op jit(solution)/shard_map/ppermute | solution.py:78
  10.9 9.3 %copy-start.5 = (bf16[32,3584]{1,0:T(8,128)(2,1)}, bf16[32,3584]{1,0:T(8,128)(2,1)S(1)}, u32[]{:S(2)}) copy-start(bf16[32,3584]{1,0:T(8,128)(2,1)S(1)} %collective-permute-done.refs_5_.refs_1_) | copy-start | bytes 688132
  10.9 1.0 copy-start.7
  12.0 13.7 %collective-permute-start.2 = (bf16[16,3584]{1,0:T(8,128)(2,1)S(1)}, bf16[16,3584]{1,0:T(8,128)(2,1)S(1)}, u32[]{:S(2)}, u32[]{:S(2)}) collective-permute-start(bf16[16,3584]{1,0:T(8,128)(2,1)S(1)} %get-tuple-element.51), channel_id=1, source_target_pairs={{0,4},{1,5},{2,14},{3,15},{4,8},{5,9},{6,2},{7,3},{8,12},{9,13},{1... | collective-permute-start | bytes 344072 | tf_op jit(solution)/shard_map/ppermute | solution.py:78
  15.9 9.8 %collective-permute-start.3 = (bf16[16,3584]{1,0:T(8,128)(2,1)S(1)}, bf16[16,3584]{1,0:T(8,128)(2,1)S(1)}, u32[]{:S(2)}, u32[]{:S(2)}) collective-permute-start(bf16[16,3584]{1,0:T(8,128)(2,1)S(1)} %get-tuple-element.52), channel_id=1, source_target_pairs={{0,14},{1,15},{2,4},{3,5},{4,2},{5,3},{6,8},{7,9},{8,6},{9,7},{10,... | collective-permute-start | bytes 344072 | tf_op jit(solution)/shard_map/ppermute | solution.py:78
  19.6 9.2 %collective-permute-start.4 = (bf16[16,3584]{1,0:T(8,128)(2,1)S(1)}, bf16[16,3584]{1,0:T(8,128)(2,1)S(1)}, u32[]{:S(2)}, u32[]{:S(2)}) collective-permute-start(bf16[16,3584]{1,0:T(8,128)(2,1)S(1)} %get-tuple-element.53), channel_id=1, source_target_pairs={{0,10},{1,11},{2,8},{3,9},{4,14},{5,15},{6,12},{7,13},{8,2},{9,3},... | collective-permute-start | bytes 344072 | tf_op jit(solution)/shard_map/ppermute | solution.py:78
  23.2 11.3 %collective-permute-start.1 = (bf16[64,3584]{1,0:T(8,128)(2,1)}, bf16[64,3584]{1,0:T(8,128)(2,1)S(1)}, u32[]{:S(2)}, u32[]{:S(2)}) collective-permute-start(bf16[64,3584]{1,0:T(8,128)(2,1)} %get-tuple-element.48), channel_id=1, source_target_pairs={{0,17},{1,16},{2,19},{3,18},{4,21},{5,20},{6,23},{7,22},{8,25},{9,... | collective-permute-start | bytes 1376264 | tf_op jit(solution)/shard_map/ppermute | solution.py:78
  25.7 14.9 %copy-start.1 = (bf16[1,3584,256]{2,1,0:T(8,128)(2,1)S(1)}, bf16[1,3584,256]{2,1,0:T(8,128)(2,1)}, u32[]{:S(2)}) copy-start(bf16[1,3584,256]{2,1,0:T(8,128)(2,1)} %param.18) | copy-start | bytes 5505028
  25.7 14.9 %copy-start = (bf16[1,3584,256]{2,1,0:T(8,128)(2,1)S(1)}, bf16[1,3584,256]{2,1,0:T(8,128)(2,1)}, u32[]{:S(2)}) copy-start(bf16[1,3584,256]{2,1,0:T(8,128)(2,1)} %param.17) | copy-start | bytes 5505028
  28.8 11.6 %collective-permute-start.12 = (bf16[64,3584]{1,0:T(8,128)(2,1)S(1)}, bf16[64,3584]{1,0:T(8,128)(2,1)S(1)}, u32[]{:S(2)}, u32[]{:S(2)}) collective-permute-start(bf16[64,3584]{1,0:T(8,128)(2,1)S(1)} %get-tuple-element.103.refs_2_), channel_id=1, source_target_pairs={{0,2},{1,3},{2,0},{3,1},{4,6},{5,7},{6,4},{7,5},{8,10},{9,11},{10,... | collective-permute-start | bytes 1376264 | tf_op jit(solution)/shard_map/ppermute | solution.py:78
  34.5 1.0 copy-start.6
  35.6 13.4 %collective-permute-start.5 = (bf16[32,3584]{1,0:T(8,128)(2,1)S(1)}, bf16[32,3584]{1,0:T(8,128)(2,1)S(1)}, u32[]{:S(2)}, u32[]{:S(2)}) collective-permute-start(bf16[32,3584]{1,0:T(8,128)(2,1)S(1)} %get-tuple-element.55), channel_id=1, source_target_pairs={{0,4},{1,5},{2,14},{3,15},{4,8},{5,9},{6,2},{7,3},{8,12},{9,13},{1... | collective-permute-start | bytes 688136 | tf_op jit(solution)/shard_map/ppermute | solution.py:78
  37.2 11.8 %collective-permute-start.6 = (bf16[32,3584]{1,0:T(8,128)(2,1)S(1)}, bf16[32,3584]{1,0:T(8,128)(2,1)S(1)}, u32[]{:S(2)}, u32[]{:S(2)}) collective-permute-start(bf16[32,3584]{1,0:T(8,128)(2,1)S(1)} %get-tuple-element.56), channel_id=1, source_target_pairs={{0,14},{1,15},{2,4},{3,5},{4,2},{5,3},{6,8},{7,9},{8,6},{9,7},{10,... | collective-permute-start | bytes 688136 | tf_op jit(solution)/shard_map/ppermute | solution.py:78
  39.6 18.7 %collective-permute-start.7 = (bf16[32,3584]{1,0:T(8,128)(2,1)S(1)}, bf16[32,3584]{1,0:T(8,128)(2,1)S(1)}, u32[]{:S(2)}, u32[]{:S(2)}) collective-permute-start(bf16[32,3584]{1,0:T(8,128)(2,1)S(1)} %get-tuple-element.57), channel_id=1, source_target_pairs={{0,10},{1,11},{2,8},{3,9},{4,14},{5,15},{6,12},{7,13},{8,2},{9,3},... | collective-permute-start | bytes 688136 | tf_op jit(solution)/shard_map/ppermute | solution.py:78
  40.5 26.3 %collective-permute-start.13 = (bf16[128,3584]{1,0:T(8,128)(2,1)S(1)}, bf16[128,3584]{1,0:T(8,128)(2,1)S(1)}, u32[]{:S(2)}, u32[]{:S(2)}) collective-permute-start(bf16[128,3584]{1,0:T(8,128)(2,1)S(1)} %constant_dynamic-update-slice_fusion.9.refs_0_), channel_id=1, source_target_pairs={{0,1},{1,0},{2,3},{3,2},{4,5},{5,4},{6,7},{7,6},{8,9},{9,8},{10,11... | collective-permute-start | bytes 2752520 | tf_op jit(solution)/shard_map/ppermute | solution.py:78
  58.3 13.5 %collective-permute-start.19 = (bf16[64,3584]{1,0:T(8,128)(2,1)S(1)}, bf16[64,3584]{1,0:T(8,128)(2,1)S(1)}, u32[]{:S(2)}, u32[]{:S(2)}) collective-permute-start(bf16[64,3584]{1,0:T(8,128)(2,1)S(1)} %pad_maximum_fusion.1.refs_0_), channel_id=1, source_target_pairs={{0,2},{1,3},{2,0},{3,1},{4,6},{5,7},{6,4},{7,5},{8,10},{9,11},{10,... | collective-permute-start | bytes 1376264 | tf_op jit(solution)/shard_map/ppermute | solution.py:78
  58.4 9.2 %copy-start.3 = (bf16[1,128,3584]{2,1,0:T(8,128)(2,1)S(1)}, bf16[1,128,3584]{2,1,0:T(8,128)(2,1)}, u32[]{:S(2)}) copy-start(bf16[1,128,3584]{2,1,0:T(8,128)(2,1)} %param.16) | copy-start | bytes 2752516
  58.4 21.4 %collective-permute-start.8 = (bf16[64,3584]{1,0:T(8,128)(2,1)S(1)}, bf16[64,3584]{1,0:T(8,128)(2,1)S(1)}, u32[]{:S(2)}, u32[]{:S(2)}) collective-permute-start(bf16[64,3584]{1,0:T(8,128)(2,1)S(1)} %pad_maximum_fusion), channel_id=1, source_target_pairs={{0,2},{1,3},{2,0},{3,1},{4,6},{5,7},{6,4},{7,5},{8,10},{9,11},{10,... | collective-permute-start | bytes 1376264 | tf_op jit(solution)/shard_map/ppermute | solution.py:78
  67.4 5.9 %copy-start.9 = (bf16[128,128]{1,0:T(8,128)(2,1)S(1)}, bf16[128,128]{1,0:T(8,128)(2,1)}, u32[]{:S(2)}) copy-start(bf16[128,128]{1,0:T(8,128)(2,1)} %get-tuple-element.66.refs_0_) | copy-start | bytes 98308
  67.4 9.7 %copy-start.2 = (bf16[1,256,3584]{2,1,0:T(8,128)(2,1)S(1)}, bf16[1,256,3584]{2,1,0:T(8,128)(2,1)}, u32[]{:S(2)}) copy-start(bf16[1,256,3584]{2,1,0:T(8,128)(2,1)} %param.19) | copy-start | bytes 5505028
  67.5 4.4 %collective-permute-start.14 = (bf16[128,256]{1,0:T(8,128)(2,1)S(1)}, bf16[128,256]{1,0:T(8,128)(2,1)S(1)}, u32[]{:S(2)}, u32[]{:S(2)}) collective-permute-start(bf16[128,256]{1,0:T(8,128)(2,1)S(1)} %shard_map.121), channel_id=1, source_target_pairs={{0,1},{1,0},{2,3},{3,2},{4,5},{5,4},{6,7},{7,6},{8,9},{9,8},{10,11... | collective-permute-start | bytes 196616 | tf_op jit(solution)/shard_map/ppermute | solution.py:78
  67.7 23.1 %collective-permute-start.22 = (bf16[128,3584]{1,0:T(8,128)(2,1)S(1)}, bf16[128,3584]{1,0:T(8,128)(2,1)S(1)}, u32[]{:S(2)}, u32[]{:S(2)}) collective-permute-start(bf16[128,3584]{1,0:T(8,128)(2,1)S(1)} %shard_map.127), channel_id=1, source_target_pairs={{32,0},{33,1},{34,2},{35,3},{36,4},{37,5},{38,6},{39,7},{40,8},{41... | collective-permute-start | bytes 2752520 | tf_op jit(solution)/shard_map/ppermute | solution.py:89
  71.9 19.5 %collective-permute-start.21 = (bf16[128,3584]{1,0:T(8,128)(2,1)S(1)}, bf16[128,3584]{1,0:T(8,128)(2,1)}, u32[]{:S(2)}, u32[]{:S(2)}) collective-permute-start(bf16[128,3584]{1,0:T(8,128)(2,1)S(1)} %shard_map.124.refs_0_), channel_id=1, source_target_pairs={{0,1},{1,0},{2,3},{3,2},{4,5},{5,4},{6,7},{7,6},{8,9},{9,8},{10,11... | collective-permute-start | bytes 2752520 | tf_op jit(solution)/shard_map/ppermute | solution.py:78
  73.3 11.5 %collective-permute-start.20 = (bf16[128,128]{1,0:T(8,128)(2,1)S(1)}, bf16[128,128]{1,0:T(8,128)(2,1)S(1)}, u32[]{:S(2)}, u32[]{:S(2)}) collective-permute-start(bf16[128,128]{1,0:T(8,128)(2,1)S(1)} %shard_map.125), channel_id=1, source_target_pairs={{32,0},{33,1},{34,2},{35,3},{36,4},{37,5},{38,6},{39,7},{40,8},{41... | collective-permute-start | bytes 98312 | tf_op jit(solution)/shard_map/ppermute | solution.py:89
  77.8 12.9 %collective-permute-start.15 = (bf16[64,3584]{1,0:T(8,128)(2,1)S(1)}, bf16[64,3584]{1,0:T(8,128)(2,1)S(1)}, u32[]{:S(2)}, u32[]{:S(2)}) collective-permute-start(bf16[64,3584]{1,0:T(8,128)(2,1)S(1)} %get-tuple-element.61), channel_id=1, source_target_pairs={{0,2},{1,3},{2,0},{3,1},{4,6},{5,7},{6,4},{7,5},{8,10},{9,11},{10,... | collective-permute-start | bytes 1376264 | tf_op jit(solution)/shard_map/ppermute | solution.py:78
  79.8 3.1 %copy-start.8 = (bf16[128,128]{1,0:T(8,128)(2,1)S(1)}, bf16[128,128]{1,0:T(8,128)(2,1)}, u32[]{:S(2)}) copy-start(bf16[128,128]{1,0:T(8,128)(2,1)} %get-tuple-element.59.refs_0_) | copy-start | bytes 98308
  81.1 12.1 %collective-permute-start.23 = (bf16[128,256]{1,0:T(8,128)(2,1)S(1)}, bf16[128,256]{1,0:T(8,128)(2,1)S(1)}, u32[]{:S(2)}, u32[]{:S(2)}) collective-permute-start(bf16[128,256]{1,0:T(8,128)(2,1)S(1)} %get-tuple-element.58.refs_1_), channel_id=1, source_target_pairs={{0,1},{1,0},{2,3},{3,2},{4,5},{5,4},{6,7},{7,6},{8,9},{9,8},{10,11... | collective-permute-start | bytes 196616 | tf_op jit(solution)/shard_map/ppermute | solution.py:78
  84.8 6.0 %collective-permute-start.11 = (bf16[128,128]{1,0:T(8,128)(2,1)S(1)}, bf16[128,128]{1,0:T(8,128)(2,1)S(1)}, u32[]{:S(2)}, u32[]{:S(2)}) collective-permute-start(bf16[128,128]{1,0:T(8,128)(2,1)S(1)} %shard_map.119), channel_id=1, source_target_pairs={{0,32},{1,33},{2,34},{3,35},{4,36},{5,37},{6,38},{7,39},{8,40},{9,... | collective-permute-start | bytes 98312 | tf_op jit(solution)/shard_map/ppermute | solution.py:89
  94.0 4.7 %copy-start.4 = (bf16[1,128,3584]{2,1,0:T(8,128)(2,1)S(1)}, bf16[1,128,3584]{2,1,0:T(8,128)(2,1)}, u32[]{:S(2)}) copy-start(bf16[1,128,3584]{2,1,0:T(8,128)(2,1)} %param.10) | copy-start | bytes 2752516
  94.0 11.7 %collective-permute-start.25 = (bf16[128,1792]{1,0:T(8,128)(2,1)S(1)}, bf16[128,1792]{1,0:T(8,128)(2,1)S(1)}, u32[]{:S(2)}, u32[]{:S(2)}) collective-permute-start(bf16[128,1792]{1,0:T(8,128)(2,1)S(1)} %get-tuple-element.78), channel_id=1, source_target_pairs={{0,2},{1,3},{2,0},{3,1},{4,6},{5,7},{6,4},{7,5},{8,10},{9,11},{10,... | collective-permute-start | bytes 1376264 | tf_op jit(solution)/shard_map/ppermute | solution.py:78
  96.3 9.7 %collective-permute-start.24 = (bf16[128,1792]{1,0:T(8,128)(2,1)S(1)}, bf16[128,1792]{1,0:T(8,128)(2,1)S(1)}, u32[]{:S(2)}, u32[]{:S(2)}) collective-permute-start(bf16[128,1792]{1,0:T(8,128)(2,1)S(1)} %get-tuple-element.75), channel_id=1, source_target_pairs={{0,1},{1,0},{2,3},{3,2},{4,5},{5,4},{6,7},{7,6},{8,9},{9,8},{10,11... | collective-permute-start | bytes 1376264 | tf_op jit(solution)/shard_map/ppermute | solution.py:78
  98.8 43.5 %collective-permute-start.10 = (bf16[128,3584]{1,0:T(8,128)(2,1)S(1)}, bf16[128,3584]{1,0:T(8,128)(2,1)S(1)}, u32[]{:S(2)}, u32[]{:S(2)}) collective-permute-start(bf16[128,3584]{1,0:T(8,128)(2,1)S(1)} %shard_map.118), channel_id=1, source_target_pairs={{0,32},{1,33},{2,34},{3,35},{4,36},{5,37},{6,38},{7,39},{8,40},{9,... | collective-permute-start | bytes 2752520 | tf_op jit(solution)/shard_map/ppermute | solution.py:89
  105.8 8.7 %collective-permute-start.29 = (bf16[64,1792]{1,0:T(8,128)(2,1)S(1)}, bf16[64,1792]{1,0:T(8,128)(2,1)S(1)}, u32[]{:S(2)}, u32[]{:S(2)}) collective-permute-start(bf16[64,1792]{1,0:T(8,128)(2,1)S(1)} %get-tuple-element.79.refs_5_), channel_id=1, source_target_pairs={{0,1},{1,0},{2,3},{3,2},{4,5},{5,4},{6,7},{7,6},{8,9},{9,8},{10,11... | collective-permute-start | bytes 688136 | tf_op jit(solution)/shard_map/ppermute | solution.py:78
  106.1 13.3 %collective-permute-start.28 = (bf16[64,1792]{1,0:T(8,128)(2,1)S(1)}, bf16[64,1792]{1,0:T(8,128)(2,1)S(1)}, u32[]{:S(2)}, u32[]{:S(2)}) collective-permute-start(bf16[64,1792]{1,0:T(8,128)(2,1)S(1)} %get-tuple-element.76.refs_4_), channel_id=1, source_target_pairs={{0,2},{1,3},{2,0},{3,1},{4,6},{5,7},{6,4},{7,5},{8,10},{9,11},{10,... | collective-permute-start | bytes 688136 | tf_op jit(solution)/shard_map/ppermute | solution.py:78
  107.0 12.6 %collective-permute-start.16 = (bf16[16,3584]{1,0:T(8,128)(2,1)S(1)}, bf16[16,3584]{1,0:T(8,128)(2,1)S(1)}, u32[]{:S(2)}, u32[]{:S(2)}) collective-permute-start(bf16[16,3584]{1,0:T(8,128)(2,1)S(1)} %get-tuple-element.63), channel_id=1, source_target_pairs={{4,0},{5,1},{14,2},{15,3},{8,4},{9,5},{2,6},{3,7},{12,8},{13,9},{6... | collective-permute-start | bytes 344072 | tf_op jit(solution)/shard_map/ppermute | solution.py:78
  114.5 8.2 %collective-permute-start.17 = (bf16[16,3584]{1,0:T(8,128)(2,1)S(1)}, bf16[16,3584]{1,0:T(8,128)(2,1)S(1)}, u32[]{:S(2)}, u32[]{:S(2)}) collective-permute-start(bf16[16,3584]{1,0:T(8,128)(2,1)S(1)} %get-tuple-element.64), channel_id=1, source_target_pairs={{14,0},{15,1},{4,2},{5,3},{2,4},{3,5},{8,6},{9,7},{6,8},{7,9},{12,... | collective-permute-start | bytes 344072 | tf_op jit(solution)/shard_map/ppermute | solution.py:78
  114.6 8.5 %collective-permute-start.18 = (bf16[16,3584]{1,0:T(8,128)(2,1)S(1)}, bf16[16,3584]{1,0:T(8,128)(2,1)S(1)}, u32[]{:S(2)}, u32[]{:S(2)}) collective-permute-start(bf16[16,3584]{1,0:T(8,128)(2,1)S(1)} %get-tuple-element.65), channel_id=1, source_target_pairs={{10,0},{11,1},{8,2},{9,3},{14,4},{15,5},{12,6},{13,7},{2,8},{3,9},... | collective-permute-start | bytes 344072 | tf_op jit(solution)/shard_map/ppermute | solution.py:78
  119.5 14.5 %collective-permute-start.30 = (bf16[16,3584]{1,0:T(8,128)(2,1)S(1)}, bf16[16,3584]{1,0:T(8,128)(2,1)S(1)}, u32[]{:S(2)}, u32[]{:S(2)}) collective-permute-start(bf16[16,3584]{1,0:T(8,128)(2,1)S(1)} %get-tuple-element.86), channel_id=1, source_target_pairs={{4,0},{5,1},{14,2},{15,3},{8,4},{9,5},{2,6},{3,7},{12,8},{13,9},{6... | collective-permute-start | bytes 344072 | tf_op jit(solution)/shard_map/ppermute | solution.py:78
  119.6 17.0 %collective-permute-start.31 = (bf16[16,3584]{1,0:T(8,128)(2,1)S(1)}, bf16[16,3584]{1,0:T(8,128)(2,1)S(1)}, u32[]{:S(2)}, u32[]{:S(2)}) collective-permute-start(bf16[16,3584]{1,0:T(8,128)(2,1)S(1)} %get-tuple-element.87), channel_id=1, source_target_pairs={{14,0},{15,1},{4,2},{5,3},{2,4},{3,5},{8,6},{9,7},{6,8},{7,9},{12,... | collective-permute-start | bytes 344072 | tf_op jit(solution)/shard_map/ppermute | solution.py:78
  122.7 13.9 %collective-permute-start.32 = (bf16[16,3584]{1,0:T(8,128)(2,1)S(1)}, bf16[16,3584]{1,0:T(8,128)(2,1)S(1)}, u32[]{:S(2)}, u32[]{:S(2)}) collective-permute-start(bf16[16,3584]{1,0:T(8,128)(2,1)S(1)} %get-tuple-element.88), channel_id=1, source_target_pairs={{10,0},{11,1},{8,2},{9,3},{14,4},{15,5},{12,6},{13,7},{2,8},{3,9},... | collective-permute-start | bytes 344072 | tf_op jit(solution)/shard_map/ppermute | solution.py:78
  123.1 19.1 %collective-permute-start.26 = (bf16[32,3584]{1,0:T(8,128)(2,1)S(1)}, bf16[32,3584]{1,0:T(8,128)(2,1)S(1)}, u32[]{:S(2)}, u32[]{:S(2)}) collective-permute-start(bf16[32,3584]{1,0:T(8,128)(2,1)S(1)} %get-tuple-element.80), channel_id=1, source_target_pairs={{0,32},{1,33},{2,34},{3,35},{4,36},{5,37},{6,38},{7,39},{8,40},{9,... | collective-permute-start | bytes 688136 | tf_op jit(solution)/shard_map/ppermute | solution.py:89
  134.0 11.3 %collective-permute-start.27 = (bf16[32,3584]{1,0:T(8,128)(2,1)S(1)}, bf16[32,3584]{1,0:T(8,128)(2,1)S(1)}, u32[]{:S(2)}, u32[]{:S(2)}) collective-permute-start(bf16[32,3584]{1,0:T(8,128)(2,1)S(1)} %get-tuple-element.81), channel_id=1, source_target_pairs={{0,49},{1,48},{2,51},{3,50},{4,53},{5,52},{6,55},{7,54},{8,57},{9,... | collective-permute-start | bytes 688136 | tf_op jit(solution)/shard_map/ppermute | solution.py:89
  136.7 9.9 %collective-permute-start.33 = (bf16[32,3584]{1,0:T(8,128)(2,1)S(1)}, bf16[32,3584]{1,0:T(8,128)(2,1)S(1)}, u32[]{:S(2)}, u32[]{:S(2)}) collective-permute-start(bf16[32,3584]{1,0:T(8,128)(2,1)S(1)} %shard_map.139), channel_id=1, source_target_pairs={{32,0},{33,1},{34,2},{35,3},{36,4},{37,5},{38,6},{39,7},{40,8},{41... | collective-permute-start | bytes 688136 | tf_op jit(solution)/shard_map/ppermute | solution.py:89
  139.4 11.4 %collective-permute-start.34 = (bf16[32,3584]{1,0:T(8,128)(2,1)S(1)}, bf16[32,3584]{1,0:T(8,128)(2,1)S(1)}, u32[]{:S(2)}, u32[]{:S(2)}) collective-permute-start(bf16[32,3584]{1,0:T(8,128)(2,1)S(1)} %shard_map.138.refs_4_), channel_id=1, source_target_pairs={{32,17},{33,16},{34,19},{35,18},{36,21},{37,20},{38,23},{39,22},{4... | collective-permute-start | bytes 688136 | tf_op jit(solution)/shard_map/ppermute | solution.py:89

commit v5 on v4

--- a/solution.py
+++ b/solution.py
@@ -276,6 +276,35 @@
     return call(join_body, [shape(rows, parts[0].shape[1])], parts, after=after)[0]
 
 
+def combine_call(base, comb, own, far, mark):
+    rows, width = base.shape
+    part = width // 2
+
+    def run(base_ref, comb_ref, own_ref, far_ref, mark_ref, out_ref):
+        combine_body(base_ref, comb_ref, own_ref, far_ref, out_ref)
+
+    def columns(count):
+        return pl.BlockSpec((count, part), lambda i: (0, i))
+
+    return pl.pallas_call(
+        run,
+        grid=(2,),
+        out_shape=shape(rows, width),
+        in_specs=[
+            columns(rows),
+            pl.BlockSpec(comb.shape, lambda i: (0, 0)),
+            columns(HALF),
+            columns(HALF),
+            pl.BlockSpec(memory_space=pl.ANY),
+        ],
+        out_specs=columns(rows),
+        compiler_params=pltpu.CompilerParams(vmem_limit_bytes=48 * 1024 * 1024),
+        cost_estimate=pl.CostEstimate(
+            flops=0, bytes_accessed=6 * rows * width, transcendentals=0
+        ),
+    )(base, comb, own, far, mark)
+
+
 def shifts(blocks, back):
     a, b, c = SHIFT_A, SHIFT_B, SHIFT_C
     if back:
@@ -391,12 +420,7 @@
         functools.partial(side_body, 0), [shape(HALF, width)], blocks, after=(far,)
     )
     far, own = relay(far, ACROSS_XHI, -1), relay(own, STAY, -1)
-    (bwd_out,) = call(
-        combine_body,
-        [shape(tokens, width)],
-        [bbase, bcomb, own, far],
-        after=(mark,),
-    )
+    bwd_out = combine_call(bbase, bcomb, own, far, mark)
     return fwd_out[None], bwd_out[None]
 
 

time: 153 us -> 153 us (level)
    pallas_call x26 -> x25, Pallas kernels: 14.5 us -> 13.2 us  [call(): pl.pallas_call(run, out_shape=tuple(outs), in_specs=specs, out_specs=tupl...]
where the time goes in v5:
time: 153 us; the launch traced here: 152 us
  starting transfers between devices  84.5 us (55%)
  waiting for transfers between devices  48.2 us (32%)
  Pallas kernels  16 us (10%)
  local copies, waits for them, and re-layouts  2.31 us (2%)
    ppermute x27, starting transfers between devices, move(): return lax.ppermute(value, ('expert', 'dp'), pairs)  48.8 us
    ppermute x27, waiting for transfers between devices, move(): return lax.ppermute(value, ('expert', 'dp'), pairs)  39.1 us
    ppermute x8, starting transfers between devices, relay(): return lax.ppermute(value, ('pipe', 'expert', 'dp'), full)  35.7 us
    pallas_call x25, Pallas kernels, call(): pl.pallas_call(run, out_shape=tuple(outs), in_specs=specs, out_specs=tupl...  13.2 us
    ppermute x8, waiting for transfers between devices, relay(): return lax.ppermute(value, ('pipe', 'expert', 'dp'), full)  9.1 us
  transfers between devices with their start and end apart: 35, of which 12 were waited for; matrix products, arithmetic and copies ran while one was open for 0% of the time, Pallas kernels for 7%

profile of v5, /device:TPU:1, one launch (start us, length us, event | category | flops | bytes accessed | tf_op | source)
XLA Modules:
  0.0 152.3 jit_solution(8237027457351193919)
XLA Ops:
  0.6 2.4 %shard_map.113 = (bf16[32,3584]{1,0:T(8,128)(2,1)}, bf16[32,3584]{1,0:T(8,128)(2,1)}, bf16[128,128]{1,0:T(8,128)(2,1)}) custom-call(s32[1]{0:T(128)} %bitcast.1.refs_0_, s32[8,128]{1,0:T(8,128)} %bitcast.42, f32[8,128]{1,0:T(8,128)} %bitcast.43, bf16[128,3584]{1,0:T(8,128)(2,1)} %bitcast.38), custom_call_target="tpu_custom_call" | custom-call | bytes 1417220 | tf_op jit(solution)/shard_map/pallas_call | solution.py:32
  3.0 3.3 %collective-permute-start = (bf16[32,3584]{1,0:T(8,128)(2,1)}, bf16[32,3584]{1,0:T(8,128)(2,1)S(1)}, u32[]{:S(2)}, u32[]{:S(2)}) collective-permute-start(bf16[32,3584]{1,0:T(8,128)(2,1)} %get-tuple-element.46), channel_id=1, source_target_pairs={{0,17},{1,16},{2,19},{3,18},{4,21},{5,20},{6,23},{7,22},{8,25},{9,... | collective-permute-start | bytes 688136 | tf_op jit(solution)/shard_map/ppermute | solution.py:78
  6.3 4.6 %collective-permute-done.refs_5_.refs_1_ = bf16[32,3584]{1,0:T(8,128)(2,1)S(1)} collective-permute-done((bf16[32,3584]{1,0:T(8,128)(2,1)}, bf16[32,3584]{1,0:T(8,128)(2,1)S(1)}, u32[]{:S(2)}, u32[]{:S(2)}) %collective-permute-start) | collective-permute-done | bytes 229408 | tf_op jit(solution)/shard_map/ppermute | solution.py:78
  10.9 1.0 copy-done.7
  12.0 3.9 %collective-permute-start.2 = (bf16[16,3584]{1,0:T(8,128)(2,1)S(1)}, bf16[16,3584]{1,0:T(8,128)(2,1)S(1)}, u32[]{:S(2)}, u32[]{:S(2)}) collective-permute-start(bf16[16,3584]{1,0:T(8,128)(2,1)S(1)} %get-tuple-element.51), channel_id=1, source_target_pairs={{0,4},{1,5},{2,14},{3,15},{4,8},{5,9},{6,2},{7,3},{8,12},{9,13},{1... | collective-permute-start | bytes 344072 | tf_op jit(solution)/shard_map/ppermute | solution.py:78
  15.9 3.8 %collective-permute-start.3 = (bf16[16,3584]{1,0:T(8,128)(2,1)S(1)}, bf16[16,3584]{1,0:T(8,128)(2,1)S(1)}, u32[]{:S(2)}, u32[]{:S(2)}) collective-permute-start(bf16[16,3584]{1,0:T(8,128)(2,1)S(1)} %get-tuple-element.52), channel_id=1, source_target_pairs={{0,14},{1,15},{2,4},{3,5},{4,2},{5,3},{6,8},{7,9},{8,6},{9,7},{10,... | collective-permute-start | bytes 344072 | tf_op jit(solution)/shard_map/ppermute | solution.py:78
  20.2 3.0 %shard_map.114 = (bf16[64,3584]{1,0:T(8,128)(2,1)}, bf16[64,3584]{1,0:T(8,128)(2,1)}, bf16[128,128]{1,0:T(8,128)(2,1)}) custom-call(s32[1]{0:T(128)} %bitcast.1.refs_0_, s32[8,128]{1,0:T(8,128)} %bitcast.44, f32[8,128]{1,0:T(8,128)} %bitcast.45, bf16[128,3584]{1,0:T(8,128)(2,1)} %bitcast.40, bf16[128,3584]{1,0:T(8,128)(2,1)} %bitcast.36, ...), custom_call_target="tpu_custom_call" | custom-call | bytes 2793476 | tf_op jit(solution)/shard_map/pallas_call | solution.py:32
  23.2 2.5 %collective-permute-start.1 = (bf16[64,3584]{1,0:T(8,128)(2,1)}, bf16[64,3584]{1,0:T(8,128)(2,1)S(1)}, u32[]{:S(2)}, u32[]{:S(2)}) collective-permute-start(bf16[64,3584]{1,0:T(8,128)(2,1)} %get-tuple-element.48), channel_id=1, source_target_pairs={{0,17},{1,16},{2,19},{3,18},{4,21},{5,20},{6,23},{7,22},{8,25},{9,... | collective-permute-start | bytes 1376264 | tf_op jit(solution)/shard_map/ppermute | solution.py:78
  25.7 3.1 %collective-permute-done.4 = bf16[16,3584]{1,0:T(8,128)(2,1)S(1)} collective-permute-done((bf16[16,3584]{1,0:T(8,128)(2,1)S(1)}, bf16[16,3584]{1,0:T(8,128)(2,1)S(1)}, u32[]{:S(2)}, u32[]{:S(2)}) %collective-permute-start.4) | collective-permute-done | bytes 114720 | tf_op jit(solution)/shard_map/ppermute | solution.py:78
  28.8 2.1 %collective-permute-start.12 = (bf16[64,3584]{1,0:T(8,128)(2,1)S(1)}, bf16[64,3584]{1,0:T(8,128)(2,1)S(1)}, u32[]{:S(2)}, u32[]{:S(2)}) collective-permute-start(bf16[64,3584]{1,0:T(8,128)(2,1)S(1)} %get-tuple-element.103.refs_2_), channel_id=1, source_target_pairs={{0,2},{1,3},{2,0},{3,1},{4,6},{5,7},{6,4},{7,5},{8,10},{9,11},{10,... | collective-permute-start | bytes 1376264 | tf_op jit(solution)/shard_map/ppermute | solution.py:78
  31.0 3.5 %collective-permute-done.1.refs_1_ = bf16[64,3584]{1,0:T(8,128)(2,1)S(1)} collective-permute-done((bf16[64,3584]{1,0:T(8,128)(2,1)}, bf16[64,3584]{1,0:T(8,128)(2,1)S(1)}, u32[]{:S(2)}, u32[]{:S(2)}) %collective-permute-start.1) | collective-permute-done | bytes 458784 | tf_op jit(solution)/shard_map/ppermute | solution.py:78
  34.5 1.0 copy-done.6
  35.6 1.6 %collective-permute-start.5 = (bf16[32,3584]{1,0:T(8,128)(2,1)S(1)}, bf16[32,3584]{1,0:T(8,128)(2,1)S(1)}, u32[]{:S(2)}, u32[]{:S(2)}) collective-permute-start(bf16[32,3584]{1,0:T(8,128)(2,1)S(1)} %get-tuple-element.55), channel_id=1, source_target_pairs={{0,4},{1,5},{2,14},{3,15},{4,8},{5,9},{6,2},{7,3},{8,12},{9,13},{1... | collective-permute-start | bytes 688136 | tf_op jit(solution)/shard_map/ppermute | solution.py:78
  37.2 2.4 %collective-permute-start.6 = (bf16[32,3584]{1,0:T(8,128)(2,1)S(1)}, bf16[32,3584]{1,0:T(8,128)(2,1)S(1)}, u32[]{:S(2)}, u32[]{:S(2)}) collective-permute-start(bf16[32,3584]{1,0:T(8,128)(2,1)S(1)} %get-tuple-element.56), channel_id=1, source_target_pairs={{0,14},{1,15},{2,4},{3,5},{4,2},{5,3},{6,8},{7,9},{8,6},{9,7},{10,... | collective-permute-start | bytes 688136 | tf_op jit(solution)/shard_map/ppermute | solution.py:78
  39.6 0.8 collective-permute-start.7
  40.6 0.7 shard_map.120.refs_3_.refs_0_.refs_1_
  41.3 7.7 %collective-permute-done.5 = bf16[32,3584]{1,0:T(8,128)(2,1)S(1)} collective-permute-done((bf16[32,3584]{1,0:T(8,128)(2,1)S(1)}, bf16[32,3584]{1,0:T(8,128)(2,1)S(1)}, u32[]{:S(2)}, u32[]{:S(2)}) %collective-permute-start.5) | collective-permute-done | bytes 229408 | tf_op jit(solution)/shard_map/ppermute | solution.py:78
  49.0 9.2 %collective-permute-done.7 = bf16[32,3584]{1,0:T(8,128)(2,1)S(1)} collective-permute-done((bf16[32,3584]{1,0:T(8,128)(2,1)S(1)}, bf16[32,3584]{1,0:T(8,128)(2,1)S(1)}, u32[]{:S(2)}, u32[]{:S(2)}) %collective-permute-start.7) | collective-permute-done | bytes 229408 | tf_op jit(solution)/shard_map/ppermute | solution.py:78
  58.4 1.5 %collective-permute-start.8 = (bf16[64,3584]{1,0:T(8,128)(2,1)S(1)}, bf16[64,3584]{1,0:T(8,128)(2,1)S(1)}, u32[]{:S(2)}, u32[]{:S(2)}) collective-permute-start(bf16[64,3584]{1,0:T(8,128)(2,1)S(1)} %pad_maximum_fusion), channel_id=1, source_target_pairs={{0,2},{1,3},{2,0},{3,1},{4,6},{5,7},{6,4},{7,5},{8,10},{9,11},{10,... | collective-permute-start | bytes 1376264 | tf_op jit(solution)/shard_map/ppermute | solution.py:78
  60.0 6.8 %collective-permute-done.13.refs_0_ = bf16[128,3584]{1,0:T(8,128)(2,1)S(1)} collective-permute-done((bf16[128,3584]{1,0:T(8,128)(2,1)S(1)}, bf16[128,3584]{1,0:T(8,128)(2,1)S(1)}, u32[]{:S(2)}, u32[]{:S(2)}) %collective-permute-start.13) | collective-permute-done | bytes 917536 | tf_op jit(solution)/shard_map/ppermute | solution.py:78
  67.7 4.1 %collective-permute-start.22 = (bf16[128,3584]{1,0:T(8,128)(2,1)S(1)}, bf16[128,3584]{1,0:T(8,128)(2,1)S(1)}, u32[]{:S(2)}, u32[]{:S(2)}) collective-permute-start(bf16[128,3584]{1,0:T(8,128)(2,1)S(1)} %shard_map.127), channel_id=1, source_target_pairs={{32,0},{33,1},{34,2},{35,3},{36,4},{37,5},{38,6},{39,7},{40,8},{41... | collective-permute-start | bytes 2752520 | tf_op jit(solution)/shard_map/ppermute | solution.py:89
  71.9 1.4 collective-permute-start.21
  73.3 3.8 %collective-permute-start.20 = (bf16[128,128]{1,0:T(8,128)(2,1)S(1)}, bf16[128,128]{1,0:T(8,128)(2,1)S(1)}, u32[]{:S(2)}, u32[]{:S(2)}) collective-permute-start(bf16[128,128]{1,0:T(8,128)(2,1)S(1)} %shard_map.125), channel_id=1, source_target_pairs={{32,0},{33,1},{34,2},{35,3},{36,4},{37,5},{38,6},{39,7},{40,8},{41... | collective-permute-start | bytes 98312 | tf_op jit(solution)/shard_map/ppermute | solution.py:89
  77.8 2.0 %collective-permute-start.15 = (bf16[64,3584]{1,0:T(8,128)(2,1)S(1)}, bf16[64,3584]{1,0:T(8,128)(2,1)S(1)}, u32[]{:S(2)}, u32[]{:S(2)}) collective-permute-start(bf16[64,3584]{1,0:T(8,128)(2,1)S(1)} %get-tuple-element.61), channel_id=1, source_target_pairs={{0,2},{1,3},{2,0},{3,1},{4,6},{5,7},{6,4},{7,5},{8,10},{9,11},{10,... | collective-permute-start | bytes 1376264 | tf_op jit(solution)/shard_map/ppermute | solution.py:78
  79.8 1.3 shard_map.117
  81.1 1.8 %collective-permute-start.23 = (bf16[128,256]{1,0:T(8,128)(2,1)S(1)}, bf16[128,256]{1,0:T(8,128)(2,1)S(1)}, u32[]{:S(2)}, u32[]{:S(2)}) collective-permute-start(bf16[128,256]{1,0:T(8,128)(2,1)S(1)} %get-tuple-element.58.refs_1_), channel_id=1, source_target_pairs={{0,1},{1,0},{2,3},{3,2},{4,5},{5,4},{6,7},{7,6},{8,9},{9,8},{10,11... | collective-permute-start | bytes 196616 | tf_op jit(solution)/shard_map/ppermute | solution.py:78
  82.9 1.9 %collective-permute-done.20.refs_3_.comb_ref = bf16[128,128]{1,0:T(8,128)(2,1)S(1)} collective-permute-done((bf16[128,128]{1,0:T(8,128)(2,1)S(1)}, bf16[128,128]{1,0:T(8,128)(2,1)S(1)}, u32[]{:S(2)}, u32[]{:S(2)}) %collective-permute-start.20) | collective-permute-done | bytes 32800 | tf_op jit(solution)/shard_map/ppermute | solution.py:89
  84.8 1.9 %collective-permute-start.11 = (bf16[128,128]{1,0:T(8,128)(2,1)S(1)}, bf16[128,128]{1,0:T(8,128)(2,1)S(1)}, u32[]{:S(2)}, u32[]{:S(2)}) collective-permute-start(bf16[128,128]{1,0:T(8,128)(2,1)S(1)} %shard_map.119), channel_id=1, source_target_pairs={{0,32},{1,33},{2,34},{3,35},{4,36},{5,37},{6,38},{7,39},{8,40},{9,... | collective-permute-start | bytes 98312 | tf_op jit(solution)/shard_map/ppermute | solution.py:89
  86.7 0.7 shard_map.126
  87.4 3.3 %collective-permute-done.15.refs_1_ = bf16[64,3584]{1,0:T(8,128)(2,1)S(1)} collective-permute-done((bf16[64,3584]{1,0:T(8,128)(2,1)S(1)}, bf16[64,3584]{1,0:T(8,128)(2,1)S(1)}, u32[]{:S(2)}, u32[]{:S(2)}) %collective-permute-start.15) | collective-permute-done | bytes 458784 | tf_op jit(solution)/shard_map/ppermute | solution.py:78
  91.4 1.8 %shard_map.128 = (f32[128,256]{1,0:T(8,128)S(1)}, f32[128,256]{1,0:T(8,128)S(1)}) custom-call(bf16[128,3584]{1,0:T(8,128)(2,1)} %collective-permute-done.21.refs_0_, bf16[3584,256]{1,0:T(8,128)(2,1)S(1)} %bitcast.24, bf16[3584,256]{1,0:T(8,128)(2,1)S(1)} %bitcast.30, bf16[16,3584]{1,0:T(8,128)(2,1)S(1)} %get-tuple-element.62.refs_3_.refs_0_, ...), custom_call_target="tpu_custom_call" | custom-call | flops 469762048 | bytes 4849664 | tf_op jit(solution)/shard_map/pallas_call | solution.py:32
  93.3 0.7 shard_map.132
  94.0 1.6 %collective-permute-start.25 = (bf16[128,1792]{1,0:T(8,128)(2,1)S(1)}, bf16[128,1792]{1,0:T(8,128)(2,1)S(1)}, u32[]{:S(2)}, u32[]{:S(2)}) collective-permute-start(bf16[128,1792]{1,0:T(8,128)(2,1)S(1)} %get-tuple-element.78), channel_id=1, source_target_pairs={{0,2},{1,3},{2,0},{3,1},{4,6},{5,7},{6,4},{7,5},{8,10},{9,11},{10,... | collective-permute-start | bytes 1376264 | tf_op jit(solution)/shard_map/ppermute | solution.py:78
  95.6 0.7 shard_map.130
  96.3 2.4 %collective-permute-start.24 = (bf16[128,1792]{1,0:T(8,128)(2,1)S(1)}, bf16[128,1792]{1,0:T(8,128)(2,1)S(1)}, u32[]{:S(2)}, u32[]{:S(2)}) collective-permute-start(bf16[128,1792]{1,0:T(8,128)(2,1)S(1)} %get-tuple-element.75), channel_id=1, source_target_pairs={{0,1},{1,0},{2,3},{3,2},{4,5},{5,4},{6,7},{7,6},{8,9},{9,8},{10,11... | collective-permute-start | bytes 1376264 | tf_op jit(solution)/shard_map/ppermute | solution.py:78
  98.8 6.9 %collective-permute-start.10 = (bf16[128,3584]{1,0:T(8,128)(2,1)S(1)}, bf16[128,3584]{1,0:T(8,128)(2,1)S(1)}, u32[]{:S(2)}, u32[]{:S(2)}) collective-permute-start(bf16[128,3584]{1,0:T(8,128)(2,1)S(1)} %shard_map.118), channel_id=1, source_target_pairs={{0,32},{1,33},{2,34},{3,35},{4,36},{5,37},{6,38},{7,39},{8,40},{9,... | collective-permute-start | bytes 2752520 | tf_op jit(solution)/shard_map/ppermute | solution.py:89
  106.1 0.9 collective-permute-start.28
  107.0 7.6 %collective-permute-start.16 = (bf16[16,3584]{1,0:T(8,128)(2,1)S(1)}, bf16[16,3584]{1,0:T(8,128)(2,1)S(1)}, u32[]{:S(2)}, u32[]{:S(2)}) collective-permute-start(bf16[16,3584]{1,0:T(8,128)(2,1)S(1)} %get-tuple-element.63), channel_id=1, source_target_pairs={{4,0},{5,1},{14,2},{15,3},{8,4},{9,5},{2,6},{3,7},{12,8},{13,9},{6... | collective-permute-start | bytes 344072 | tf_op jit(solution)/shard_map/ppermute | solution.py:78
  114.6 4.9 %collective-permute-start.18 = (bf16[16,3584]{1,0:T(8,128)(2,1)S(1)}, bf16[16,3584]{1,0:T(8,128)(2,1)S(1)}, u32[]{:S(2)}, u32[]{:S(2)}) collective-permute-start(bf16[16,3584]{1,0:T(8,128)(2,1)S(1)} %get-tuple-element.65), channel_id=1, source_target_pairs={{10,0},{11,1},{8,2},{9,3},{14,4},{15,5},{12,6},{13,7},{2,8},{3,9},... | collective-permute-start | bytes 344072 | tf_op jit(solution)/shard_map/ppermute | solution.py:78
  119.6 3.1 %collective-permute-start.31 = (bf16[16,3584]{1,0:T(8,128)(2,1)S(1)}, bf16[16,3584]{1,0:T(8,128)(2,1)S(1)}, u32[]{:S(2)}, u32[]{:S(2)}) collective-permute-start(bf16[16,3584]{1,0:T(8,128)(2,1)S(1)} %get-tuple-element.87), channel_id=1, source_target_pairs={{14,0},{15,1},{4,2},{5,3},{2,4},{3,5},{8,6},{9,7},{6,8},{7,9},{12,... | collective-permute-start | bytes 344072 | tf_op jit(solution)/shard_map/ppermute | solution.py:78
  123.1 10.9 %collective-permute-start.26 = (bf16[32,3584]{1,0:T(8,128)(2,1)S(1)}, bf16[32,3584]{1,0:T(8,128)(2,1)S(1)}, u32[]{:S(2)}, u32[]{:S(2)}) collective-permute-start(bf16[32,3584]{1,0:T(8,128)(2,1)S(1)} %get-tuple-element.80), channel_id=1, source_target_pairs={{0,32},{1,33},{2,34},{3,35},{4,36},{5,37},{6,38},{7,39},{8,40},{9,... | collective-permute-start | bytes 688136 | tf_op jit(solution)/shard_map/ppermute | solution.py:89
  134.0 2.7 %collective-permute-start.27 = (bf16[32,3584]{1,0:T(8,128)(2,1)S(1)}, bf16[32,3584]{1,0:T(8,128)(2,1)S(1)}, u32[]{:S(2)}, u32[]{:S(2)}) collective-permute-start(bf16[32,3584]{1,0:T(8,128)(2,1)S(1)} %get-tuple-element.81), channel_id=1, source_target_pairs={{0,49},{1,48},{2,51},{3,50},{4,53},{5,52},{6,55},{7,54},{8,57},{9,... | collective-permute-start | bytes 688136 | tf_op jit(solution)/shard_map/ppermute | solution.py:89
  136.7 2.6 %collective-permute-start.33 = (bf16[32,3584]{1,0:T(8,128)(2,1)S(1)}, bf16[32,3584]{1,0:T(8,128)(2,1)S(1)}, u32[]{:S(2)}, u32[]{:S(2)}) collective-permute-start(bf16[32,3584]{1,0:T(8,128)(2,1)S(1)} %shard_map.139), channel_id=1, source_target_pairs={{32,0},{33,1},{34,2},{35,3},{36,4},{37,5},{38,6},{39,7},{40,8},{41... | collective-permute-start | bytes 688136 | tf_op jit(solution)/shard_map/ppermute | solution.py:89
  139.4 2.8 %collective-permute-start.34 = (bf16[32,3584]{1,0:T(8,128)(2,1)S(1)}, bf16[32,3584]{1,0:T(8,128)(2,1)S(1)}, u32[]{:S(2)}, u32[]{:S(2)}) collective-permute-start(bf16[32,3584]{1,0:T(8,128)(2,1)S(1)} %shard_map.138.refs_4_), channel_id=1, source_target_pairs={{32,17},{33,16},{34,19},{35,18},{36,21},{37,20},{38,23},{39,22},{4... | collective-permute-start | bytes 688136 | tf_op jit(solution)/shard_map/ppermute | solution.py:89
  142.3 3.0 %collective-permute-done.27.refs_3_ = bf16[32,3584]{1,0:T(8,128)(2,1)S(1)} collective-permute-done((bf16[32,3584]{1,0:T(8,128)(2,1)S(1)}, bf16[32,3584]{1,0:T(8,128)(2,1)S(1)}, u32[]{:S(2)}, u32[]{:S(2)}) %collective-permute-start.27) | collective-permute-done | bytes 229408 | tf_op jit(solution)/shard_map/ppermute | solution.py:89
  145.3 1.3 shard_map.135
  146.6 4.2 %collective-permute-done.34.far_ref = bf16[32,3584]{1,0:T(8,128)(2,1)S(1)} collective-permute-done((bf16[32,3584]{1,0:T(8,128)(2,1)S(1)}, bf16[32,3584]{1,0:T(8,128)(2,1)S(1)}, u32[]{:S(2)}, u32[]{:S(2)}) %collective-permute-start.34) | collective-permute-done | bytes 229408 | tf_op jit(solution)/shard_map/ppermute | solution.py:89
  150.8 1.5 shard_map.140
  (82 shorter events, 4.6 us)
Async XLA Ops:
  3.0 7.9 %collective-permute-start = (bf16[32,3584]{1,0:T(8,128)(2,1)}, bf16[32,3584]{1,0:T(8,128)(2,1)S(1)}, u32[]{:S(2)}, u32[]{:S(2)}) collective-permute-start(bf16[32,3584]{1,0:T(8,128)(2,1)} %get-tuple-element.46), channel_id=1, source_target_pairs={{0,17},{1,16},{2,19},{3,18},{4,21},{5,20},{6,23},{7,22},{8,25},{9,... | collective-permute-start | bytes 688136 | tf_op jit(solution)/shard_map/ppermute | solution.py:78
  6.3 70.8 %collective-permute-start.9 = (bf16[256,3584]{1,0:T(8,128)(2,1)}, bf16[256,3584]{1,0:T(8,128)(2,1)S(1)}, u32[]{:S(2)}, u32[]{:S(2)}) collective-permute-start(bf16[256,3584]{1,0:T(8,128)(2,1)} %bitcast.33), channel_id=1, source_target_pairs={{0,1},{1,0},{2,3},{3,2},{4,5},{5,4},{6,7},{7,6},{8,9},{9,8},{10,11... | collective-permute-start | bytes 5505032 | tf_op jit(solution)/shard_map/ppermute | solution.py:78
  10.9 9.3 %copy-start.5 = (bf16[32,3584]{1,0:T(8,128)(2,1)}, bf16[32,3584]{1,0:T(8,128)(2,1)S(1)}, u32[]{:S(2)}) copy-start(bf16[32,3584]{1,0:T(8,128)(2,1)S(1)} %collective-permute-done.refs_5_.refs_1_) | copy-start | bytes 688132
  10.9 1.0 copy-start.7
  12.0 13.7 %collective-permute-start.2 = (bf16[16,3584]{1,0:T(8,128)(2,1)S(1)}, bf16[16,3584]{1,0:T(8,128)(2,1)S(1)}, u32[]{:S(2)}, u32[]{:S(2)}) collective-permute-start(bf16[16,3584]{1,0:T(8,128)(2,1)S(1)} %get-tuple-element.51), channel_id=1, source_target_pairs={{0,4},{1,5},{2,14},{3,15},{4,8},{5,9},{6,2},{7,3},{8,12},{9,13},{1... | collective-permute-start | bytes 344072 | tf_op jit(solution)/shard_map/ppermute | solution.py:78
  15.9 9.8 %collective-permute-start.3 = (bf16[16,3584]{1,0:T(8,128)(2,1)S(1)}, bf16[16,3584]{1,0:T(8,128)(2,1)S(1)}, u32[]{:S(2)}, u32[]{:S(2)}) collective-permute-start(bf16[16,3584]{1,0:T(8,128)(2,1)S(1)} %get-tuple-element.52), channel_id=1, source_target_pairs={{0,14},{1,15},{2,4},{3,5},{4,2},{5,3},{6,8},{7,9},{8,6},{9,7},{10,... | collective-permute-start | bytes 344072 | tf_op jit(solution)/shard_map/ppermute | solution.py:78
  19.6 9.2 %collective-permute-start.4 = (bf16[16,3584]{1,0:T(8,128)(2,1)S(1)}, bf16[16,3584]{1,0:T(8,128)(2,1)S(1)}, u32[]{:S(2)}, u32[]{:S(2)}) collective-permute-start(bf16[16,3584]{1,0:T(8,128)(2,1)S(1)} %get-tuple-element.53), channel_id=1, source_target_pairs={{0,10},{1,11},{2,8},{3,9},{4,14},{5,15},{6,12},{7,13},{8,2},{9,3},... | collective-permute-start | bytes 344072 | tf_op jit(solution)/shard_map/ppermute | solution.py:78
  23.2 11.3 %collective-permute-start.1 = (bf16[64,3584]{1,0:T(8,128)(2,1)}, bf16[64,3584]{1,0:T(8,128)(2,1)S(1)}, u32[]{:S(2)}, u32[]{:S(2)}) collective-permute-start(bf16[64,3584]{1,0:T(8,128)(2,1)} %get-tuple-element.48), channel_id=1, source_target_pairs={{0,17},{1,16},{2,19},{3,18},{4,21},{5,20},{6,23},{7,22},{8,25},{9,... | collective-permute-start | bytes 1376264 | tf_op jit(solution)/shard_map/ppermute | solution.py:78
  25.7 14.9 %copy-start.1 = (bf16[1,3584,256]{2,1,0:T(8,128)(2,1)S(1)}, bf16[1,3584,256]{2,1,0:T(8,128)(2,1)}, u32[]{:S(2)}) copy-start(bf16[1,3584,256]{2,1,0:T(8,128)(2,1)} %param.18) | copy-start | bytes 5505028
  25.7 14.9 %copy-start = (bf16[1,3584,256]{2,1,0:T(8,128)(2,1)S(1)}, bf16[1,3584,256]{2,1,0:T(8,128)(2,1)}, u32[]{:S(2)}) copy-start(bf16[1,3584,256]{2,1,0:T(8,128)(2,1)} %param.17) | copy-start | bytes 5505028
  28.8 11.6 %collective-permute-start.12 = (bf16[64,3584]{1,0:T(8,128)(2,1)S(1)}, bf16[64,3584]{1,0:T(8,128)(2,1)S(1)}, u32[]{:S(2)}, u32[]{:S(2)}) collective-permute-start(bf16[64,3584]{1,0:T(8,128)(2,1)S(1)} %get-tuple-element.103.refs_2_), channel_id=1, source_target_pairs={{0,2},{1,3},{2,0},{3,1},{4,6},{5,7},{6,4},{7,5},{8,10},{9,11},{10,... | collective-permute-start | bytes 1376264 | tf_op jit(solution)/shard_map/ppermute | solution.py:78
  34.5 1.0 copy-start.6
  35.6 13.4 %collective-permute-start.5 = (bf16[32,3584]{1,0:T(8,128)(2,1)S(1)}, bf16[32,3584]{1,0:T(8,128)(2,1)S(1)}, u32[]{:S(2)}, u32[]{:S(2)}) collective-permute-start(bf16[32,3584]{1,0:T(8,128)(2,1)S(1)} %get-tuple-element.55), channel_id=1, source_target_pairs={{0,4},{1,5},{2,14},{3,15},{4,8},{5,9},{6,2},{7,3},{8,12},{9,13},{1... | collective-permute-start | bytes 688136 | tf_op jit(solution)/shard_map/ppermute | solution.py:78
  37.2 11.8 %collective-permute-start.6 = (bf16[32,3584]{1,0:T(8,128)(2,1)S(1)}, bf16[32,3584]{1,0:T(8,128)(2,1)S(1)}, u32[]{:S(2)}, u32[]{:S(2)}) collective-permute-start(bf16[32,3584]{1,0:T(8,128)(2,1)S(1)} %get-tuple-element.56), channel_id=1, source_target_pairs={{0,14},{1,15},{2,4},{3,5},{4,2},{5,3},{6,8},{7,9},{8,6},{9,7},{10,... | collective-permute-start | bytes 688136 | tf_op jit(solution)/shard_map/ppermute | solution.py:78
  39.6 18.7 %collective-permute-start.7 = (bf16[32,3584]{1,0:T(8,128)(2,1)S(1)}, bf16[32,3584]{1,0:T(8,128)(2,1)S(1)}, u32[]{:S(2)}, u32[]{:S(2)}) collective-permute-start(bf16[32,3584]{1,0:T(8,128)(2,1)S(1)} %get-tuple-element.57), channel_id=1, source_target_pairs={{0,10},{1,11},{2,8},{3,9},{4,14},{5,15},{6,12},{7,13},{8,2},{9,3},... | collective-permute-start | bytes 688136 | tf_op jit(solution)/shard_map/ppermute | solution.py:78
  40.5 26.3 %collective-permute-start.13 = (bf16[128,3584]{1,0:T(8,128)(2,1)S(1)}, bf16[128,3584]{1,0:T(8,128)(2,1)S(1)}, u32[]{:S(2)}, u32[]{:S(2)}) collective-permute-start(bf16[128,3584]{1,0:T(8,128)(2,1)S(1)} %constant_dynamic-update-slice_fusion.9.refs_0_), channel_id=1, source_target_pairs={{0,1},{1,0},{2,3},{3,2},{4,5},{5,4},{6,7},{7,6},{8,9},{9,8},{10,11... | collective-permute-start | bytes 2752520 | tf_op jit(solution)/shard_map/ppermute | solution.py:78
  58.3 13.5 %collective-permute-start.19 = (bf16[64,3584]{1,0:T(8,128)(2,1)S(1)}, bf16[64,3584]{1,0:T(8,128)(2,1)S(1)}, u32[]{:S(2)}, u32[]{:S(2)}) collective-permute-start(bf16[64,3584]{1,0:T(8,128)(2,1)S(1)} %pad_maximum_fusion.1.refs_0_), channel_id=1, source_target_pairs={{0,2},{1,3},{2,0},{3,1},{4,6},{5,7},{6,4},{7,5},{8,10},{9,11},{10,... | collective-permute-start | bytes 1376264 | tf_op jit(solution)/shard_map/ppermute | solution.py:78
  58.4 9.2 %copy-start.3 = (bf16[1,128,3584]{2,1,0:T(8,128)(2,1)S(1)}, bf16[1,128,3584]{2,1,0:T(8,128)(2,1)}, u32[]{:S(2)}) copy-start(bf16[1,128,3584]{2,1,0:T(8,128)(2,1)} %param.16) | copy-start | bytes 2752516
  58.4 21.4 %collective-permute-start.8 = (bf16[64,3584]{1,0:T(8,128)(2,1)S(1)}, bf16[64,3584]{1,0:T(8,128)(2,1)S(1)}, u32[]{:S(2)}, u32[]{:S(2)}) collective-permute-start(bf16[64,3584]{1,0:T(8,128)(2,1)S(1)} %pad_maximum_fusion), channel_id=1, source_target_pairs={{0,2},{1,3},{2,0},{3,1},{4,6},{5,7},{6,4},{7,5},{8,10},{9,11},{10,... | collective-permute-start | bytes 1376264 | tf_op jit(solution)/shard_map/ppermute | solution.py:78
  67.4 5.9 %copy-start.9 = (bf16[128,128]{1,0:T(8,128)(2,1)S(1)}, bf16[128,128]{1,0:T(8,128)(2,1)}, u32[]{:S(2)}) copy-start(bf16[128,128]{1,0:T(8,128)(2,1)} %get-tuple-element.66.refs_0_) | copy-start | bytes 98308
  67.4 9.7 %copy-start.2 = (bf16[1,256,3584]{2,1,0:T(8,128)(2,1)S(1)}, bf16[1,256,3584]{2,1,0:T(8,128)(2,1)}, u32[]{:S(2)}) copy-start(bf16[1,256,3584]{2,1,0:T(8,128)(2,1)} %param.19) | copy-start | bytes 5505028
  67.5 4.4 %collective-permute-start.14 = (bf16[128,256]{1,0:T(8,128)(2,1)S(1)}, bf16[128,256]{1,0:T(8,128)(2,1)S(1)}, u32[]{:S(2)}, u32[]{:S(2)}) collective-permute-start(bf16[128,256]{1,0:T(8,128)(2,1)S(1)} %shard_map.121), channel_id=1, source_target_pairs={{0,1},{1,0},{2,3},{3,2},{4,5},{5,4},{6,7},{7,6},{8,9},{9,8},{10,11... | collective-permute-start | bytes 196616 | tf_op jit(solution)/shard_map/ppermute | solution.py:78
  67.7 23.1 %collective-permute-start.22 = (bf16[128,3584]{1,0:T(8,128)(2,1)S(1)}, bf16[128,3584]{1,0:T(8,128)(2,1)S(1)}, u32[]{:S(2)}, u32[]{:S(2)}) collective-permute-start(bf16[128,3584]{1,0:T(8,128)(2,1)S(1)} %shard_map.127), channel_id=1, source_target_pairs={{32,0},{33,1},{34,2},{35,3},{36,4},{37,5},{38,6},{39,7},{40,8},{41... | collective-permute-start | bytes 2752520 | tf_op jit(solution)/shard_map/ppermute | solution.py:89
  71.9 19.5 %collective-permute-start.21 = (bf16[128,3584]{1,0:T(8,128)(2,1)S(1)}, bf16[128,3584]{1,0:T(8,128)(2,1)}, u32[]{:S(2)}, u32[]{:S(2)}) collective-permute-start(bf16[128,3584]{1,0:T(8,128)(2,1)S(1)} %shard_map.124.refs_0_), channel_id=1, source_target_pairs={{0,1},{1,0},{2,3},{3,2},{4,5},{5,4},{6,7},{7,6},{8,9},{9,8},{10,11... | collective-permute-start | bytes 2752520 | tf_op jit(solution)/shard_map/ppermute | solution.py:78
  73.3 11.5 %collective-permute-start.20 = (bf16[128,128]{1,0:T(8,128)(2,1)S(1)}, bf16[128,128]{1,0:T(8,128)(2,1)S(1)}, u32[]{:S(2)}, u32[]{:S(2)}) collective-permute-start(bf16[128,128]{1,0:T(8,128)(2,1)S(1)} %shard_map.125), channel_id=1, source_target_pairs={{32,0},{33,1},{34,2},{35,3},{36,4},{37,5},{38,6},{39,7},{40,8},{41... | collective-permute-start | bytes 98312 | tf_op jit(solution)/shard_map/ppermute | solution.py:89
  77.8 12.9 %collective-permute-start.15 = (bf16[64,3584]{1,0:T(8,128)(2,1)S(1)}, bf16[64,3584]{1,0:T(8,128)(2,1)S(1)}, u32[]{:S(2)}, u32[]{:S(2)}) collective-permute-start(bf16[64,3584]{1,0:T(8,128)(2,1)S(1)} %get-tuple-element.61), channel_id=1, source_target_pairs={{0,2},{1,3},{2,0},{3,1},{4,6},{5,7},{6,4},{7,5},{8,10},{9,11},{10,... | collective-permute-start | bytes 1376264 | tf_op jit(solution)/shard_map/ppermute | solution.py:78
  79.8 3.1 %copy-start.8 = (bf16[128,128]{1,0:T(8,128)(2,1)S(1)}, bf16[128,128]{1,0:T(8,128)(2,1)}, u32[]{:S(2)}) copy-start(bf16[128,128]{1,0:T(8,128)(2,1)} %get-tuple-element.59.refs_0_) | copy-start | bytes 98308
  81.1 12.1 %collective-permute-start.23 = (bf16[128,256]{1,0:T(8,128)(2,1)S(1)}, bf16[128,256]{1,0:T(8,128)(2,1)S(1)}, u32[]{:S(2)}, u32[]{:S(2)}) collective-permute-start(bf16[128,256]{1,0:T(8,128)(2,1)S(1)} %get-tuple-element.58.refs_1_), channel_id=1, source_target_pairs={{0,1},{1,0},{2,3},{3,2},{4,5},{5,4},{6,7},{7,6},{8,9},{9,8},{10,11... | collective-permute-start | bytes 196616 | tf_op jit(solution)/shard_map/ppermute | solution.py:78
  84.8 6.0 %collective-permute-start.11 = (bf16[128,128]{1,0:T(8,128)(2,1)S(1)}, bf16[128,128]{1,0:T(8,128)(2,1)S(1)}, u32[]{:S(2)}, u32[]{:S(2)}) collective-permute-start(bf16[128,128]{1,0:T(8,128)(2,1)S(1)} %shard_map.119), channel_id=1, source_target_pairs={{0,32},{1,33},{2,34},{3,35},{4,36},{5,37},{6,38},{7,39},{8,40},{9,... | collective-permute-start | bytes 98312 | tf_op jit(solution)/shard_map/ppermute | solution.py:89
  94.0 4.7 %copy-start.4 = (bf16[1,128,3584]{2,1,0:T(8,128)(2,1)S(1)}, bf16[1,128,3584]{2,1,0:T(8,128)(2,1)}, u32[]{:S(2)}) copy-start(bf16[1,128,3584]{2,1,0:T(8,128)(2,1)} %param.10) | copy-start | bytes 2752516
  94.0 11.7 %collective-permute-start.25 = (bf16[128,1792]{1,0:T(8,128)(2,1)S(1)}, bf16[128,1792]{1,0:T(8,128)(2,1)S(1)}, u32[]{:S(2)}, u32[]{:S(2)}) collective-permute-start(bf16[128,1792]{1,0:T(8,128)(2,1)S(1)} %get-tuple-element.78), channel_id=1, source_target_pairs={{0,2},{1,3},{2,0},{3,1},{4,6},{5,7},{6,4},{7,5},{8,10},{9,11},{10,... | collective-permute-start | bytes 1376264 | tf_op jit(solution)/shard_map/ppermute | solution.py:78
  96.3 9.7 %collective-permute-start.24 = (bf16[128,1792]{1,0:T(8,128)(2,1)S(1)}, bf16[128,1792]{1,0:T(8,128)(2,1)S(1)}, u32[]{:S(2)}, u32[]{:S(2)}) collective-permute-start(bf16[128,1792]{1,0:T(8,128)(2,1)S(1)} %get-tuple-element.75), channel_id=1, source_target_pairs={{0,1},{1,0},{2,3},{3,2},{4,5},{5,4},{6,7},{7,6},{8,9},{9,8},{10,11... | collective-permute-start | bytes 1376264 | tf_op jit(solution)/shard_map/ppermute | solution.py:78
  98.8 43.5 %collective-permute-start.10 = (bf16[128,3584]{1,0:T(8,128)(2,1)S(1)}, bf16[128,3584]{1,0:T(8,128)(2,1)S(1)}, u32[]{:S(2)}, u32[]{:S(2)}) collective-permute-start(bf16[128,3584]{1,0:T(8,128)(2,1)S(1)} %shard_map.118), channel_id=1, source_target_pairs={{0,32},{1,33},{2,34},{3,35},{4,36},{5,37},{6,38},{7,39},{8,40},{9,... | collective-permute-start | bytes 2752520 | tf_op jit(solution)/shard_map/ppermute | solution.py:89
  105.8 8.7 %collective-permute-start.29 = (bf16[64,1792]{1,0:T(8,128)(2,1)S(1)}, bf16[64,1792]{1,0:T(8,128)(2,1)S(1)}, u32[]{:S(2)}, u32[]{:S(2)}) collective-permute-start(bf16[64,1792]{1,0:T(8,128)(2,1)S(1)} %get-tuple-element.79.refs_5_), channel_id=1, source_target_pairs={{0,1},{1,0},{2,3},{3,2},{4,5},{5,4},{6,7},{7,6},{8,9},{9,8},{10,11... | collective-permute-start | bytes 688136 | tf_op jit(solution)/shard_map/ppermute | solution.py:78
  106.1 13.3 %collective-permute-start.28 = (bf16[64,1792]{1,0:T(8,128)(2,1)S(1)}, bf16[64,1792]{1,0:T(8,128)(2,1)S(1)}, u32[]{:S(2)}, u32[]{:S(2)}) collective-permute-start(bf16[64,1792]{1,0:T(8,128)(2,1)S(1)} %get-tuple-element.76.refs_4_), channel_id=1, source_target_pairs={{0,2},{1,3},{2,0},{3,1},{4,6},{5,7},{6,4},{7,5},{8,10},{9,11},{10,... | collective-permute-start | bytes 688136 | tf_op jit(solution)/shard_map/ppermute | solution.py:78
  107.0 12.6 %collective-permute-start.16 = (bf16[16,3584]{1,0:T(8,128)(2,1)S(1)}, bf16[16,3584]{1,0:T(8,128)(2,1)S(1)}, u32[]{:S(2)}, u32[]{:S(2)}) collective-permute-start(bf16[16,3584]{1,0:T(8,128)(2,1)S(1)} %get-tuple-element.63), channel_id=1, source_target_pairs={{4,0},{5,1},{14,2},{15,3},{8,4},{9,5},{2,6},{3,7},{12,8},{13,9},{6... | collective-permute-start | bytes 344072 | tf_op jit(solution)/shard_map/ppermute | solution.py:78
  114.5 8.2 %collective-permute-start.17 = (bf16[16,3584]{1,0:T(8,128)(2,1)S(1)}, bf16[16,3584]{1,0:T(8,128)(2,1)S(1)}, u32[]{:S(2)}, u32[]{:S(2)}) collective-permute-start(bf16[16,3584]{1,0:T(8,128)(2,1)S(1)} %get-tuple-element.64), channel_id=1, source_target_pairs={{14,0},{15,1},{4,2},{5,3},{2,4},{3,5},{8,6},{9,7},{6,8},{7,9},{12,... | collective-permute-start | bytes 344072 | tf_op jit(solution)/shard_map/ppermute | solution.py:78
  114.6 8.5 %collective-permute-start.18 = (bf16[16,3584]{1,0:T(8,128)(2,1)S(1)}, bf16[16,3584]{1,0:T(8,128)(2,1)S(1)}, u32[]{:S(2)}, u32[]{:S(2)}) collective-permute-start(bf16[16,3584]{1,0:T(8,128)(2,1)S(1)} %get-tuple-element.65), channel_id=1, source_target_pairs={{10,0},{11,1},{8,2},{9,3},{14,4},{15,5},{12,6},{13,7},{2,8},{3,9},... | collective-permute-start | bytes 344072 | tf_op jit(solution)/shard_map/ppermute | solution.py:78
  119.5 14.5 %collective-permute-start.30 = (bf16[16,3584]{1,0:T(8,128)(2,1)S(1)}, bf16[16,3584]{1,0:T(8,128)(2,1)S(1)}, u32[]{:S(2)}, u32[]{:S(2)}) collective-permute-start(bf16[16,3584]{1,0:T(8,128)(2,1)S(1)} %get-tuple-element.86), channel_id=1, source_target_pairs={{4,0},{5,1},{14,2},{15,3},{8,4},{9,5},{2,6},{3,7},{12,8},{13,9},{6... | collective-permute-start | bytes 344072 | tf_op jit(solution)/shard_map/ppermute | solution.py:78
  119.6 17.0 %collective-permute-start.31 = (bf16[16,3584]{1,0:T(8,128)(2,1)S(1)}, bf16[16,3584]{1,0:T(8,128)(2,1)S(1)}, u32[]{:S(2)}, u32[]{:S(2)}) collective-permute-start(bf16[16,3584]{1,0:T(8,128)(2,1)S(1)} %get-tuple-element.87), channel_id=1, source_target_pairs={{14,0},{15,1},{4,2},{5,3},{2,4},{3,5},{8,6},{9,7},{6,8},{7,9},{12,... | collective-permute-start | bytes 344072 | tf_op jit(solution)/shard_map/ppermute | solution.py:78
  122.7 13.9 %collective-permute-start.32 = (bf16[16,3584]{1,0:T(8,128)(2,1)S(1)}, bf16[16,3584]{1,0:T(8,128)(2,1)S(1)}, u32[]{:S(2)}, u32[]{:S(2)}) collective-permute-start(bf16[16,3584]{1,0:T(8,128)(2,1)S(1)} %get-tuple-element.88), channel_id=1, source_target_pairs={{10,0},{11,1},{8,2},{9,3},{14,4},{15,5},{12,6},{13,7},{2,8},{3,9},... | collective-permute-start | bytes 344072 | tf_op jit(solution)/shard_map/ppermute | solution.py:78
  123.1 19.1 %collective-permute-start.26 = (bf16[32,3584]{1,0:T(8,128)(2,1)S(1)}, bf16[32,3584]{1,0:T(8,128)(2,1)S(1)}, u32[]{:S(2)}, u32[]{:S(2)}) collective-permute-start(bf16[32,3584]{1,0:T(8,128)(2,1)S(1)} %get-tuple-element.80), channel_id=1, source_target_pairs={{0,32},{1,33},{2,34},{3,35},{4,36},{5,37},{6,38},{7,39},{8,40},{9,... | collective-permute-start | bytes 688136 | tf_op jit(solution)/shard_map/ppermute | solution.py:89
  134.0 11.3 %collective-permute-start.27 = (bf16[32,3584]{1,0:T(8,128)(2,1)S(1)}, bf16[32,3584]{1,0:T(8,128)(2,1)S(1)}, u32[]{:S(2)}, u32[]{:S(2)}) collective-permute-start(bf16[32,3584]{1,0:T(8,128)(2,1)S(1)} %get-tuple-element.81), channel_id=1, source_target_pairs={{0,49},{1,48},{2,51},{3,50},{4,53},{5,52},{6,55},{7,54},{8,57},{9,... | collective-permute-start | bytes 688136 | tf_op jit(solution)/shard_map/ppermute | solution.py:89
  136.7 9.9 %collective-permute-start.33 = (bf16[32,3584]{1,0:T(8,128)(2,1)S(1)}, bf16[32,3584]{1,0:T(8,128)(2,1)S(1)}, u32[]{:S(2)}, u32[]{:S(2)}) collective-permute-start(bf16[32,3584]{1,0:T(8,128)(2,1)S(1)} %shard_map.139), channel_id=1, source_target_pairs={{32,0},{33,1},{34,2},{35,3},{36,4},{37,5},{38,6},{39,7},{40,8},{41... | collective-permute-start | bytes 688136 | tf_op jit(solution)/shard_map/ppermute | solution.py:89
  139.4 11.4 %collective-permute-start.34 = (bf16[32,3584]{1,0:T(8,128)(2,1)S(1)}, bf16[32,3584]{1,0:T(8,128)(2,1)S(1)}, u32[]{:S(2)}, u32[]{:S(2)}) collective-permute-start(bf16[32,3584]{1,0:T(8,128)(2,1)S(1)} %shard_map.138.refs_4_), channel_id=1, source_target_pairs={{32,17},{33,16},{34,19},{35,18},{36,21},{37,20},{38,23},{39,22},{4... | collective-permute-start | bytes 688136 | tf_op jit(solution)/shard_map/ppermute | solution.py:89
